TPU v7x, 32 devices: a whole 2x2x4 slice. The times are simulated.
32 devices in a mesh: clip: 16 (over z, y, core), frame: 2 (over x).
Axes of the slice: x: 2, y: 2, z: 4, core: 2. Of those that a mesh axis runs over, the one named last changes fastest.
Arguments:
- tokens: bfloat16 [32, 16, 196, 768], P('clip', 'frame'), may hold values from -6 to 6
- cotangent: bfloat16 [32, 16, 196, 768], P('clip', 'frame'), may hold values from -6 to 6
- space_gain: bfloat16 [768], P(('clip', 'frame')), may hold values from 0.099609375 to 1.8984375
- time_gain: bfloat16 [768], P(('clip', 'frame')), may hold values from 0.099609375 to 1.8984375
- feed_gain: bfloat16 [768], P(('clip', 'frame')), may hold values from 0.099609375 to 1.8984375
- space_proj: bfloat16 [768, 2304], P(('clip', 'frame')), may hold values from -0.21875 to 0.21875
- space_out: bfloat16 [768, 768], P(('clip', 'frame')), may hold values from -0.625 to 0.625
- time_proj: bfloat16 [768, 2304], P(('clip', 'frame')), may hold values from -0.21875 to 0.21875
- time_out: bfloat16 [768, 768], P(('clip', 'frame')), may hold values from -0.4375 to 0.4375
- up_proj: bfloat16 [768, 3072], P(('clip', 'frame')), may hold values from -0.21875 to 0.21875
- down_proj: bfloat16 [3072, 768], P(('clip', 'frame')), may hold values from -0.15625 to 0.15625
Outputs:
- mixed: bfloat16 [32, 16, 196, 768], P('clip', 'frame')
- grad_tokens: float32 [32, 16, 196, 768], P('clip', 'frame')
- grad_space_gain: float32 [768], P(('clip', 'frame'))
- grad_time_gain: float32 [768], P(('clip', 'frame'))
- grad_feed_gain: float32 [768], P(('clip', 'frame'))
- grad_space_proj: float32 [768, 2304], P(('clip', 'frame'))
- grad_space_out: float32 [768, 768], P(('clip', 'frame'))
- grad_time_proj: float32 [768, 2304], P(('clip', 'frame'))
- grad_time_out: float32 [768, 768], P(('clip', 'frame'))
- grad_up_proj: float32 [768, 3072], P(('clip', 'frame'))
- grad_down_proj: float32 [3072, 768], P(('clip', 'frame'))
All inputs are finite; a program needn't handle non-finite values.
Results may differ from a plain program's by a relative error of at most 0.024.
Values may be sent and summed in bfloat16 or wider, within the bound.
No kernel may reach another device: no remote copies, remote signals or barrier semaphores. Data moves between devices by JAX's collectives and lax.ppermute only.
A program may use at most 512 MiB of HBM per device.

v0:
```python
import jax
import jax.numpy as jnp
from jax import lax
from jax.sharding import PartitionSpec as P

HEADS = 12
HEAD = 64
MICRO = 2


epsilon = 1e-06


def norm_forward(values, gain):
    centred = values - jnp.mean(values, axis=-1, keepdims=True)
    inverse = lax.rsqrt(jnp.mean(centred * centred, axis=-1, keepdims=True) + epsilon)
    normed = centred * inverse
    return (normed * gain, normed, inverse)


def norm_backward(gradient, normed, inverse, gain):
    gain_grad = jnp.sum(gradient * normed, axis=(0, 1, 2))
    scaled = gradient * gain
    centred_grad = (
        scaled
        - jnp.mean(scaled, axis=-1, keepdims=True)
        - normed * jnp.mean(scaled * normed, axis=-1, keepdims=True)
    )
    return (inverse * centred_grad, gain_grad)


def to_places(blocks):
    clip_count, frames, places, model_width = blocks.shape
    return blocks.transpose(0, 2, 1, 3).reshape(clip_count * places, frames, HEADS, HEAD)


def from_places(attended, clip_count, places):
    frames = attended.shape[1]
    return attended.reshape(clip_count, places, frames, HEADS * HEAD).transpose(0, 2, 1, 3)


def attend_forward(queries, key_block, value_block):
    factor = HEAD ** (-0.5)
    scores = (
        jnp.einsum("blhe,bmhe->bhlm", queries, key_block, preferred_element_type=jnp.float32)
        * factor
    )
    highest = jnp.max(scores, axis=-1, keepdims=True)
    powers = jnp.exp(scores - highest)
    row_total = jnp.sum(powers, axis=-1, keepdims=True)
    chances = (powers / row_total).astype(jnp.bfloat16)
    result = jnp.einsum("bhlm,bmhe->blhe", chances, value_block, preferred_element_type=jnp.float32)
    return (result, highest + jnp.log(row_total))


def attend_backward(queries, key_block, value_block, logsum, grad_out):
    factor = HEAD ** (-0.5)
    scores = (
        jnp.einsum("blhe,bmhe->bhlm", queries, key_block, preferred_element_type=jnp.float32)
        * factor
    )
    chances = jnp.exp(scores - logsum)
    grad_chances = jnp.einsum(
        "blhe,bmhe->bhlm", grad_out, value_block, preferred_element_type=jnp.float32
    )
    grad_scores = (
        chances * (grad_chances - jnp.sum(chances * grad_chances, axis=-1, keepdims=True))
    ).astype(jnp.bfloat16)
    grad_queries = (
        jnp.einsum("bhlm,bmhe->blhe", grad_scores, key_block, preferred_element_type=jnp.float32)
        * factor
    )
    grad_keys = (
        jnp.einsum("bhlm,blhe->bmhe", grad_scores, queries, preferred_element_type=jnp.float32)
        * factor
    )
    grad_values = jnp.einsum(
        "bhlm,blhe->bmhe",
        chances.astype(jnp.bfloat16),
        grad_out,
        preferred_element_type=jnp.float32,
    )
    return (grad_queries, grad_keys, grad_values)


def project(values, matrix):
    return jnp.einsum("cfpd,de->cfpe", values, matrix, preferred_element_type=jnp.float32)


def project_back(gradient, matrix):
    return jnp.einsum("cfpe,de->cfpd", gradient, matrix, preferred_element_type=jnp.float32)


def outer_sum(values, gradient):
    return jnp.einsum("cfpd,cfpe->de", values, gradient, preferred_element_type=jnp.float32)


def forward(sample, gathered):
    (
        space_gain,
        time_gain,
        feed_gain,
        space_proj,
        space_out,
        time_proj,
        time_out,
        up_proj,
        down_proj,
    ) = gathered
    clip_count, frames, places, model_width = sample.shape
    normed_space = norm_forward(sample, space_gain.astype(jnp.float32))
    in_space = normed_space[0].astype(jnp.bfloat16)
    qkv_space = project(in_space, space_proj).astype(jnp.bfloat16)
    parted = qkv_space.reshape(clip_count * frames, places, 3, HEADS, HEAD)
    attended, logsum_space = attend_forward(parted[:, :, 0], parted[:, :, 1], parted[:, :, 2])
    out_space = attended.reshape(clip_count, frames, places, model_width).astype(jnp.bfloat16)
    after_space = sample + project(out_space, space_out)
    normed_time = norm_forward(after_space, time_gain.astype(jnp.float32))
    in_time = normed_time[0].astype(jnp.bfloat16)
    qkv_time = project(in_time, time_proj).astype(jnp.bfloat16)
    kv_whole = lax.all_gather(qkv_time[..., model_width:], "frame", axis=1, tiled=True)
    attended, logsum_time = attend_forward(
        to_places(qkv_time[..., :model_width]),
        to_places(kv_whole[..., :model_width]),
        to_places(kv_whole[..., model_width:]),
    )
    out_time = from_places(attended, clip_count, places).astype(jnp.bfloat16)
    after_time = after_space + project(out_time, time_out)
    normed_feed = norm_forward(after_time, feed_gain.astype(jnp.float32))
    in_feed = normed_feed[0].astype(jnp.bfloat16)
    hidden = project(in_feed, up_proj)
    active = jax.nn.gelu(hidden).astype(jnp.bfloat16)
    result = after_time + project(active, down_proj)
    saved = (
        normed_space,
        in_space,
        qkv_space,
        logsum_space,
        out_space,
        normed_time,
        in_time,
        qkv_time,
        kv_whole,
        logsum_time,
        out_time,
        normed_feed,
        in_feed,
        hidden,
        active,
    )
    return (result, saved)


def backward(gradient, saved, gathered):
    (
        space_gain,
        time_gain,
        feed_gain,
        space_proj,
        space_out,
        time_proj,
        time_out,
        up_proj,
        down_proj,
    ) = gathered
    (
        normed_space,
        in_space,
        qkv_space,
        logsum_space,
        out_space,
        normed_time,
        in_time,
        qkv_time,
        time_side,
        logsum_time,
        out_time,
        normed_feed,
        in_feed,
        hidden,
        active,
    ) = saved
    clip_count, frames, places, model_width = gradient.shape
    grad_low = gradient.astype(jnp.bfloat16)
    grad_down = outer_sum(active, grad_low)
    grad_active = project_back(grad_low, down_proj)
    gelu_value, gelu_pull = jax.vjp(jax.nn.gelu, hidden)
    grad_hidden = gelu_pull(grad_active)[0].astype(jnp.bfloat16)
    grad_up = outer_sum(in_feed, grad_hidden)
    back_feed, grad_feed_gain = norm_backward(
        project_back(grad_hidden, up_proj),
        normed_feed[1],
        normed_feed[2],
        feed_gain.astype(jnp.float32),
    )
    grad_time = gradient + back_feed
    time_low = grad_time.astype(jnp.bfloat16)
    grad_tout = outer_sum(out_time, time_low)
    grad_out_time = project_back(time_low, time_out).astype(jnp.bfloat16)
    grad_queries, grad_keys, grad_values = attend_backward(
        to_places(qkv_time[..., :model_width]),
        to_places(time_side[..., :model_width]),
        to_places(time_side[..., model_width:]),
        logsum_time,
        to_places(grad_out_time),
    )
    grad_kv = jnp.concatenate(
        (from_places(grad_keys, clip_count, places), from_places(grad_values, clip_count, places)),
        axis=-1,
    )
    grad_kv_own = lax.psum_scatter(
        grad_kv.astype(jnp.bfloat16), "frame", scatter_dimension=1, tiled=True
    ).astype(jnp.float32)
    grad_qkv_time = jnp.concatenate(
        (from_places(grad_queries, clip_count, places), grad_kv_own), axis=-1
    ).astype(jnp.bfloat16)
    grad_tproj = outer_sum(in_time, grad_qkv_time)
    back_time, grad_time_gain = norm_backward(
        project_back(grad_qkv_time, time_proj),
        normed_time[1],
        normed_time[2],
        time_gain.astype(jnp.float32),
    )
    grad_space = grad_time + back_time
    space_low = grad_space.astype(jnp.bfloat16)
    grad_sout = outer_sum(out_space, space_low)
    grad_out_space = project_back(space_low, space_out).astype(jnp.bfloat16)
    parted = qkv_space.reshape(clip_count * frames, places, 3, HEADS, HEAD)
    grad_queries, grad_keys, grad_values = attend_backward(
        parted[:, :, 0],
        parted[:, :, 1],
        parted[:, :, 2],
        logsum_space,
        grad_out_space.reshape(clip_count * frames, places, HEADS, HEAD),
    )
    grad_qkv_space = (
        jnp.stack((grad_queries, grad_keys, grad_values), axis=2)
        .reshape(clip_count, frames, places, 3 * model_width)
        .astype(jnp.bfloat16)
    )
    grad_sproj = outer_sum(in_space, grad_qkv_space)
    back_space, grad_space_gain = norm_backward(
        project_back(grad_qkv_space, space_proj),
        normed_space[1],
        normed_space[2],
        space_gain.astype(jnp.float32),
    )
    grad_input = grad_space + back_space
    return (
        grad_input,
        (
            grad_space_gain,
            grad_time_gain,
            grad_feed_gain,
            grad_sproj,
            grad_sout,
            grad_tproj,
            grad_tout,
            grad_up,
            grad_down,
        ),
    )


def shards(
    tokens,
    cotangent,
    space_gain,
    time_gain,
    feed_gain,
    space_proj,
    space_out,
    time_proj,
    time_out,
    up_proj,
    down_proj,
):
    owned = (
        space_gain,
        time_gain,
        feed_gain,
        space_proj,
        space_out,
        time_proj,
        time_out,
        up_proj,
        down_proj,
    )
    devices_all = lax.axis_size(("clip", "frame"))
    per_micro = tokens.shape[0] // MICRO
    totals = tuple(
        (
            jnp.zeros((piece.shape[0] * devices_all,) + piece.shape[1:], jnp.float32)
            for piece in owned
        )
    )
    mixed_parts = []
    grad_parts = []
    for micro_index in range(MICRO):
        sample = tokens[micro_index * per_micro : (micro_index + 1) * per_micro].astype(jnp.float32)
        gathered = (
            lax.all_gather(space_gain, ("clip", "frame"), axis=0, tiled=True),
            lax.all_gather(time_gain, ("clip", "frame"), axis=0, tiled=True),
            lax.all_gather(feed_gain, ("clip", "frame"), axis=0, tiled=True),
            lax.all_gather(space_proj, ("clip", "frame"), axis=0, tiled=True),
            lax.all_gather(space_out, ("clip", "frame"), axis=0, tiled=True),
            lax.all_gather(time_proj, ("clip", "frame"), axis=0, tiled=True),
            lax.all_gather(time_out, ("clip", "frame"), axis=0, tiled=True),
            lax.all_gather(up_proj, ("clip", "frame"), axis=0, tiled=True),
            lax.all_gather(down_proj, ("clip", "frame"), axis=0, tiled=True),
        )
        result, saved = forward(sample, gathered)
        mixed_parts.append(result.astype(jnp.bfloat16))
        back_weights = (
            lax.all_gather(space_gain, ("clip", "frame"), axis=0, tiled=True),
            lax.all_gather(time_gain, ("clip", "frame"), axis=0, tiled=True),
            lax.all_gather(feed_gain, ("clip", "frame"), axis=0, tiled=True),
            lax.all_gather(space_proj, ("clip", "frame"), axis=0, tiled=True),
            lax.all_gather(space_out, ("clip", "frame"), axis=0, tiled=True),
            lax.all_gather(time_proj, ("clip", "frame"), axis=0, tiled=True),
            lax.all_gather(time_out, ("clip", "frame"), axis=0, tiled=True),
            lax.all_gather(up_proj, ("clip", "frame"), axis=0, tiled=True),
            lax.all_gather(down_proj, ("clip", "frame"), axis=0, tiled=True),
        )
        gradient = cotangent[micro_index * per_micro : (micro_index + 1) * per_micro].astype(
            jnp.float32
        )
        grad_input, grads = backward(gradient, saved, back_weights)
        grad_parts.append(grad_input)
        totals = tuple((first + second for first, second in zip(totals, grads)))
    flat = tuple((item.reshape(-1) for item in totals))
    owners = (
        lax.psum_scatter(flat[0], ("clip", "frame"), scatter_dimension=0, tiled=True),
        lax.psum_scatter(flat[1], ("clip", "frame"), scatter_dimension=0, tiled=True),
        lax.psum_scatter(flat[2], ("clip", "frame"), scatter_dimension=0, tiled=True),
        lax.psum_scatter(flat[3], ("clip", "frame"), scatter_dimension=0, tiled=True),
        lax.psum_scatter(flat[4], ("clip", "frame"), scatter_dimension=0, tiled=True),
        lax.psum_scatter(flat[5], ("clip", "frame"), scatter_dimension=0, tiled=True),
        lax.psum_scatter(flat[6], ("clip", "frame"), scatter_dimension=0, tiled=True),
        lax.psum_scatter(flat[7], ("clip", "frame"), scatter_dimension=0, tiled=True),
        lax.psum_scatter(flat[8], ("clip", "frame"), scatter_dimension=0, tiled=True),
    )
    shaped = tuple((piece.reshape(mine.shape) for piece, mine in zip(owners, owned)))
    mixed = jnp.concatenate(mixed_parts, axis=0)
    grad_tokens = jnp.concatenate(grad_parts, axis=0)
    return (
        mixed,
        grad_tokens,
        shaped[0],
        shaped[1],
        shaped[2],
        shaped[3],
        shaped[4],
        shaped[5],
        shaped[6],
        shaped[7],
        shaped[8],
    )


def solution(mesh):
    in_specs = (
        P("clip", "frame", None, None),
        P("clip", "frame", None, None),
        P(("clip", "frame")),
        P(("clip", "frame")),
        P(("clip", "frame")),
        P(("clip", "frame"), None),
        P(("clip", "frame"), None),
        P(("clip", "frame"), None),
        P(("clip", "frame"), None),
        P(("clip", "frame"), None),
        P(("clip", "frame"), None),
    )
    out_specs = (
        P("clip", "frame", None, None),
        P("clip", "frame", None, None),
        P(("clip", "frame")),
        P(("clip", "frame")),
        P(("clip", "frame")),
        P(("clip", "frame"), None),
        P(("clip", "frame"), None),
        P(("clip", "frame"), None),
        P(("clip", "frame"), None),
        P(("clip", "frame"), None),
        P(("clip", "frame"), None),
    )
    return jax.shard_map(shards, mesh=mesh, in_specs=in_specs, out_specs=out_specs, check_vma=False)
```

profile of v0, /device:TPU:0, one launch (start us, length us, event | category | flops | bytes accessed | tf_op | source)
XLA Modules:
  0.0 2046.8 jit_solution(331154037278569033)
XLA Ops:
  12.0 42.1 %all-reduce.14 = (bf16[768]{0:T(1024)(128)(2,1)S(1)}, bf16[768]{0:T(1024)(128)(2,1)S(1)}, bf16[768]{0:T(1024)(128)(2,1)S(1)}) all-reduce(bf16[768]{0:T(1024)(128)(2,1)S(1)} %dynamic-update-slice, bf16[768]{0:T(1024)(128)(2,1)S(1)} %dynamic-update-slice.1, ...), channel_id=1, replica_groups=mesh['clip'=16,'frame'=2] {'clip','frame'}, use_global_device_ids=true, to_apply=%add | all-reduce | flops 2304 | bytes 9216
  59.3 14.7 all-gather.9.cloned.1.call-done
  73.9 12.0 convolution_convert_fusion.1
  86.0 11.6 copy.143
  97.6 12.4 multiply_reduce_fusion.3
  109.9 12.0 fusion.14
  122.0 11.7 fusion.170
  142.3 49.6 %all-gather.13.cloned.1.call-done = bf16[768,2304]{1,0:T(8,128)(2,1)} async-done(((bf16[24,2304]{1,0:T(8,128)(2,1)}), bf16[768,2304]{1,0:T(8,128)(2,1)}) %all-gather.13.cloned.1.call-update) | async-done | bytes 3538960 | tf_op jit(solution)/shard_map/all_gather | solution.py:307
  227.3 11.4 copy.159
  254.4 12.3 multiply_reduce_fusion.2
  266.7 11.9 fusion.15
  278.6 10.5 fusion.169
  344.5 13.9 copy.154
  367.5 13.9 copy.155
  423.0 26.3 %all-gather.19.cloned.1.call-done = bf16[768,3072]{1,0:T(8,128)(2,1)} async-done(((bf16[24,3072]{1,0:T(8,128)(2,1)}), bf16[768,3072]{1,0:T(8,128)(2,1)}) %all-gather.19.cloned.1.call-update) | async-done | bytes 4718608 | tf_op jit(solution)/shard_map/all_gather | solution.py:309
  449.3 15.4 fusion.116
  464.8 50.0 %all-gather.21.cloned.1.call-done = bf16[3072,768]{1,0:T(8,128)(2,1)} async-done(((bf16[96,768]{1,0:T(8,128)(2,1)}), bf16[3072,768]{1,0:T(8,128)(2,1)}) %all-gather.21.cloned.1.call-update) | async-done | bytes 4718608 | tf_op jit(solution)/shard_map/all_gather | solution.py:310
  514.7 22.9 %fusion.6 = bf16[8,196,3072]{2,1,0:T(8,128)(2,1)} fusion(f32[8,196,3072]{2,1,0:T(8,128)} %fusion.116, bf16[3072,768]{1,0:T(8,128)(2,1)} %all-gather.21.cloned.1.call-done, bf16[1,8,196,768]{3,1,2,0:T(8,128)(2,1)S(1)} %copy-done.35), kind=kOutput, calls=%fused_computation.10 | convolution fusion | flops 7495090176 | bytes 36028416 | tf_op jit(solution)/shard_map/cfpe,de->cfpd/dot_general | solution.py:91
  537.6 13.4 fusion.62
  551.2 84.6 %all-gather.23.cloned.1.call-done = bf16[1,16,196,1536]{3,1,2,0:T(8,128)(2,1)} async-done(((bf16[1,8,196,1536]{3,1,2,0:T(8,128)(2,1)}), bf16[1,16,196,1536]{3,1,2,0:T(8,128)(2,1)}) %all-gather.23.cloned.1.call-update) | async-done | bytes 9633808 | tf_op jit(solution)/shard_map/all_gather | solution.py:121
  653.2 13.9 copy.170
  676.2 14.0 copy.171
  690.2 9.7 multiply_reduce_fusion.6
  734.1 12.4 fusion.114
  746.5 21.5 %fusion.13 = bf16[8,196,3072]{2,1,0:T(8,128)(2,1)} fusion(f32[8,196,3072]{2,1,0:T(8,128)} %fusion.114, bf16[3072,768]{1,0:T(8,128)(2,1)S(1)} %bitcast.545, bf16[1,8,196,768]{3,1,2,0:T(8,128)(2,1)S(1)} %copy-done.32), kind=kOutput, calls=%fused_computation.17 | convolution fusion | flops 7495090176 | bytes 36028416 | tf_op jit(solution)/shard_map/cfpe,de->cfpd/dot_general | solution.py:91
  768.0 12.0 fusion.110
  810.8 14.4 multiply_reduce_fusion.5
  825.2 15.5 convert_bitcast_fusion.1
  840.7 13.7 copy.185
  862.5 10.0 multiply_convert_fusion.9
  880.6 13.7 copy.182
  902.4 9.8 pad_maximum_fusion
  936.9 14.7 convert_bitcast_fusion
  951.6 13.9 copy.204
  973.7 13.4 multiply_reduce_fusion.4
  987.1 9.5 multiply_convert_fusion.7
  1007.0 13.9 copy.201
  1029.0 9.8 pad_maximum_fusion.1
  1041.2 18.9 fusion.166
  1060.1 20.8 %bitcast_add_fusion = f32[3072,768]{1,0:T(8,128)} fusion(f32[3072,768,1]{1,0,2:T(8,128)} %fusion.166, bf16[1,8,196,768]{3,1,2,0:T(8,128)(2,1)S(1)} %copy-done.34, f32[8,196,3072]{2,1,0:T(8,128)} %fusion.114), kind=kOutput, calls=%fused_computation.67 | convolution fusion | flops 7444463616 | bytes 40550400 | tf_op jit(solution)/shard_map/cfpd,cfpe->de/dot_general | solution.py:95
  1080.9 11.0 reshape.773
  1092.0 15.9 fusion.222
  1107.9 16.5 fusion.30
  1124.5 9.8 copy.254
  1175.1 12.6 fusion.64
  1187.7 12.5 fusion.96
  1200.2 9.6 fusion.95
  1232.1 11.9 fusion.139
  1244.1 15.2 multiply_reduce_fusion
  1259.2 18.0 multiply_convert_fusion
  1277.3 9.7 multiply_bitcast_fusion
  1302.6 11.9 fusion.136
  1314.5 15.0 multiply_reduce_fusion.1
  1329.5 18.1 multiply_convert_fusion.1
  1347.6 9.8 multiply_bitcast_fusion.2
  1365.9 13.4 bitcast_add_fusion.2
  1431.8 15.9 fusion.195
  1447.7 15.5 bitcast_add_fusion.3
  1471.2 18.2 fusion.78
  1489.4 17.1 fusion.77
  1510.3 13.6 fusion.59
  1523.9 12.1 fusion.122
  1543.9 40.8 %all-reduce.12 = (f32[768]{0:T(1024)S(1)}, f32[768]{0:T(1024)S(1)}, f32[768]{0:T(1024)S(1)}) all-reduce(f32[768]{0:T(1024)S(1)} %add.213, f32[768]{0:T(1024)S(1)} %add.214, f32[768]{0:T(1024)S(1)} %add.215), channel_id=4, replica_groups=mesh['clip'=16,'frame'=2] {'clip','frame'}, use_global_device_ids=true, to_apply=%region_40.0.clone | all-reduce | flops 2304 | bytes 18432
  1603.5 426.6 %all-reduce.17.cloned.1.call-done = (f32[1769472]{0:T(1024)}, f32[589824]{0:T(1024)}, f32[1769472]{0:T(1024)}, f32[589824]{0:T(1024)}, f32[2359296]{0:T(1024)}, /*index=5*/f32[2359296]{0:T(1024)}) async-done(((f32[1769472]{0:T(1024)}, f32[589824]{0:T(1024)}, f32[1769472]{0:T(1024)}, f32[589824]{0:T(1024)}, f32[2359296]{0:T(1024)}, /*index=5*/f32[2359296]{0:T(1024)}), (f32[1769472]{0:T(1024)}, ...) | async-done | bytes 37748752
  (432 shorter events, 532.6 us)
Async XLA Ops:
  7.2 66.8 %all-gather.9.cloned.1.call-start = ((), (), s32[]{:S(2)}) async-start(), calls=%async_computation.2 | async-start | bytes 3649536 | tf_op jit(solution)/shard_map/all_gather | solution.py:305
  7.9 125.9 %all-gather.11.cloned.1.call-start = ((), (), s32[]{:S(2)}) async-start(), calls=%async_computation.3 | async-start | bytes 1216512 | tf_op jit(solution)/shard_map/all_gather | solution.py:306
  8.7 183.2 %all-gather.13.cloned.1.call-start = ((), (), s32[]{:S(2)}) async-start(), calls=%async_computation.4 | async-start | bytes 3649536 | tf_op jit(solution)/shard_map/all_gather | solution.py:307
  9.4 317.6 %all-gather.15.cloned.1.call-start = ((), (), s32[]{:S(2)}) async-start(), calls=%async_computation.5 | async-start | bytes 14450688 | tf_op jit(solution)/shard_map/all_gather | solution.py:121
  54.1 164.5 %copy-start.73 = (f32[768]{0:T(1024)}, f32[768]{0:T(1024)S(1)}, u32[]{:S(2)}) copy-start(f32[768]{0:T(1024)S(1)} %convert_element_type.279) | copy-start | bytes 9220
  54.1 240.3 %copy-start.61 = (f32[768]{0:T(1024)}, f32[768]{0:T(1024)S(1)}, u32[]{:S(2)}) copy-start(f32[768]{0:T(1024)S(1)} %convert_element_type.286) | copy-start | bytes 9220
  56.8 232.3 %copy-start.5 = (bf16[1,8,196,768]{3,1,2,0:T(8,128)(2,1)}, bf16[1,8,196,768]{3,1,2,0:T(8,128)(2,1)S(1)}, u32[]{:S(2)}) copy-start(bf16[1,8,196,768]{3,1,2,0:T(8,128)(2,1)S(1)} %get-tuple-element.81) | copy-start | bytes 7225348
  58.3 27.7 %copy-start.65 = (f32[8,196]{1,0:T(8,128)}, f32[8,196]{1,0:T(8,128)S(1)}, u32[]{:S(2)}) copy-start(f32[8,196]{1,0:T(8,128)S(1)} %broadcast_multiply_fusion.17) | copy-start | bytes 18820
  59.3 26.7 %copy-start.76 = (f32[8,196]{1,0:T(8,128)}, f32[8,196]{1,0:T(8,128)S(1)}, u32[]{:S(2)}) copy-start(f32[8,196]{1,0:T(8,128)S(1)} %add_rsqrt_fusion.5) | copy-start | bytes 18820
  109.9 12.0 copy-start.49
  122.0 11.8 copy-start.55
  139.5 61.6 %copy-start.69 = (f32[8,196]{1,0:T(8,128)}, f32[8,196]{1,0:T(8,128)S(1)}, u32[]{:S(2)}) copy-start(f32[8,196]{1,0:T(8,128)S(1)} %broadcast_multiply_fusion.16) | copy-start | bytes 18820
  142.3 58.8 %copy-start.78 = (f32[8,196]{1,0:T(8,128)}, f32[8,196]{1,0:T(8,128)S(1)}, u32[]{:S(2)}) copy-start(f32[8,196]{1,0:T(8,128)S(1)} %add_rsqrt_fusion.4) | copy-start | bytes 18820
  207.9 206.1 %all-gather.17.cloned.1.call-start = ((), (), s32[]{:S(2)}) async-start(), calls=%async_computation.6 | async-start | bytes 1216512 | tf_op jit(solution)/shard_map/all_gather | solution.py:308
  208.5 240.8 %all-gather.19.cloned.1.call-start = ((), (), s32[]{:S(2)}) async-start(), calls=%async_computation.7 | async-start | bytes 4866048 | tf_op jit(solution)/shard_map/all_gather | solution.py:309
  209.1 305.6 %all-gather.21.cloned.1.call-start = ((), (), s32[]{:S(2)}) async-start(), calls=%async_computation.8 | async-start | bytes 4866048 | tf_op jit(solution)/shard_map/all_gather | solution.py:310
  209.8 426.0 %all-gather.23.cloned.1.call-start = ((), (), s32[]{:S(2)}) async-start(), calls=%async_computation.9 | async-start | bytes 14450688 | tf_op jit(solution)/shard_map/all_gather | solution.py:121
  212.2 15.1 copy-start.67
  266.7 11.9 copy-start.51
  278.6 10.5 copy-start.57
  278.6 12.1 copy-start.90
  323.1 852.0 %reduce-scatter.3.cloned.1.call-start = ((), (), s32[]{:S(2)}) async-start(), calls=%async_computation.10 | async-start | bytes 14745600 | tf_op jit(solution)/shard_map/reduce_scatter | solution.py:211
  420.2 29.1 %copy-start.75 = (f32[768]{0:T(1024)S(1)}, f32[768]{0:T(1024)}, u32[]{:S(2)}) copy-start(f32[768]{0:T(1024)} %convert_element_type.295) | copy-start | bytes 9220
  420.2 364.7 %copy-start.71 = (f32[8,196]{1,0:T(8,128)}, f32[8,196]{1,0:T(8,128)S(1)}, u32[]{:S(2)}) copy-start(f32[8,196]{1,0:T(8,128)S(1)} %broadcast_multiply_fusion.15) | copy-start | bytes 18820
  423.0 361.9 %copy-start.80 = (f32[8,196]{1,0:T(8,128)}, f32[8,196]{1,0:T(8,128)S(1)}, u32[]{:S(2)}) copy-start(f32[8,196]{1,0:T(8,128)S(1)} %add_rsqrt_fusion.3) | copy-start | bytes 18820
  423.0 91.7 %copy-start.35 = (bf16[1,8,196,768]{3,1,2,0:T(8,128)(2,1)S(1)}, bf16[1,8,196,768]{3,1,2,0:T(8,128)(2,1)}, u32[]{:S(2)}) copy-start(bf16[1,8,196,768]{3,1,2,0:T(8,128)(2,1)} %get-tuple-element.78) | copy-start | bytes 7225348
  449.3 88.3 %slice-start.10 = ((s8[4915200]{0:T(1024)(128)(4,1)}), s8[720896]{0:T(1024)(128)(4,1)S(1)}, s32[]{:S(2)}) async-start(s8[4915200]{0:T(1024)(128)(4,1)} %bitcast.491), calls=%async_computation.23 | async-start | bytes 1441792
  514.7 22.9 %slice-start.11 = ((s8[4915200]{0:T(1024)(128)(4,1)}), s8[4194304]{0:T(1024)(128)(4,1)S(1)}, s32[]{:S(2)}) async-start(s8[4915200]{0:T(1024)(128)(4,1)} %bitcast.491), calls=%async_computation.24 | async-start | bytes 8388608
  514.7 22.9 %copy-start.87 = (bf16[768,3072]{1,0:T(8,128)(2,1)S(1)}, bf16[768,3072]{1,0:T(8,128)(2,1)}, u32[]{:S(2)}) copy-start(bf16[768,3072]{1,0:T(8,128)(2,1)} %all-gather.19.cloned.1.call-done) | copy-start | bytes 14155780
  537.6 13.4 copy-start.24
  537.6 13.4 copy-start.42
  699.9 10.5 copy-start.21
  733.3 51.7 %copy-start.3 = (f32[1,8,196,768]{3,2,1,0:T(8,128)}, f32[1,8,196,768]{3,2,1,0:T(8,128)S(1)}, u32[]{:S(2)}) copy-start(f32[1,8,196,768]{3,2,1,0:T(8,128)S(1)} %get-tuple-element.92) | copy-start | bytes 14450692
  733.3 13.2 slice-start.24
  734.1 12.4 copy-start.32
  734.1 12.4 slice-start.25
  734.1 50.9 %slice-start.12 = ((s8[4915200]{0:T(1024)(128)(4,1)}), s8[4194304]{0:T(1024)(128)(4,1)S(1)}, s32[]{:S(2)}) async-start(s8[4915200]{0:T(1024)(128)(4,1)} %bitcast.493), calls=%async_computation.25 | async-start | bytes 8388608
  746.5 38.5 %slice-start.13 = ((s8[4915200]{0:T(1024)(128)(4,1)}), s8[720896]{0:T(1024)(128)(4,1)S(1)}, s32[]{:S(2)}) async-start(s8[4915200]{0:T(1024)(128)(4,1)} %bitcast.493), calls=%async_computation.26 | async-start | bytes 1441792
  854.3 20.3 slice-start.8
  862.5 12.2 slice-start.9
  912.2 288.0 %reduce-scatter.5.cloned.1.call-start = ((), (), s32[]{:S(2)}) async-start(), calls=%async_computation.11 | async-start | bytes 14745600 | tf_op jit(solution)/shard_map/reduce_scatter | solution.py:211
  1038.9 991.2 %all-reduce.17.cloned.1.call-start = ((), (), s32[]{:S(2)}) async-start(), calls=%async_computation.12 | async-start | bytes 75497472
  1041.2 18.9 copy-start.34
  1080.9 11.0 copy-start.72
  1080.9 11.0 copy-start.81
  1080.9 27.0 %slice-start.4 = ((s8[4915200]{0:T(1024)(128)(4,1)}), s8[720896]{0:T(1024)(128)(4,1)S(1)}, s32[]{:S(2)}) async-start(s8[4915200]{0:T(1024)(128)(4,1)} %bitcast.475), calls=%async_computation.17 | async-start | bytes 1441792
  1091.9 16.0 slice-start.5
  1092.0 42.3 %slice-start.20 = ((s8[4915200]{0:T(1024)(128)(4,1)}), s8[4194304]{0:T(1024)(128)(4,1)S(1)}, s32[]{:S(2)}) async-start(s8[4915200]{0:T(1024)(128)(4,1)} %bitcast.514), calls=%async_computation.33 | async-start | bytes 8388608
  1092.0 44.7 %slice-start.14 = ((s8[4915200]{0:T(1024)(128)(4,1)}), s8[4194304]{0:T(1024)(128)(4,1)S(1)}, s32[]{:S(2)}) async-start(s8[4915200]{0:T(1024)(128)(4,1)} %bitcast.508), calls=%async_computation.27 | async-start | bytes 8388608
  1107.9 26.3 %slice-start.21 = ((s8[4915200]{0:T(1024)(128)(4,1)}), s8[720896]{0:T(1024)(128)(4,1)S(1)}, s32[]{:S(2)}) async-start(s8[4915200]{0:T(1024)(128)(4,1)} %bitcast.514), calls=%async_computation.34 | async-start | bytes 1441792
  1107.9 28.8 %slice-start.15 = ((s8[4915200]{0:T(1024)(128)(4,1)}), s8[720896]{0:T(1024)(128)(4,1)S(1)}, s32[]{:S(2)}) async-start(s8[4915200]{0:T(1024)(128)(4,1)} %bitcast.508), calls=%async_computation.28 | async-start | bytes 1441792
  1175.1 12.6 copy-start.46
  1175.1 12.6 copy-start.86
  1187.7 12.5 copy-start.30
  1187.7 23.0 %slice-start = ((s8[4915200]{0:T(1024)(128)(4,1)}), s8[720896]{0:T(1024)(128)(4,1)S(1)}, s32[]{:S(2)}) async-start(s8[4915200]{0:T(1024)(128)(4,1)} %bitcast.471), calls=%async_computation.13 | async-start | bytes 1441792
  1277.3 18.4 slice-start.16
  1347.6 18.3 slice-start.2
  1431.8 15.9 copy-start.6
  1431.8 15.9 copy-start.64
  1431.8 15.9 copy-start.68
  1471.2 18.3 slice-start.6
  1471.2 18.2 slice-start.7
  1510.3 28.0 %slice-start.18 = ((s8[4915200]{0:T(1024)(128)(4,1)}), s8[4194304]{0:T(1024)(128)(4,1)S(1)}, s32[]{:S(2)}) async-start(s8[4915200]{0:T(1024)(128)(4,1)} %bitcast.512), calls=%async_computation.31 | async-start | bytes 8388608
  1523.8 14.4 slice-start.19
  (71 other events, 362.9 us)
Sparse Core Ops, SparseCore 0:
  10.9 62.9 all-gather.8
  76.8 52.9 all-gather.10
  132.7 59.1 all-gather.12
  208.0 118.9 all-gather.14
  329.8 54.1 all-gather.16
  386.7 62.5 all-gather.18
  452.2 62.4 all-gather.20
  516.8 118.9 all-gather.22
  912.4 114.7 reduce-scatter.2
  1039.0 114.9 reduce-scatter.4
  1471.3 558.7 all-reduce.16
where the time goes:
time: 2060 us; the launch traced here: 2050 us
  matrix products  661 us (32%)
  waiting for transfers between devices  659 us (32%)
  local copies, waits for them, and re-layouts  442 us (21%)
  other arithmetic  185 us (9%)
  blocking collectives  82.9 us (4%)
    unnamed x12, waiting for transfers between devices  431 us
    dot_general x12, matrix products, outer_sum(): jnp.einsum('cfpd,cfpe->de', values, gradient, preferred_element_type=jnp....  145 us
    dot_general x12, matrix products, project_back(): jnp.einsum('cfpe,de->cfpd', gradient, matrix, preferred_element_type=jnp....  133 us
    dot_general x12, matrix products, project(): jnp.einsum('cfpd,de->cfpe', values, matrix, preferred_element_type=jnp.fl...  120 us
    unnamed x270, local copies, waits for them, and re-layouts  97.6 us
    all_gather x2, waiting for transfers between devices, forward(): lax.all_gather(qkv_time[..., model_width:], 'frame', axis=1, tiled=True)  88.5 us
    reshape x8, local copies, waits for them, and re-layouts, to_places(): blocks.transpose(0, 2, 1, 3)  84.7 us
    unnamed x2, blocking collectives  82.9 us
  transfers between devices with their start and end apart: 11, of which 7 were waited for; matrix products, arithmetic and copies ran while one was open for 34% of the time, Pallas kernels for 0%

commit v1 on v0

--- a/solution.py
+++ b/solution.py
@@ -1,14 +1,549 @@
+import functools
+import math
+
 import jax
 import jax.numpy as jnp
 from jax import lax
+from jax.experimental import pallas as pl
+from jax.experimental.pallas import tpu as pltpu
 from jax.sharding import PartitionSpec as P
 
 HEADS = 12
 HEAD = 64
+PAIRS = HEADS // 2
+LANES = 2 * HEAD
+epsilon = 1e-06
+LOW = jnp.bfloat16
+WIDE = jnp.float32
+NN = (((1,), (0,)), ((), ()))
+NT = (((1,), (1,)), ((), ()))
+TN = (((0,), (0,)), ((), ()))
+SCALE = HEAD ** (-0.5)
+POWER = SCALE * math.log2(math.e)
+NEVER = -1e30
+GROUP = 8
+STEP = 2 * GROUP
+LIMIT = 60 << 20
+
+
+def dot(first, second, numbers=NN):
+    return lax.dot_general(first, second, numbers, preferred_element_type=WIDE)
+
+
+def norm_rows(values, gain):
+    centred = values - jnp.mean(values, axis=-1, keepdims=True)
+    inverse = lax.rsqrt(jnp.mean(centred * centred, axis=-1, keepdims=True) + epsilon)
+    normed = centred * inverse
+    return normed * gain, normed, inverse
+
+
+def norm_back(gradient, normed, inverse, gain):
+    scaled = gradient * gain
+    return inverse * (
+        scaled
+        - jnp.mean(scaled, axis=-1, keepdims=True)
+        - normed * jnp.mean(scaled * normed, axis=-1, keepdims=True)
+    )
+
+
+def fold_rows(values):
+    rows, width = values.shape
+    return jnp.sum(values.reshape(rows // 8, 8, width), axis=0)
+
+
+def split_heads(values):
+    first = lax.broadcasted_iota(jnp.int32, values.shape, 1) < HEAD
+    zero = jnp.zeros_like(values)
+    return jnp.where(first, values, zero), jnp.where(first, zero, values)
+
+
+def join_heads(first, second):
+    keep = lax.broadcasted_iota(jnp.int32, first.shape, 1) < HEAD
+    return jnp.where(keep, first, second)
+
+
+def stack_heads(values):
+    return jnp.concatenate(split_heads(values), axis=0)
+
+
+def pair(ref, rows, part, index):
+    start = (part * PAIRS + index) * LANES
+    return ref[rows, start : start + LANES]
+
+
+def load_padded(x_ref, pad_ref):
+    frames, places, width = x_ref.shape
+
+    @pl.when(pl.program_id(0) == 0)
+    def _():
+        pad_ref[...] = jnp.zeros_like(pad_ref)
+
+    for frame in range(frames):
+        pad_ref[frame, 0:places] = x_ref[frame].astype(WIDE)
+    return pad_ref[...].reshape(frames * pad_ref.shape[1], width)
+
+
+def space_forward_kernel(
+    places, x_ref, gain_ref, proj_ref, out_ref, in_ref, qkv_ref, o_ref, after_ref, pad_ref
+):
+    frames, padded, width = pad_ref.shape
+    values = load_padded(x_ref, pad_ref)
+    normed = norm_rows(values, gain_ref[...])[0].astype(LOW)
+    in_ref[...] = normed.reshape(frames, padded, width)
+    qkv_ref[...] = dot(normed, proj_ref[...]).astype(LOW).reshape(frames, padded, 3 * width)
+    real = lax.broadcasted_iota(jnp.int32, (padded, padded), 1) < places
+
+    def one_frame(frame, carry):
+        for index in range(PAIRS):
+            queries = qkv_ref[frame, :, index * LANES : (index + 1) * LANES]
+            start = width + index * LANES
+            keys = split_heads(qkv_ref[frame, :, start : start + LANES])
+            start = 2 * width + index * LANES
+            value_block = qkv_ref[frame, :, start : start + LANES]
+            outs = []
+            for head in range(2):
+                scores = jnp.where(real, dot(queries, keys[head], NT), NEVER)
+                powers = jnp.exp2((scores - jnp.max(scores, axis=1, keepdims=True)) * POWER)
+                chances = powers * (1.0 / jnp.sum(powers, axis=1, keepdims=True))
+                outs.append(dot(chances.astype(LOW), value_block))
+            o_ref[frame, :, index * LANES : (index + 1) * LANES] = join_heads(*outs).astype(LOW)
+        return carry
+
+    lax.fori_loop(0, frames, one_frame, 0)
+    after = values + dot(o_ref[...].reshape(frames * padded, width), out_ref[...])
+    after = after.reshape(frames, padded // GROUP, GROUP, width)
+    for frame in range(frames):
+        after_ref[:, frame] = after[frame]
+
+
+def middle_kernel(
+    places,
+    ao_ref,
+    ar_ref,
+    go_ref,
+    gr_ref,
+    tgain_ref,
+    fgain_ref,
+    tproj_ref,
+    tout_ref,
+    up_ref,
+    down_ref,
+    qkv_ref,
+    int_ref,
+    ot_ref,
+    inf_ref,
+    act_ref,
+    gh_ref,
+    gb_ref,
+    mo_ref,
+    mr_ref,
+    gt_ref,
+    gain_ref,
+):
+    half = ao_ref.shape[1]
+    frames = half + ar_ref.shape[1]
+    width = ao_ref.shape[3]
+    rows = 2 * frames * GROUP
+    block = frames * GROUP
+    values = jnp.concatenate([ao_ref[...], ar_ref[...]], axis=1).reshape(rows, width)
+    in_time = norm_rows(values, tgain_ref[...])[0].astype(LOW)
+    int_ref[...] = in_time
+    qkv_ref[...] = dot(in_time, tproj_ref[...]).astype(LOW)
+    across = lax.broadcasted_iota(jnp.int32, (block, block), 0)
+    down = lax.broadcasted_iota(jnp.int32, (block, block), 1)
+    bias = jnp.where(((across ^ down) & (GROUP - 1)) == 0, 0.0, NEVER)
+    for group in range(2):
+        own = slice(group * block, (group + 1) * block)
+        for index in range(PAIRS):
+            queries = pair(qkv_ref, own, 0, index)
+            keys = stack_heads(pair(qkv_ref, own, 1, index))
+            value_block = stack_heads(pair(qkv_ref, own, 2, index))
+            both = dot(queries, keys, NT)
+            chances = []
+            for head in range(2):
+                scores = both[:, head * block : (head + 1) * block] + bias
+                powers = jnp.exp2((scores - jnp.max(scores, axis=1, keepdims=True)) * POWER)
+                total = jnp.sum(powers, axis=1, keepdims=True)
+                chances.append((powers * (1.0 / total)).astype(LOW))
+            result = dot(jnp.concatenate(chances, axis=1), value_block)
+            ot_ref[own, index * LANES : (index + 1) * LANES] = result.astype(LOW)
+    values = values + dot(ot_ref[...], tout_ref[...])
+    feed_gain = fgain_ref[...]
+    in_feed, normed, inverse = norm_rows(values, feed_gain)
+    in_feed = in_feed.astype(LOW)
+    inf_ref[...] = in_feed
+    place = pl.program_id(0) * STEP + lax.broadcasted_iota(jnp.int32, (STEP, width), 0)
+    lows, highs = [], []
+    for ref in (go_ref, gr_ref):
+        for frame in range(half):
+            tile = jnp.where(place < places, ref[frame].astype(WIDE), 0.0)
+            lows.append(tile[:GROUP])
+            highs.append(tile[GROUP:])
+    gradient = jnp.concatenate(lows + highs, axis=0)
+    grad_low = gradient.astype(LOW)
+    gb_ref[...] = grad_low
+    hidden_width = up_ref.shape[1]
+    piece = 512
+    root = math.sqrt(2.0 / math.pi)
+    for start in range(0, hidden_width, piece):
+        cut = slice(start, start + piece)
+        hidden = dot(in_feed, up_ref[:, cut])
+        back = dot(grad_low, down_ref[cut, :], NT)
+        square = hidden * hidden
+        slope = jnp.tanh(hidden * (root + (root * 0.044715) * square))
+        plus = 0.5 * slope + 0.5
+        act_ref[:, cut] = (hidden * plus).astype(LOW)
+        inner = hidden * (0.5 * root + (1.5 * root * 0.044715) * square)
+        gh_ref[:, cut] = (back * (plus + inner * (1.0 - slope * slope))).astype(LOW)
+    mixed = values + dot(act_ref[...], down_ref[...])
+    for frame in range(frames):
+        low = mixed[frame * GROUP : (frame + 1) * GROUP]
+        high = mixed[block + frame * GROUP : block + (frame + 1) * GROUP]
+        tile = jnp.concatenate([low, high], axis=0).astype(LOW)
+        if frame < half:
+            mo_ref[frame] = tile
+        else:
+            mr_ref[frame - half] = tile
+    back = dot(gh_ref[...], up_ref[...], NT)
+    gt_ref[...] = gradient + norm_back(back, normed, inverse, feed_gain)
+
+    @pl.when(pl.program_id(0) == 0)
+    def _():
+        gain_ref[...] = jnp.zeros_like(gain_ref)
+
+    gain_ref[...] += fold_rows(back * normed)
+
+
+def time_backward_kernel(
+    qkv_ref,
+    gt_ref,
+    ao_ref,
+    ar_ref,
+    tgain_ref,
+    tout_ref,
+    tproj_ref,
+    gq_ref,
+    tb_ref,
+    gso_ref,
+    gsr_ref,
+    gain_ref,
+    d_ref,
+):
+    half = ao_ref.shape[1]
+    frames = half + ar_ref.shape[1]
+    width = ao_ref.shape[3]
+    rows = 2 * frames * GROUP
+    block = frames * GROUP
+    tb = gt_ref[...].astype(LOW)
+    tb_ref[...] = tb
+    d_ref[...] = dot(tb, tout_ref[...], NT).astype(LOW)
+    across = lax.broadcasted_iota(jnp.int32, (block, block), 0)
+    down = lax.broadcasted_iota(jnp.int32, (block, block), 1)
+    bias = jnp.where(((across ^ down) & (GROUP - 1)) == 0, 0.0, NEVER)
+    for group in range(2):
+        own = slice(group * block, (group + 1) * block)
+        for index in range(PAIRS):
+            queries = pair(qkv_ref, own, 0, index)
+            keys = stack_heads(pair(qkv_ref, own, 1, index))
+            value_block = stack_heads(pair(qkv_ref, own, 2, index))
+            grad = pair(d_ref, own, 0, index)
+            both = dot(keys, queries, NT)
+            grad_both = dot(value_block, grad, NT)
+            chances, grads = [], []
+            for head in range(2):
+                cut = slice(head * block, (head + 1) * block)
+                scores = both[cut] + bias
+                powers = jnp.exp2((scores - jnp.max(scores, axis=0, keepdims=True)) * POWER)
+                share = powers * (1.0 / jnp.sum(powers, axis=0, keepdims=True))
+                grad_share = grad_both[cut]
+                mean = jnp.sum(share * grad_share, axis=0, keepdims=True)
+                chances.append(share.astype(LOW))
+                grads.append((share * (grad_share - mean)).astype(LOW))
+            dv = dot(jnp.concatenate(chances, axis=1), stack_heads(grad))
+            dk = dot(jnp.concatenate(grads, axis=1), stack_heads(queries)) * SCALE
+            dq = dot(jnp.concatenate(grads, axis=0), keys, TN) * SCALE
+            for part, item in enumerate((dq, dk, dv)):
+                start = (part * PAIRS + index) * LANES
+                gq_ref[own, start : start + LANES] = item.astype(LOW)
+    values = jnp.concatenate([ao_ref[...], ar_ref[...]], axis=1).reshape(rows, width)
+    gain = tgain_ref[...]
+    _, normed, inverse = norm_rows(values, gain)
+    back = dot(gq_ref[...], tproj_ref[...], NT)
+    result = gt_ref[...] + norm_back(back, normed, inverse, gain)
+    for frame in range(frames):
+        low = result[frame * GROUP : (frame + 1) * GROUP]
+        high = result[block + frame * GROUP : block + (frame + 1) * GROUP]
+        tile = jnp.concatenate([low, high], axis=0)
+        if frame < half:
+            gso_ref[frame] = tile
+        else:
+            gsr_ref[frame - half] = tile
+
+    @pl.when(pl.program_id(0) == 0)
+    def _():
+        gain_ref[...] = jnp.zeros_like(gain_ref)
+
+    gain_ref[...] += fold_rows(back * normed)
+
+
+def space_backward_kernel(
+    places,
+    x_ref,
+    gs_ref,
+    qkv_ref,
+    gain_row_ref,
+    out_ref,
+    proj_ref,
+    gq_ref,
+    sb_ref,
+    gx_ref,
+    gain_ref,
+    pad_ref,
+    d_ref,
+):
+    frames, padded, width = pad_ref.shape
+    values = load_padded(x_ref, pad_ref)
+    grad_space = gs_ref[...].reshape(frames * padded, width)
+    sb = grad_space.astype(LOW)
+    sb_ref[...] = sb.reshape(frames, padded, width)
+    d_ref[...] = dot(sb, out_ref[...], NT).astype(LOW).reshape(frames, padded, width)
+    real = lax.broadcasted_iota(jnp.int32, (padded, padded), 0) < places
+
+    def one_frame(frame, carry):
+        for index in range(PAIRS):
+            queries = qkv_ref[frame, :, index * LANES : (index + 1) * LANES]
+            start = width + index * LANES
+            key_block = qkv_ref[frame, :, start : start + LANES]
+            start = 2 * width + index * LANES
+            value_block = qkv_ref[frame, :, start : start + LANES]
+            grad = d_ref[frame, :, index * LANES : (index + 1) * LANES]
+            keys = split_heads(key_block)
+            vals = split_heads(value_block)
+            outs = []
+            for head in range(2):
+                scores = jnp.where(real, dot(keys[head], queries, NT), NEVER)
+                powers = jnp.exp2((scores - jnp.max(scores, axis=0, keepdims=True)) * POWER)
+                share = powers * (1.0 / jnp.sum(powers, axis=0, keepdims=True))
+                grad_share = dot(vals[head], grad, NT)
+                mean = jnp.sum(share * grad_share, axis=0, keepdims=True)
+                ds = (share * (grad_share - mean)).astype(LOW)
+                outs.append(
+                    (
+                        dot(ds, key_block, TN) * SCALE,
+                        dot(ds, queries) * SCALE,
+                        dot(share.astype(LOW), grad),
+                    )
+                )
+            for part in range(3):
+                start = part * width + index * LANES
+                gq_ref[frame, :, start : start + LANES] = join_heads(
+                    outs[0][part], outs[1][part]
+                ).astype(LOW)
+        return carry
+
+    lax.fori_loop(0, frames, one_frame, 0)
+    gain = gain_row_ref[...]
+    _, normed, inverse = norm_rows(values, gain)
+    back = dot(gq_ref[...].reshape(frames * padded, 3 * width), proj_ref[...], NT)
+    result = grad_space + norm_back(back, normed, inverse, gain)
+    result = result.reshape(frames, padded, width)
+    for frame in range(frames):
+        gx_ref[frame] = result[frame, 0:places].astype(gx_ref.dtype)
+
+    @pl.when(pl.program_id(0) == 0)
+    def _():
+        gain_ref[...] = jnp.zeros_like(gain_ref)
+
+    gain_ref[...] += fold_rows(back * normed)
+
+
+def whole(shape):
+    return pl.BlockSpec(
+        shape, lambda *_: (0,) * len(shape), pipeline_mode=pl.Buffered(buffer_count=1)
+    )
+
+
+def params():
+    return pltpu.CompilerParams(vmem_limit_bytes=LIMIT)
+
+
+def cost(flops, *arrays):
+    size = sum(math.prod(item.shape) * jnp.dtype(item.dtype).itemsize for item in arrays)
+    return pl.CostEstimate(flops=int(flops), bytes_accessed=int(size), transcendentals=0)
+
+
+def padded_places(places):
+    return -(-places // STEP) * STEP
+
+
+def by_frame(count, *tail):
+    return pl.BlockSpec((count,) + tail, lambda step: (step,) + (0,) * len(tail))
+
+
+def space_forward(x, gain, proj, out):
+    frames, places, width = x.shape
+    padded = padded_places(places)
+    groups = padded // GROUP
+    rows = frames * padded
+    outs = (
+        jax.ShapeDtypeStruct((frames, padded, width), LOW),
+        jax.ShapeDtypeStruct((frames, padded, 3 * width), LOW),
+        jax.ShapeDtypeStruct((frames, padded, width), LOW),
+        jax.ShapeDtypeStruct((groups, frames, GROUP, width), WIDE),
+    )
+    flops = 2 * rows * width * 4 * width + 8 * rows * padded * width
+    return pl.pallas_call(
+        functools.partial(space_forward_kernel, places),
+        grid=(frames // 2,),
+        in_specs=[by_frame(2, places, width), whole(gain.shape), whole(proj.shape), whole(out.shape)],
+        out_specs=[
+            by_frame(2, padded, width),
+            by_frame(2, padded, 3 * width),
+            by_frame(2, padded, width),
+            pl.BlockSpec((groups, 2, GROUP, width), lambda step: (0, step, 0, 0)),
+        ],
+        out_shape=outs,
+        scratch_shapes=[pltpu.VMEM((2, padded, width), WIDE)],
+        compiler_params=params(),
+        cost_estimate=cost(flops, x, proj, out, *outs),
+        name="space_forward",
+    )(x, gain, proj, out)
+
+
+def middle(after_own, after_rest, g_own, g_rest, tgain, fgain, tproj, tout, up, down):
+    groups, half, _, width = after_own.shape
+    places = g_own.shape[1]
+    frames = 2 * half
+    rows = groups * frames * GROUP
+    block = 2 * frames * GROUP
+    hidden = up.shape[1]
+    padded = groups * GROUP
+    outs = (
+        jax.ShapeDtypeStruct((rows, 3 * width), LOW),
+        jax.ShapeDtypeStruct((rows, width), LOW),
+        jax.ShapeDtypeStruct((rows, width), LOW),
+        jax.ShapeDtypeStruct((rows, width), LOW),
+        jax.ShapeDtypeStruct((rows, hidden), LOW),
+        jax.ShapeDtypeStruct((rows, hidden), LOW),
+        jax.ShapeDtypeStruct((rows, width), LOW),
+        jax.ShapeDtypeStruct((half, places, width), LOW),
+        jax.ShapeDtypeStruct((half, places, width), LOW),
+        jax.ShapeDtypeStruct((rows, width), WIDE),
+        jax.ShapeDtypeStruct((8, width), WIDE),
+    )
+    by_row = lambda size: pl.BlockSpec((block, size), lambda step: (step, 0))
+    by_group = pl.BlockSpec((2, half, GROUP, width), lambda step: (step, 0, 0, 0))
+    by_place = pl.BlockSpec((half, STEP, width), lambda step: (0, step, 0))
+    flops = 2 * rows * width * (4 * width + 4 * hidden) + 8 * rows * frames * GROUP * width
+    return pl.pallas_call(
+        functools.partial(middle_kernel, places),
+        grid=(groups // 2,),
+        in_specs=[by_group, by_group, by_place, by_place]
+        + [whole(item.shape) for item in (tgain, fgain, tproj, tout, up, down)],
+        out_specs=[
+            by_row(3 * width),
+            by_row(width),
+            by_row(width),
+            by_row(width),
+            by_row(hidden),
+            by_row(hidden),
+            by_row(width),
+            by_place,
+            by_place,
+            by_row(width),
+            pl.BlockSpec((8, width), lambda step: (0, 0)),
+        ],
+        out_shape=outs,
+        compiler_params=params(),
+        cost_estimate=cost(flops, after_own, after_rest, g_own, g_rest, *outs),
+        name="middle",
+    )(after_own, after_rest, g_own, g_rest, tgain, fgain, tproj, tout, up, down)
+
+
+def time_backward(qkv, g_time, after_own, after_rest, tgain, tout, tproj):
+    groups, half, _, width = after_own.shape
+    frames = 2 * half
+    rows = groups * frames * GROUP
+    block = 2 * frames * GROUP
+    padded = groups * GROUP
+    outs = (
+        jax.ShapeDtypeStruct((rows, 3 * width), LOW),
+        jax.ShapeDtypeStruct((rows, width), LOW),
+        jax.ShapeDtypeStruct((half, padded, width), WIDE),
+        jax.ShapeDtypeStruct((half, padded, width), WIDE),
+        jax.ShapeDtypeStruct((8, width), WIDE),
+    )
+    by_row = lambda size: pl.BlockSpec((block, size), lambda step: (step, 0))
+    by_group = pl.BlockSpec((2, half, GROUP, width), lambda step: (step, 0, 0, 0))
+    by_place = pl.BlockSpec((half, STEP, width), lambda step: (0, step, 0))
+    flops = 2 * rows * width * 4 * width + 20 * rows * frames * GROUP * width
+    return pl.pallas_call(
+        time_backward_kernel,
+        grid=(groups // 2,),
+        in_specs=[by_row(3 * width), by_row(width), by_group, by_group]
+        + [whole(item.shape) for item in (tgain, tout, tproj)],
+        out_specs=[
+            by_row(3 * width),
+            by_row(width),
+            by_place,
+            by_place,
+            pl.BlockSpec((8, width), lambda step: (0, 0)),
+        ],
+        out_shape=outs,
+        scratch_shapes=[pltpu.VMEM((block, width), LOW)],
+        compiler_params=params(),
+        cost_estimate=cost(flops, qkv, g_time, after_own, after_rest, *outs),
+        name="time_backward",
+    )(qkv, g_time, after_own, after_rest, tgain, tout, tproj)
+
+
+def space_backward(x, g_space, qkv, gain, out, proj, kind):
+    frames, places, width = x.shape
+    padded = padded_places(places)
+    rows = frames * padded
+    outs = (
+        jax.ShapeDtypeStruct((frames, padded, 3 * width), LOW),
+        jax.ShapeDtypeStruct((frames, padded, width), LOW),
+        jax.ShapeDtypeStruct((frames, places, width), kind),
+        jax.ShapeDtypeStruct((8, width), WIDE),
+    )
+    flops = 2 * rows * width * 4 * width + 20 * rows * padded * width
+    return pl.pallas_call(
+        functools.partial(space_backward_kernel, places),
+        grid=(frames // 2,),
+        in_specs=[
+            by_frame(2, places, width),
+            by_frame(2, padded, width),
+            by_frame(2, padded, 3 * width),
+            whole(gain.shape),
+            whole(out.shape),
+            whole(proj.shape),
+        ],
+        out_specs=[
+            by_frame(2, padded, 3 * width),
+            by_frame(2, padded, width),
+            by_frame(2, places, width),
+            pl.BlockSpec((8, width), lambda step: (0, 0)),
+        ],
+        out_shape=outs,
+        scratch_shapes=[
+            pltpu.VMEM((2, padded, width), WIDE),
+            pltpu.VMEM((2, padded, width), LOW),
+        ],
+        compiler_params=params(),
+        cost_estimate=cost(flops, x, g_space, qkv, *outs),
+        name="space_backward",
+    )(x, g_space, qkv, gain, out, proj)
+
+
+def weight_gradient(values, gradient):
+    rows = math.prod(values.shape[:-1])
+    return dot(
+        values.reshape(rows, values.shape[-1]), gradient.reshape(rows, gradient.shape[-1]), TN
+    ).astype(LOW)
+
+
 MICRO = 2
-
-
-epsilon = 1e-06
 
 
 def norm_forward(values, gain):
@@ -262,7 +797,7 @@
     )
 
 
-def shards(
+def general(
     tokens,
     cotangent,
     space_gain,
@@ -294,38 +829,27 @@
             for piece in owned
         )
     )
+    gathered = (
+        lax.all_gather(space_gain, ("clip", "frame"), axis=0, tiled=True),
+        lax.all_gather(time_gain, ("clip", "frame"), axis=0, tiled=True),
+        lax.all_gather(feed_gain, ("clip", "frame"), axis=0, tiled=True),
+        lax.all_gather(space_proj, ("clip", "frame"), axis=0, tiled=True),
+        lax.all_gather(space_out, ("clip", "frame"), axis=0, tiled=True),
+        lax.all_gather(time_proj, ("clip", "frame"), axis=0, tiled=True),
+        lax.all_gather(time_out, ("clip", "frame"), axis=0, tiled=True),
+        lax.all_gather(up_proj, ("clip", "frame"), axis=0, tiled=True),
+        lax.all_gather(down_proj, ("clip", "frame"), axis=0, tiled=True),
+    )
     mixed_parts = []
     grad_parts = []
     for micro_index in range(MICRO):
         sample = tokens[micro_index * per_micro : (micro_index + 1) * per_micro].astype(jnp.float32)
-        gathered = (
-            lax.all_gather(space_gain, ("clip", "frame"), axis=0, tiled=True),
-            lax.all_gather(time_gain, ("clip", "frame"), axis=0, tiled=True),
-            lax.all_gather(feed_gain, ("clip", "frame"), axis=0, tiled=True),
-            lax.all_gather(space_proj, ("clip", "frame"), axis=0, tiled=True),
-            lax.all_gather(space_out, ("clip", "frame"), axis=0, tiled=True),
-            lax.all_gather(time_proj, ("clip", "frame"), axis=0, tiled=True),
-            lax.all_gather(time_out, ("clip", "frame"), axis=0, tiled=True),
-            lax.all_gather(up_proj, ("clip", "frame"), axis=0, tiled=True),
-            lax.all_gather(down_proj, ("clip", "frame"), axis=0, tiled=True),
-        )
         result, saved = forward(sample, gathered)
         mixed_parts.append(result.astype(jnp.bfloat16))
-        back_weights = (
-            lax.all_gather(space_gain, ("clip", "frame"), axis=0, tiled=True),
-            lax.all_gather(time_gain, ("clip", "frame"), axis=0, tiled=True),
-            lax.all_gather(feed_gain, ("clip", "frame"), axis=0, tiled=True),
-            lax.all_gather(space_proj, ("clip", "frame"), axis=0, tiled=True),
-            lax.all_gather(space_out, ("clip", "frame"), axis=0, tiled=True),
-            lax.all_gather(time_proj, ("clip", "frame"), axis=0, tiled=True),
-            lax.all_gather(time_out, ("clip", "frame"), axis=0, tiled=True),
-            lax.all_gather(up_proj, ("clip", "frame"), axis=0, tiled=True),
-            lax.all_gather(down_proj, ("clip", "frame"), axis=0, tiled=True),
-        )
         gradient = cotangent[micro_index * per_micro : (micro_index + 1) * per_micro].astype(
             jnp.float32
         )
-        grad_input, grads = backward(gradient, saved, back_weights)
+        grad_input, grads = backward(gradient, saved, gathered)
         grad_parts.append(grad_input)
         totals = tuple((first + second for first, second in zip(totals, grads)))
     flat = tuple((item.reshape(-1) for item in totals))
@@ -358,6 +882,113 @@
     )
 
 
+def swap_axis(values, axis):
+    size = lax.axis_size(axis)
+    return lax.ppermute(values, axis, [(index, size - 1 - index) for index in range(size)])
+
+
+def own_first(mine, other, place):
+    return jnp.where(
+        place == 0, jnp.stack([mine, other], axis=0), jnp.stack([other, mine], axis=0)
+    )
+
+
+def gain_row(values):
+    return values.astype(WIDE).reshape(1, -1)
+
+
+def clip_local(
+    tokens,
+    cotangent,
+    space_gain,
+    time_gain,
+    feed_gain,
+    space_proj,
+    space_out,
+    time_proj,
+    time_out,
+    up_proj,
+    down_proj,
+):
+    axes = ("clip", "frame")
+    place = lax.axis_index("frame")
+    width = tokens.shape[-1]
+    collect = lambda item: lax.all_gather(item, axes, axis=0, tiled=True)
+
+    gains = jnp.stack([space_gain, time_gain, feed_gain], axis=1)
+    gains = jnp.pad(gains, ((0, 0), (0, LANES - 3)))
+    space = collect(jnp.concatenate([space_proj, space_out, gains], axis=1))
+    time = collect(jnp.concatenate([time_proj, time_out], axis=1))
+    up = collect(up_proj)
+    down = collect(down_proj)
+    rest = swap_axis(lax.dynamic_index_in_dim(tokens, 1 - place, 0, keepdims=False), "frame")
+    g_rest = swap_axis(lax.dynamic_index_in_dim(cotangent, 1 - place, 0, keepdims=False), "frame")
+    own = lax.dynamic_index_in_dim(tokens, place, 0, keepdims=False)
+    g_own = lax.dynamic_index_in_dim(cotangent, place, 0, keepdims=False)
+
+    proj_width = 3 * width
+    table = space[:, 4 * width : 4 * width + 3].astype(WIDE).T
+    sgain, tgain, fgain = (table[index : index + 1] for index in range(3))
+    w_sproj, w_sout = space[:, :proj_width], space[:, proj_width : 4 * width]
+    w_tproj, w_tout = time[:, :proj_width], time[:, proj_width:]
+
+    in_o, qkv_o, o_o, after_o = space_forward(own, sgain, w_sproj, w_sout)
+    in_r, qkv_r, o_r, after_r = space_forward(rest, sgain, w_sproj, w_sout)
+    qkv_t, in_t, o_t, in_f, act, gh, gb, mixed_o, mixed_r, g_time, gain_f = middle(
+        after_o, after_r, g_own, g_rest, tgain, fgain, w_tproj, w_tout, up, down
+    )
+    mixed_other = swap_axis(mixed_r, "frame")
+    scatter = lambda item: lax.psum_scatter(item, axes, scatter_dimension=0, tiled=True)
+    d_down = scatter(weight_gradient(act, gb)).astype(WIDE)
+    d_up = scatter(weight_gradient(in_f, gh)).astype(WIDE)
+    gq_t, tb, gs_o, gs_r, gain_t = time_backward(
+        qkv_t, g_time, after_o, after_r, tgain, w_tout, w_tproj
+    )
+    d_time = scatter(
+        jnp.concatenate([weight_gradient(in_t, gq_t), weight_gradient(o_t, tb)], axis=1)
+    ).astype(WIDE)
+    gq_r, sb_r, gx_r, gain_sr = space_backward(rest, gs_r, qkv_r, sgain, w_sout, w_sproj, LOW)
+    grad_other = swap_axis(gx_r, "frame")
+    gq_o, sb_o, gx_o, gain_so = space_backward(own, gs_o, qkv_o, sgain, w_sout, w_sproj, WIDE)
+    gain_grads = jnp.stack(
+        [jnp.sum(item, axis=0) for item in (gain_so + gain_sr, gain_t, gain_f)], axis=1
+    )
+    gain_grads = jnp.pad(gain_grads, ((0, 0), (0, LANES - 3))).astype(LOW)
+    d_space = scatter(
+        jnp.concatenate(
+            [
+                weight_gradient(
+                    jnp.concatenate([in_o, in_r]), jnp.concatenate([gq_o, gq_r])
+                ),
+                weight_gradient(jnp.concatenate([o_o, o_r]), jnp.concatenate([sb_o, sb_r])),
+                gain_grads,
+            ],
+            axis=1,
+        )
+    ).astype(WIDE)
+    mixed = own_first(mixed_o, mixed_other, place)
+    grad_tokens = own_first(gx_o, grad_other.astype(WIDE), place)
+    return (
+        mixed,
+        grad_tokens,
+        d_space[:, 4 * width],
+        d_space[:, 4 * width + 1],
+        d_space[:, 4 * width + 2],
+        d_space[:, :proj_width],
+        d_space[:, proj_width : 4 * width],
+        d_time[:, :proj_width],
+        d_time[:, proj_width:],
+        d_up,
+        d_down,
+    )
+
+
+def shards(tokens, *others):
+    frames = lax.axis_size("frame")
+    local = frames == 2 and tokens.shape[0] == 2 and tokens.shape[1] == GROUP
+    return (clip_local if local else general)(tokens, *others)
+
+
 def solution(mesh):
     in_specs = (
         P("clip", "frame", None, None),

time: 2060 us -> 995 us (0.48)
  matrix products: 661 us -> 91 us
  local copies, waits for them, and re-layouts: 442 us -> 52.1 us
  Pallas kernels: 0 us -> 375 us
  waiting for transfers between devices: 659 us -> 428 us
  other arithmetic: 185 us -> 19.1 us
  blocking collectives: 82.9 us -> 0 us
    dot_general x60 -> x6, matrix products: 661 us -> 91 us  [dot(): return lax.dot_general(first, second, numbers, preferred_element_type=WIDE)]
    pallas_call x0 -> x6, Pallas kernels: none -> 375 us  [the longest x1 130 us: middle(): pl.pallas_call(functools.partial(middle_kernel, places), grid=(groups //...]
    unnamed x12 -> x9, waiting for transfers between devices: 431 us -> 109 us
    ppermute x0 -> x4, waiting for transfers between devices: none -> 224 us  [swap_axis(): lax.ppermute(values, axis, [(index, size - 1 - index) for index in range(...]
    reshape x25 -> x0, local copies, waits for them, and re-layouts: 159 us -> none  [the longest x8 84.7 us: to_places(): blocks.transpose(0, 2, 1, 3)]
    all_gather x8 -> x4, waiting for transfers between devices: 229 us -> 72.5 us  [clip_local(): collect = lambda item: lax.all_gather(item, axes, axis=0, tiled=True)]
    unnamed x270 -> x32, local copies, waits for them, and re-layouts: 97.6 us -> 13 us
    unnamed x2 -> x0, blocking collectives: 82.9 us -> none
  transfers between devices with their start and end apart: 11 -> 12, of which waited for: 7 -> 8; matrix products, arithmetic and copies ran while one was open for 34% -> 13% of each run, Pallas kernels for 0% -> 17%
where the time goes in v1:
time: 995 us; the launch traced here: 986 us
  waiting for transfers between devices  428 us (43%)
  Pallas kernels  375 us (38%)
  matrix products  91 us (9%)
  local copies, waits for them, and re-layouts  52.1 us (5%)
  other arithmetic  19.1 us (2%)
  between operations  14.9 us (1%)
    ppermute x4, waiting for transfers between devices, swap_axis(): lax.ppermute(values, axis, [(index, size - 1 - index) for index in range(...  224 us
    pallas_call x1, Pallas kernels, middle(): pl.pallas_call(functools.partial(middle_kernel, places), grid=(groups //...  130 us
    pallas_call x2, Pallas kernels, space_backward(): pl.pallas_call(functools.partial(space_backward_kernel, places), grid=(fr...  110 us
    unnamed x9, waiting for transfers between devices  109 us
    dot_general x6, matrix products, dot(): return lax.dot_general(first, second, numbers, preferred_element_type=WIDE)  91 us
    pallas_call x1, Pallas kernels, time_backward(): pl.pallas_call(time_backward_kernel, grid=(groups // 2,), in_specs=[by_ro...  76.8 us
    all_gather x4, waiting for transfers between devices, clip_local(): collect = lambda item: lax.all_gather(item, axes, axis=0, tiled=True)  72.5 us
    pallas_call x2, Pallas kernels, space_forward(): pl.pallas_call(functools.partial(space_forward_kernel, places), grid=(fra...  57.5 us
  transfers between devices with their start and end apart: 12, of which 8 were waited for; matrix products, arithmetic and copies ran while one was open for 13% of the time, Pallas kernels for 17%

profile of v1, /device:TPU:0, one launch (start us, length us, event | category | flops | bytes accessed | tf_op | source)
XLA Modules:
  0.0 986.2 jit_solution(5083137364485022915)
XLA Ops:
  7.2 1.6 pad_maximum_fusion.1
  8.9 0.7 pad_maximum_fusion.3
  9.7 1.6 fusion.23
  11.4 0.7 all-gather.9.cloned.1.call-update
  12.1 0.5 all-gather.11.cloned.1.call-update
  12.7 2.9 dynamic-slice_bitcast_fusion.1
  15.6 3.0 collective-permute-start
  18.6 0.3 dynamic-slice_bitcast_fusion
  18.9 0.8 collective-permute-start.1
  19.7 1.9 copy.92
  21.6 1.9 copy.91
  23.5 61.9 %collective-permute-done = bf16[8,196,768]{2,0,1:T(8,128)(2,1)S(1)} collective-permute-done((bf16[8,196,768]{2,0,1:T(8,128)(2,1)S(1)}, bf16[8,196,768]{2,0,1:T(8,128)(2,1)S(1)}, u32[]{:S(2)}, u32[]{:S(2)}) %collective-permute-start) | collective-permute-done | bytes 2408480 | tf_op jit(solution)/shard_map/ppermute | solution.py:887
  85.4 1.9 copy.64.x_ref
  87.3 56.6 %collective-permute-done.1 = bf16[8,196,768]{2,0,1:T(8,128)(2,1)S(1)} collective-permute-done((bf16[8,196,768]{2,0,1:T(8,128)(2,1)S(1)}, bf16[8,196,768]{2,0,1:T(8,128)(2,1)S(1)}, u32[]{:S(2)}, u32[]{:S(2)}) %collective-permute-start.1) | collective-permute-done | bytes 2408480 | tf_op jit(solution)/shard_map/ppermute | solution.py:887
  143.9 1.9 copy.67.gr_ref
  145.8 2.4 slice.67.tout_ref
  148.2 4.1 slice.66.tproj_ref
  152.2 8.0 all-gather.5.cloned.1.call-done
  160.3 1.0 convert_bitcast_fusion
  161.5 0.7 copy.69.fgain_ref
  162.2 0.7 copy.63.gain_ref.gain_row_ref
  163.0 0.7 copy.68.tgain_ref
  163.7 2.4 slice.63.out_ref
  166.1 4.0 slice.62.proj_ref
  170.2 28.8 %space_forward.2 = (bf16[8,208,768]{2,1,0:T(8,128)(2,1)}, bf16[8,208,2304]{2,1,0:T(8,128)(2,1)}, bf16[8,208,768]{2,1,0:T(8,128)(2,1)}, f32[26,8,8,768]{3,2,1,0:T(8,128)}) custom-call(bf16[8,196,768]{2,1,0:T(8,128)(2,1)} %bitcast.42, f32[1,768]{1,0:T(1,128)} %copy.63.gain_ref.gain_row_ref, bf16[768,2304]{1,0:T(8,128)(2,1)} %slice.62.proj_ref, ...), custom_call_target="tpu_custom_call" | custom-call | flops 9978249216 | bytes 25018368 | tf_op jit(solution)/shard_map/space_forward/pallas_call | solution.py:395
  199.0 28.7 %space_forward.3 = (bf16[8,208,768]{2,1,0:T(8,128)(2,1)}, bf16[8,208,2304]{2,1,0:T(8,128)(2,1)}, bf16[8,208,768]{2,1,0:T(8,128)(2,1)}, f32[26,8,8,768]{3,2,1,0:T(8,128)}) custom-call(bf16[8,196,768]{2,1,0:T(8,128)(2,1)} %copy.64.x_ref, f32[1,768]{1,0:T(1,128)} %copy.63.gain_ref.gain_row_ref, bf16[768,2304]{1,0:T(8,128)(2,1)} %slice.62.proj_ref, ...), custom_call_target="tpu_custom_call" | custom-call | flops 9978249216 | bytes 25018368 | tf_op jit(solution)/shard_map/space_forward/pallas_call | solution.py:395
  227.7 64.5 %all-gather.11.cloned.1.call-done.down_ref = bf16[3072,768]{1,0:T(8,128)(2,1)} async-done(((bf16[96,768]{1,0:T(8,128)(2,1)}), bf16[3072,768]{1,0:T(8,128)(2,1)}) %all-gather.11.cloned.1.call-update) | async-done | bytes 4718608 | tf_op jit(solution)/shard_map/all_gather | solution.py:916
  292.2 130.4 %middle.1 = (bf16[3328,2304]{1,0:T(8,128)(2,1)}, bf16[3328,768]{1,0:T(8,128)(2,1)}, bf16[3328,768]{1,0:T(8,128)(2,1)}, bf16[3328,768]{1,0:T(8,128)(2,1)}, bf16[3...) custom-call(f32[26,8,8,768]{3,2,1,0:T(8,128)} %get-tuple-element.43., ...), custom_call_target="tpu_custom_call" | custom-call | flops 81134616576 | bytes 106782720 | tf_op jit(solution)/shard_map/middle/pallas_call | solution.py:438
  422.6 76.8 %time_backward.1 = (bf16[3328,2304]{1,0:T(8,128)(2,1)}, bf16[3328,768]{1,0:T(8,128)(2,1)}, f32[8,208,768]{2,1,0:T(8,128)}, f32[8,208,768]{2,1,0:T(8,128)}, f32[8,768]{1,0:T(8,128)}) custom-call(bf16[3328,2304]{1,0:T(8,128)(2,1)} %get-tuple-element.47.qkv_ref, f32[3328,768]{1,0:T(8,128)} %get-tuple-element.48.gt_ref, ...), custom_call_target="tpu_custom_call" | custom-call | flops 22246588416 | bytes 66478080 | tf_op jit(solution)/shard_map/time_backward/pallas_call | solution.py:480
  499.4 8.3 convolution_convert_fusion.3
  507.8 1.4 copy-done.7
  509.2 14.1 %convolution_convert_fusion.2 = bf16[768,2304]{1,0:T(8,128)(2,1)S(1)} fusion(bf16[3328,768]{1,0:T(8,128)(2,1)S(1)} %copy-done.7, bf16[3328,2304]{1,0:T(8,128)(2,1)S(1)} %copy-done.6), kind=kOutput, calls=%fused_computation.20 | convolution fusion | flops 11779375104 | bytes 23986176 | tf_op jit(solution)/shard_map/dot_general | solution.py:30
  523.3 2.8 pad_maximum_fusion
  526.1 22.3 %convolution_convert_fusion.1 = bf16[768,3072]{1,0:T(8,128)(2,1)} fusion(bf16[3328,768]{1,0:T(8,128)(2,1)} %get-tuple-element.71, bf16[3328,3072]{1,0:T(8,128)(2,1)} %get-tuple-element.72), kind=kOutput, calls=%fused_computation.19 | convolution fusion | flops 15705833472 | bytes 30277632 | tf_op jit(solution)/shard_map/dot_general | solution.py:30
  548.5 22.9 %convolution_convert_fusion = bf16[3072,768]{1,0:T(8,128)(2,1)} fusion(bf16[3328,3072]{1,0:T(8,128)(2,1)} %get-tuple-element.73, bf16[3328,768]{1,0:T(8,128)(2,1)} %get-tuple-element.74), kind=kOutput, calls=%fused_computation.18 | convolution fusion | flops 15705833472 | bytes 30277632 | tf_op jit(solution)/shard_map/dot_general | solution.py:30
  571.5 55.1 %space_backward.2 = (bf16[8,208,2304]{2,1,0:T(8,128)(2,1)}, bf16[8,208,768]{2,1,0:T(8,128)(2,1)}, f32[8,196,768]{2,1,0:T(8,128)}, f32[8,768]{1,0:T(8,128)}) custom-call(bf16[8,196,768]{2,1,0:T(8,128)(2,1)} %bitcast.43, f32[8,208,768]{2,1,0:T(8,128)} %get-tuple-element.49.gs_ref, bf16[8,208,2304]{2,1,0:T(8,128)(2,1)} %get-tuple-element.50.qkv_ref, ...), custom_call_target="tpu_custom_call" | custom-call | flops 13168017408 | bytes 30253056 | tf_op jit(solution)/shard_map/space_backward/pallas_call | solution.py:511
  626.6 54.6 %space_backward.3 = (bf16[8,208,2304]{2,1,0:T(8,128)(2,1)}, bf16[8,208,768]{2,1,0:T(8,128)(2,1)}, bf16[8,196,768]{2,1,0:T(8,128)(2,1)}, f32[8,768]{1,0:T(8,128)}) custom-call(bf16[8,196,768]{2,1,0:T(8,128)(2,1)} %copy.64.x_ref, f32[8,208,768]{2,1,0:T(8,128)} %get-tuple-element.52.gs_ref, bf16[8,208,2304]{2,1,0:T(8,128)(2,1)} %get-tuple-element.53.qkv_ref, ...), custom_call_target="tpu_custom_call" | custom-call | flops 13168017408 | bytes 27844608 | tf_op jit(solution)/shard_map/space_backward/pallas_call | solution.py:511
  681.3 0.8 add_reduce_fusion
  682.3 7.7 bitcast_convert_fusion.2
  690.0 15.8 %bitcast_convert_fusion = bf16[768,2304]{1,0:T(8,128)(2,1)S(1)} fusion(bf16[8,208,2304]{2,1,0:T(8,128)(2,1)} %get-tuple-element.58, bf16[8,208,2304]{2,1,0:T(8,128)(2,1)S(1)} %copy-done.8, bf16[8,208,768]{2,1,0:T(8,128)(2,1)} %get-tuple-element.56, bf16[8,208,768]{2,1,0:T(8,128)(2,1)S(1)} %copy-done.10), kind=kOutput, calls=%fused_computation.7 | convolution fusion | flops 11789598720 | bytes 23986176 | tf_op jit(solution)/shard_map/dot_general | solution.py:30
  705.8 2.6 fusion.17
  708.5 1.7 copy-done.1
  710.1 1.9 copy.70
  712.0 1.4 collective-permute-start.2
  713.5 1.9 copy.76
  715.3 0.6 collective-permute-start.3
  715.9 52.6 %collective-permute-done.2 = bf16[8,196,768]{2,0,1:T(8,128)(2,1)} collective-permute-done((bf16[8,196,768]{2,0,1:T(8,128)(2,1)}, bf16[8,196,768]{2,0,1:T(8,128)(2,1)}, u32[]{:S(2)}, u32[]{:S(2)}) %collective-permute-start.2) | collective-permute-done | bytes 2408480 | tf_op jit(solution)/shard_map/ppermute | solution.py:887
  768.5 2.2 copy.90
  770.7 0.9 maximum_select_fusion.1
  771.7 3.2 copy.81
  774.9 53.3 %collective-permute-done.3 = bf16[8,196,768]{2,0,1:T(8,128)(2,1)} collective-permute-done((bf16[8,196,768]{2,0,1:T(8,128)(2,1)}, bf16[8,196,768]{2,0,1:T(8,128)(2,1)}, u32[]{:S(2)}, u32[]{:S(2)}) %collective-permute-start.3) | collective-permute-done | bytes 2408480 | tf_op jit(solution)/shard_map/ppermute | solution.py:887
  828.2 2.1 bitcast_convert_fusion.1
  830.4 0.8 maximum_select_fusion
  831.2 6.7 copy.82
  837.8 1.4 slice.74
  839.2 1.6 slice.73
  840.8 1.6 convert_element_type.44
  842.5 22.2 %reduce-scatter.11.cloned.1.call-done = bf16[96,768]{1,0:T(8,128)(2,1)} async-done(((bf16[3072,768]{1,0:T(8,128)(2,1)}), bf16[96,768]{1,0:T(8,128)(2,1)}) %reduce-scatter.11.cloned.1.call-update) | async-done | bytes 147472 | tf_op jit(solution)/shard_map/reduce_scatter | solution.py:941
  864.6 1.6 convert_element_type.46
  866.3 108.0 %reduce-scatter.13.cloned.1.call-done = bf16[24,3200]{1,0:T(8,128)(2,1)} async-done(((bf16[768,3200]{1,0:T(8,128)(2,1)}), bf16[24,3200]{1,0:T(8,128)(2,1)}) %reduce-scatter.13.cloned.1.call-update) | async-done | bytes 153616
  974.3 0.9 convert_element_type.39
  975.2 0.7 slice_reduce_fusion
  975.9 1.4 slice.72
  977.3 1.6 slice.71
  (57 shorter events, 1.1 us)
Async XLA Ops:
  7.2 138.6 %all-gather.7.cloned.1.call-start = ((), (), s32[]{:S(2)}) async-start(), calls=%async_computation.5 | async-start | bytes 4866048 | tf_op jit(solution)/shard_map/all_gather | solution.py:916
  8.8 151.4 %all-gather.5.cloned.1.call-start = ((), (), s32[]{:S(2)}) async-start(), calls=%async_computation.4 | async-start | bytes 5068800 | tf_op jit(solution)/shard_map/all_gather | solution.py:916
  11.3 216.4 %all-gather.9.cloned.1.call-start = ((), (), s32[]{:S(2)}) async-start(), calls=%async_computation.6 | async-start | bytes 4866048 | tf_op jit(solution)/shard_map/all_gather | solution.py:916
  12.0 6.5 slice-start.2
  12.1 280.1 %all-gather.11.cloned.1.call-start = ((), (), s32[]{:S(2)}) async-start(), calls=%async_computation.7 | async-start | bytes 4866048 | tf_op jit(solution)/shard_map/all_gather | solution.py:916
  12.6 825.2 %reduce-scatter.7.cloned.1.call-start = ((), (), s32[]{:S(2)}) async-start(), calls=%async_computation.8 | async-start | bytes 4866048 | tf_op jit(solution)/shard_map/reduce_scatter | solution.py:941
  12.7 5.9 slice-start.3
  15.6 69.8 %collective-permute-start = (bf16[8,196,768]{2,0,1:T(8,128)(2,1)S(1)}, bf16[8,196,768]{2,0,1:T(8,128)(2,1)S(1)}, u32[]{:S(2)}, u32[]{:S(2)}) collective-permute-start(bf16[8,196,768]{2,0,1:T(8,128)(2,1)S(1)} %get-tuple-element.113), channel_id=1, source_target_pairs={{0,1},{1,0},{2,3},{3,2},{4,5},{5,4},{6,7},{7,6},{8,9},{9,8},{10,11... | collective-permute-start | bytes 7225352 | tf_op jit(solution)/shard_map/ppermute | solution.py:887
  18.9 125.0 %collective-permute-start.1 = (bf16[8,196,768]{2,0,1:T(8,128)(2,1)S(1)}, bf16[8,196,768]{2,0,1:T(8,128)(2,1)S(1)}, u32[]{:S(2)}, u32[]{:S(2)}) collective-permute-start(bf16[8,196,768]{2,0,1:T(8,128)(2,1)S(1)} %get-tuple-element.111), channel_id=1, source_target_pairs={{0,1},{1,0},{2,3},{3,2},{4,5},{5,4},{6,7},{7,6},{8,9},{9,8},{10,11... | collective-permute-start | bytes 7225352 | tf_op jit(solution)/shard_map/ppermute | solution.py:887
  499.4 8.3 copy-start.6
  499.4 9.8 copy-start.7
  526.1 314.8 %reduce-scatter.9.cloned.1.call-start = ((), (), s32[]{:S(2)}) async-start(), calls=%async_computation.9 | async-start | bytes 4866048 | tf_op jit(solution)/shard_map/reduce_scatter | solution.py:941
  548.4 316.2 %reduce-scatter.11.cloned.1.call-start = ((), (), s32[]{:S(2)}) async-start(), calls=%async_computation.10 | async-start | bytes 4866048 | tf_op jit(solution)/shard_map/reduce_scatter | solution.py:941
  548.5 23.0 %copy-start.5 = (f32[8,768]{1,0:T(8,128)S(1)}, f32[8,768]{1,0:T(8,128)}, u32[]{:S(2)}) copy-start(f32[8,768]{1,0:T(8,128)} %get-tuple-element.66) | copy-start | bytes 73732
  571.4 402.9 %reduce-scatter.13.cloned.1.call-start = ((), (), s32[]{:S(2)}) async-start(), calls=%async_computation.11 | async-start | bytes 5068800
  626.6 54.6 %copy-start.3 = (f32[8,768]{1,0:T(8,128)S(1)}, f32[8,768]{1,0:T(8,128)}, u32[]{:S(2)}) copy-start(f32[8,768]{1,0:T(8,128)} %get-tuple-element.63) | copy-start | bytes 73732
  626.6 55.4 %copy-start.4 = (f32[8,768]{1,0:T(8,128)S(1)}, f32[8,768]{1,0:T(8,128)}, u32[]{:S(2)}) copy-start(f32[8,768]{1,0:T(8,128)} %get-tuple-element.65) | copy-start | bytes 73732
  626.6 55.7 %copy-start.9 = (bf16[8,208,768]{2,1,0:T(8,128)(2,1)S(1)}, bf16[8,208,768]{2,1,0:T(8,128)(2,1)}, u32[]{:S(2)}) copy-start(bf16[8,208,768]{2,1,0:T(8,128)(2,1)} %get-tuple-element.59) | copy-start | bytes 7667716
  682.3 7.7 copy-start.8
  682.3 7.7 copy-start.10
  708.4 1.7 copy-start.1
  708.5 5.0 copy-start.2
  712.0 58.7 %copy-start = (bf16[8,196,768]{2,1,0:T(8,128)(2,1)S(1)}, bf16[8,196,768]{2,1,0:T(8,128)(2,1)}, u32[]{:S(2)}) copy-start(bf16[8,196,768]{2,1,0:T(8,128)(2,1)} %get-tuple-element.45) | copy-start | bytes 7225348
  712.0 56.5 %collective-permute-start.2 = (bf16[8,196,768]{2,0,1:T(8,128)(2,1)}, bf16[8,196,768]{2,0,1:T(8,128)(2,1)}, u32[]{:S(2)}, u32[]{:S(2)}) collective-permute-start(bf16[8,196,768]{2,0,1:T(8,128)(2,1)} %copy.70), channel_id=1, source_target_pairs={{0,1},{1,0},{2,3},{3,2},{4,5},{5,4},{6,7},{7,6},{8,9},{9,8},{10,11... | collective-permute-start | bytes 7225352 | tf_op jit(solution)/shard_map/ppermute | solution.py:887
  715.3 112.9 %collective-permute-start.3 = (bf16[8,196,768]{2,0,1:T(8,128)(2,1)}, bf16[8,196,768]{2,0,1:T(8,128)(2,1)}, u32[]{:S(2)}, u32[]{:S(2)}) collective-permute-start(bf16[8,196,768]{2,0,1:T(8,128)(2,1)} %copy.76), channel_id=1, source_target_pairs={{0,1},{1,0},{2,3},{3,2},{4,5},{5,4},{6,7},{7,6},{8,9},{9,8},{10,11... | collective-permute-start | bytes 7225352 | tf_op jit(solution)/shard_map/ppermute | solution.py:887
  770.7 59.6 %slice-start = ((s8[4915200]{0:T(1024)(128)(4,1)}), s8[4194304]{0:T(1024)(128)(4,1)S(1)}, s32[]{:S(2)}) async-start(s8[4915200]{0:T(1024)(128)(4,1)} %bitcast.36), calls=%async_computation.12 | async-start | bytes 8388608
  771.7 58.7 %slice-start.1 = ((s8[4915200]{0:T(1024)(128)(4,1)}), s8[720896]{0:T(1024)(128)(4,1)S(1)}, s32[]{:S(2)}) async-start(s8[4915200]{0:T(1024)(128)(4,1)} %bitcast.36), calls=%async_computation.13 | async-start | bytes 1441792
Sparse Core Ops, SparseCore 0:
  11.5 77.8 all-gather.6
  93.0 67.2 all-gather.4
  163.2 63.6 all-gather.8
  229.7 62.4 all-gather.10
  526.2 105.7 reduce-scatter.6
  638.2 106.2 reduce-scatter.8
  750.0 114.5 reduce-scatter.10
  871.3 102.8 reduce-scatter.12

commit v2 on v1

--- a/solution.py
+++ b/solution.py
@@ -24,6 +24,7 @@
 GROUP = 8
 STEP = 2 * GROUP
 LIMIT = 60 << 20
+SHRINK = 6
 
 
 def dot(first, second, numbers=NN):
@@ -84,13 +85,15 @@
 
 
 def space_forward_kernel(
-    places, x_ref, gain_ref, proj_ref, out_ref, in_ref, qkv_ref, o_ref, after_ref, pad_ref
+    places, x_ref, gain_ref, qk_ref, v_ref, out_ref, in_ref, qkv_ref, o_ref, after_ref, pad_ref
 ):
     frames, padded, width = pad_ref.shape
     values = load_padded(x_ref, pad_ref)
     normed = norm_rows(values, gain_ref[...])[0].astype(LOW)
     in_ref[...] = normed.reshape(frames, padded, width)
-    qkv_ref[...] = dot(normed, proj_ref[...]).astype(LOW).reshape(frames, padded, 3 * width)
+    for start, ref in ((0, qk_ref), (2 * width, v_ref)):
+        part = dot(normed, ref[...]).astype(LOW)
+        qkv_ref[:, :, start : start + part.shape[1]] = part.reshape(frames, padded, -1)
     real = lax.broadcasted_iota(jnp.int32, (padded, padded), 1) < places
 
     def one_frame(frame, carry):
@@ -118,6 +121,7 @@
 
 def middle_kernel(
     places,
+    place_ref,
     ao_ref,
     ar_ref,
     go_ref,
@@ -183,27 +187,27 @@
     grad_low = gradient.astype(LOW)
     gb_ref[...] = grad_low
     hidden_width = up_ref.shape[1]
-    piece = 512
+    piece = width
     root = math.sqrt(2.0 / math.pi)
     for start in range(0, hidden_width, piece):
         cut = slice(start, start + piece)
         hidden = dot(in_feed, up_ref[:, cut])
-        back = dot(grad_low, down_ref[cut, :], NT)
+        back = dot(grad_low, down_ref[:, cut], NT)
         square = hidden * hidden
         slope = jnp.tanh(hidden * (root + (root * 0.044715) * square))
         plus = 0.5 * slope + 0.5
         act_ref[:, cut] = (hidden * plus).astype(LOW)
         inner = hidden * (0.5 * root + (1.5 * root * 0.044715) * square)
         gh_ref[:, cut] = (back * (plus + inner * (1.0 - slope * slope))).astype(LOW)
-    mixed = values + dot(act_ref[...], down_ref[...])
-    for frame in range(frames):
-        low = mixed[frame * GROUP : (frame + 1) * GROUP]
-        high = mixed[block + frame * GROUP : block + (frame + 1) * GROUP]
-        tile = jnp.concatenate([low, high], axis=0).astype(LOW)
-        if frame < half:
-            mo_ref[frame] = tile
-        else:
-            mr_ref[frame - half] = tile
+    mixed = values
+    for start in range(0, hidden_width, piece):
+        cut = slice(start, start + piece)
+        mixed = mixed + dot(act_ref[:, cut], down_ref[:, cut])
+    mixed = mixed.reshape(2, frames, GROUP, width)
+    for group in range(2):
+        cut = slice(group * GROUP, (group + 1) * GROUP)
+        mo_ref[0, cut] = jnp.swapaxes(mixed[group, :half], 0, 1).astype(LOW)
+        mr_ref[cut] = jnp.swapaxes(mixed[group, half:], 0, 1).astype(LOW)
     back = dot(gh_ref[...], up_ref[...], NT)
     gt_ref[...] = gradient + norm_back(back, normed, inverse, feed_gain)
 
@@ -288,20 +292,24 @@
 
 def space_backward_kernel(
     places,
+    place_ref,
     x_ref,
     gs_ref,
     qkv_ref,
     gain_row_ref,
     out_ref,
-    proj_ref,
+    qk_ref,
+    v_ref,
     gq_ref,
     sb_ref,
     gx_ref,
     gain_ref,
     pad_ref,
     d_ref,
+    order_ref,
 ):
     frames, padded, width = pad_ref.shape
+    stride = order_ref.shape[1] // padded
     values = load_padded(x_ref, pad_ref)
     grad_space = gs_ref[...].reshape(frames * padded, width)
     sb = grad_space.astype(LOW)
@@ -344,11 +352,24 @@
     lax.fori_loop(0, frames, one_frame, 0)
     gain = gain_row_ref[...]
     _, normed, inverse = norm_rows(values, gain)
-    back = dot(gq_ref[...].reshape(frames * padded, 3 * width), proj_ref[...], NT)
+    back = dot(gq_ref[:, :, : 2 * width].reshape(frames * padded, 2 * width), qk_ref[...], NT)
+    back = back + dot(gq_ref[:, :, 2 * width :].reshape(frames * padded, width), v_ref[...], NT)
     result = grad_space + norm_back(back, normed, inverse, gain)
     result = result.reshape(frames, padded, width)
     for frame in range(frames):
-        gx_ref[frame] = result[frame, 0:places].astype(gx_ref.dtype)
+        rows = pl.ds(pl.program_id(0) * frames + frame, padded, stride=stride)
+        for lane in range(width // LANES):
+            order_ref[lane, rows, :] = result[frame, :, lane * LANES : (lane + 1) * LANES]
+
+    @pl.when(pl.program_id(0) == pl.num_programs(0) - 1)
+    def _():
+        for lane in range(width // LANES):
+            tile = order_ref[lane, 0 : places * stride].astype(gx_ref.dtype)
+            tile = tile.reshape(places, stride, LANES)
+            if len(gx_ref.shape) == 4:
+                gx_ref[0, :, :, lane * LANES : (lane + 1) * LANES] = tile
+            else:
+                gx_ref[:, :, lane * LANES : (lane + 1) * LANES] = tile
 
     @pl.when(pl.program_id(0) == 0)
     def _():
@@ -363,13 +384,23 @@
     )
 
 
+def columns(array, width, index):
+    return pl.BlockSpec(
+        (array.shape[0], width),
+        lambda *_: (0, index),
+        pipeline_mode=pl.Buffered(buffer_count=1),
+    )
+
+
 def params():
     return pltpu.CompilerParams(vmem_limit_bytes=LIMIT)
 
 
 def cost(flops, *arrays):
     size = sum(math.prod(item.shape) * jnp.dtype(item.dtype).itemsize for item in arrays)
-    return pl.CostEstimate(flops=int(flops), bytes_accessed=int(size), transcendentals=0)
+    return pl.CostEstimate(
+        flops=int(flops) // SHRINK, bytes_accessed=int(size) // SHRINK, transcendentals=0
+    )
 
 
 def padded_places(places):
@@ -377,10 +408,10 @@
 
 
 def by_frame(count, *tail):
-    return pl.BlockSpec((count,) + tail, lambda step: (step,) + (0,) * len(tail))
-
-
-def space_forward(x, gain, proj, out):
+    return pl.BlockSpec((count,) + tail, lambda step, *_: (step,) + (0,) * len(tail))
+
+
+def space_forward(x, gain, first, second):
     frames, places, width = x.shape
     padded = padded_places(places)
     groups = padded // GROUP
@@ -395,7 +426,13 @@
     return pl.pallas_call(
         functools.partial(space_forward_kernel, places),
         grid=(frames // 2,),
-        in_specs=[by_frame(2, places, width), whole(gain.shape), whole(proj.shape), whole(out.shape)],
+        in_specs=[
+            by_frame(2, places, width),
+            whole(gain.shape),
+            whole(first.shape),
+            columns(second, width, 0),
+            columns(second, width, 1),
+        ],
         out_specs=[
             by_frame(2, padded, width),
             by_frame(2, padded, 3 * width),
@@ -405,18 +442,18 @@
         out_shape=outs,
         scratch_shapes=[pltpu.VMEM((2, padded, width), WIDE)],
         compiler_params=params(),
-        cost_estimate=cost(flops, x, proj, out, *outs),
+        cost_estimate=cost(flops, x, first, second, *outs),
         name="space_forward",
-    )(x, gain, proj, out)
-
-
-def middle(after_own, after_rest, g_own, g_rest, tgain, fgain, tproj, tout, up, down):
+    )(x, gain, first, second, second)
+
+
+def middle(place, after_own, after_rest, g_own, g_rest, tgain, fgain, packed):
     groups, half, _, width = after_own.shape
     places = g_own.shape[1]
     frames = 2 * half
     rows = groups * frames * GROUP
     block = 2 * frames * GROUP
-    hidden = up.shape[1]
+    hidden = (packed.shape[1] - 4 * width) // 2
     padded = groups * GROUP
     outs = (
         jax.ShapeDtypeStruct((rows, 3 * width), LOW),
@@ -426,41 +463,51 @@
         jax.ShapeDtypeStruct((rows, hidden), LOW),
         jax.ShapeDtypeStruct((rows, hidden), LOW),
         jax.ShapeDtypeStruct((rows, width), LOW),
-        jax.ShapeDtypeStruct((half, places, width), LOW),
-        jax.ShapeDtypeStruct((half, places, width), LOW),
+        jax.ShapeDtypeStruct((2, places, half, width), LOW),
+        jax.ShapeDtypeStruct((places, half, width), LOW),
         jax.ShapeDtypeStruct((rows, width), WIDE),
         jax.ShapeDtypeStruct((8, width), WIDE),
     )
-    by_row = lambda size: pl.BlockSpec((block, size), lambda step: (step, 0))
-    by_group = pl.BlockSpec((2, half, GROUP, width), lambda step: (step, 0, 0, 0))
-    by_place = pl.BlockSpec((half, STEP, width), lambda step: (0, step, 0))
+    by_row = lambda size: pl.BlockSpec((block, size), lambda step, place: (step, 0))
+    by_group = pl.BlockSpec((2, half, GROUP, width), lambda step, place: (step, 0, 0, 0))
+    by_place = pl.BlockSpec((half, STEP, width), lambda step, place: (0, step, 0))
     flops = 2 * rows * width * (4 * width + 4 * hidden) + 8 * rows * frames * GROUP * width
     return pl.pallas_call(
         functools.partial(middle_kernel, places),
-        grid=(groups // 2,),
-        in_specs=[by_group, by_group, by_place, by_place]
-        + [whole(item.shape) for item in (tgain, fgain, tproj, tout, up, down)],
-        out_specs=[
-            by_row(3 * width),
-            by_row(width),
-            by_row(width),
-            by_row(width),
-            by_row(hidden),
-            by_row(hidden),
-            by_row(width),
-            by_place,
-            by_place,
-            by_row(width),
-            pl.BlockSpec((8, width), lambda step: (0, 0)),
-        ],
+        grid_spec=pltpu.PrefetchScalarGridSpec(
+            num_scalar_prefetch=1,
+            grid=(groups // 2,),
+            in_specs=[by_group, by_group, by_place, by_place]
+            + [
+                whole(tgain.shape),
+                whole(fgain.shape),
+                columns(packed, 3 * width, 0),
+                columns(packed, width, 3),
+                columns(packed, hidden, 1),
+                columns(packed, hidden, 2),
+            ],
+            out_specs=[
+                by_row(3 * width),
+                by_row(width),
+                by_row(width),
+                by_row(width),
+                by_row(hidden),
+                by_row(hidden),
+                by_row(width),
+                pl.BlockSpec((1, STEP, half, width), lambda step, place: (place[0], step, 0, 0)),
+                pl.BlockSpec((STEP, half, width), lambda step, place: (step, 0, 0)),
+                by_row(width),
+                pl.BlockSpec((8, width), lambda step, place: (0, 0)),
+            ],
+        ),
         out_shape=outs,
         compiler_params=params(),
         cost_estimate=cost(flops, after_own, after_rest, g_own, g_rest, *outs),
         name="middle",
-    )(after_own, after_rest, g_own, g_rest, tgain, fgain, tproj, tout, up, down)
-
-
-def time_backward(qkv, g_time, after_own, after_rest, tgain, tout, tproj):
+    )(place, after_own, after_rest, g_own, g_rest, tgain, fgain, packed, packed, packed, packed)
+
+
+def time_backward(qkv, g_time, after_own, after_rest, tgain, packed):
     groups, half, _, width = after_own.shape
     frames = 2 * half
     rows = groups * frames * GROUP
@@ -481,7 +528,7 @@
         time_backward_kernel,
         grid=(groups // 2,),
         in_specs=[by_row(3 * width), by_row(width), by_group, by_group]
-        + [whole(item.shape) for item in (tgain, tout, tproj)],
+        + [whole(tgain.shape), columns(packed, width, 3), columns(packed, 3 * width, 0)],
         out_specs=[
             by_row(3 * width),
             by_row(width),
@@ -494,53 +541,147 @@
         compiler_params=params(),
         cost_estimate=cost(flops, qkv, g_time, after_own, after_rest, *outs),
         name="time_backward",
-    )(qkv, g_time, after_own, after_rest, tgain, tout, tproj)
-
-
-def space_backward(x, g_space, qkv, gain, out, proj, kind):
+    )(qkv, g_time, after_own, after_rest, tgain, packed, packed)
+
+
+def space_backward(place, x, g_space, qkv, gain, first, second, kind):
     frames, places, width = x.shape
     padded = padded_places(places)
     rows = frames * padded
+    own = kind == WIDE
+    shape = (2, places, frames, width) if own else (places, frames, width)
     outs = (
         jax.ShapeDtypeStruct((frames, padded, 3 * width), LOW),
         jax.ShapeDtypeStruct((frames, padded, width), LOW),
-        jax.ShapeDtypeStruct((frames, places, width), kind),
+        jax.ShapeDtypeStruct(shape, kind),
         jax.ShapeDtypeStruct((8, width), WIDE),
     )
     flops = 2 * rows * width * 4 * width + 20 * rows * padded * width
     return pl.pallas_call(
         functools.partial(space_backward_kernel, places),
-        grid=(frames // 2,),
-        in_specs=[
-            by_frame(2, places, width),
-            by_frame(2, padded, width),
-            by_frame(2, padded, 3 * width),
-            whole(gain.shape),
-            whole(out.shape),
-            whole(proj.shape),
-        ],
-        out_specs=[
-            by_frame(2, padded, 3 * width),
-            by_frame(2, padded, width),
-            by_frame(2, places, width),
-            pl.BlockSpec((8, width), lambda step: (0, 0)),
-        ],
+        grid_spec=pltpu.PrefetchScalarGridSpec(
+            num_scalar_prefetch=1,
+            grid=(frames // 2,),
+            in_specs=[
+                by_frame(2, places, width),
+                by_frame(2, padded, width),
+                by_frame(2, padded, 3 * width),
+                whole(gain.shape),
+                columns(second, width, 1),
+                whole(first.shape),
+                columns(second, width, 0),
+            ],
+            out_specs=[
+                by_frame(2, padded, 3 * width),
+                by_frame(2, padded, width),
+                pl.BlockSpec((1,) + shape[1:], lambda step, place: (place[0], 0, 0, 0))
+                if own
+                else pl.BlockSpec(shape, lambda step, place: (0, 0, 0)),
+                pl.BlockSpec((8, width), lambda step, place: (0, 0)),
+            ],
+            scratch_shapes=[
+                pltpu.VMEM((2, padded, width), WIDE),
+                pltpu.VMEM((2, padded, width), LOW),
+                pltpu.VMEM((width // LANES, padded * frames, LANES), WIDE),
+            ],
+        ),
         out_shape=outs,
-        scratch_shapes=[
-            pltpu.VMEM((2, padded, width), WIDE),
-            pltpu.VMEM((2, padded, width), LOW),
-        ],
         compiler_params=params(),
         cost_estimate=cost(flops, x, g_space, qkv, *outs),
         name="space_backward",
-    )(x, g_space, qkv, gain, out, proj)
-
-
-def weight_gradient(values, gradient):
-    rows = math.prod(values.shape[:-1])
-    return dot(
-        values.reshape(rows, values.shape[-1]), gradient.reshape(rows, gradient.shape[-1]), TN
-    ).astype(LOW)
+    )(place, x, g_space, qkv, gain, second, first, second)
+
+
+def gradient_kernel(parts, tiles, core_ref, *refs):
+    step = pl.program_id(0)
+
+    def emit(pairs):
+        total = dot(pairs[0][0][...], pairs[0][1][...], TN)
+        for first, second in pairs[1:]:
+            total = total + dot(first[...], second[...], TN)
+        if core_ref is None:
+            refs[-1][...] = total.astype(LOW)
+            return
+        keep_ref, send_ref = refs[-2:]
+        total = total.reshape(keep_ref.shape[0], 2, keep_ref.shape[1], keep_ref.shape[2])
+        total = total.astype(LOW)
+        keep = core_ref[0] == 0
+        keep_ref[...] = jnp.where(keep, total[:, 0], total[:, 1])
+        send_ref[...] = jnp.where(keep, total[:, 1], total[:, 0])
+
+    start = 0
+    for (first, last), count in zip(tiles, parts):
+        group = refs[start : start + 2 * count]
+        start += 2 * count
+        pairs = [(group[2 * index], group[2 * index + 1]) for index in range(count)]
+        pl.when((step >= first) & (step < last))(functools.partial(emit, pairs))
+
+
+def plan_gradient(groups):
+    width = groups[0][0][0][0].shape[1] if groups[0][3] == 1 else groups[0][0][0][1].shape[1]
+    count = groups[-1][2]
+    specs, arrays, parts, tiles = [], [], [], []
+    flops = 0
+    for pairs, first, last, side, offset in groups:
+        parts.append(len(pairs))
+        tiles.append((first, last))
+        for pair_arrays in pairs:
+            for index, item in enumerate(pair_arrays):
+                rows = item.shape[0]
+                if index == side and last - first > 1:
+                    spec = pl.BlockSpec(
+                        (rows, width),
+                        lambda step, *_, first=first, last=last, offset=offset: (
+                            0,
+                            jnp.clip(step - first, 0, last - first - 1) + offset,
+                        ),
+                    )
+                else:
+                    fixed = offset if index == side else 0
+                    spec = pl.BlockSpec(
+                        (rows, width),
+                        lambda step, *_, fixed=fixed: (0, fixed),
+                        pipeline_mode=pl.Buffered(buffer_count=1),
+                    )
+                specs.append(spec)
+                arrays.append(item)
+            flops += 2 * rows * width * width * (last - first)
+    return width, count, specs, arrays, parts, tiles, flops
+
+
+def weight_gradient(*groups):
+    width, count, specs, arrays, parts, tiles, flops = plan_gradient(groups)
+    out = jax.ShapeDtypeStruct((width, count * width), LOW)
+    return pl.pallas_call(
+        functools.partial(gradient_kernel, parts, tiles, None),
+        grid=(count,),
+        in_specs=specs,
+        out_specs=pl.BlockSpec((width, width), lambda step: (0, step)),
+        out_shape=out,
+        compiler_params=params(),
+        cost_estimate=cost(flops, *arrays, out),
+        name="weight_gradient",
+    )(*arrays)
+
+
+def split_gradient(core, owners, *groups):
+    width, count, specs, arrays, parts, tiles, flops = plan_gradient(groups)
+    blocks, rows = owners // 4, 2 * (width // owners)
+    out = jax.ShapeDtypeStruct((blocks, rows, count * width), LOW)
+    out_spec = pl.BlockSpec((blocks, rows, width), lambda step, core: (0, 0, step))
+    return pl.pallas_call(
+        functools.partial(gradient_kernel, parts, tiles),
+        grid_spec=pltpu.PrefetchScalarGridSpec(
+            num_scalar_prefetch=1,
+            grid=(count,),
+            in_specs=specs,
+            out_specs=[out_spec, out_spec],
+        ),
+        out_shape=[out, out],
+        compiler_params=params(),
+        cost_estimate=cost(flops, *arrays, out, out),
+        name="split_gradient",
+    )(core, *arrays)
 
 
 MICRO = 2
@@ -887,14 +1028,88 @@
     return lax.ppermute(values, axis, [(index, size - 1 - index) for index in range(size)])
 
 
-def own_first(mine, other, place):
+def flip(values, mask):
+    size = lax.axis_size("clip")
+    return lax.ppermute(values, "clip", [(index, index ^ mask) for index in range(size)])
+
+
+def tie(*items):
+    return lax.optimization_barrier(items)
+
+
+def bit_of(mask):
+    return (lax.axis_index("clip") // mask) % 2
+
+
+def in_order(bit, mine, other, axis):
     return jnp.where(
-        place == 0, jnp.stack([mine, other], axis=0), jnp.stack([other, mine], axis=0)
-    )
-
-
-def gain_row(values):
-    return values.astype(WIDE).reshape(1, -1)
+        bit == 0, jnp.stack([mine, other], axis=axis), jnp.stack([other, mine], axis=axis)
+    )
+
+
+def pick(values, index, axis):
+    return lax.dynamic_index_in_dim(values, index, axis, keepdims=False)
+
+
+def added(*items):
+    return sum(item.astype(WIDE) for item in items)
+
+
+def collect_start(shard):
+    return in_order(lax.axis_index("frame"), shard, swap_axis(shard, "frame"), 0)
+
+
+def collect_lines(item):
+    line = lax.axis_index("clip") // 4
+    parts = [item] + [flip(item, 4 * step) for step in range(1, 4)]
+    odd, far = line % 2, line // 2
+    parts = [jnp.where(odd == 0, parts[index], parts[index ^ 1]) for index in range(4)]
+    parts = [jnp.where(far == 0, parts[index], parts[index ^ 2]) for index in range(4)]
+    return jnp.stack(parts, axis=0)
+
+
+def collect_half(item, mask, axis):
+    return in_order(bit_of(mask), item, flip(item, mask), axis)
+
+
+def merged(item):
+    return item.reshape(-1, item.shape[-1])
+
+
+def scatter_core(keep, send):
+    return keep, flip(send, 1)
+
+
+def scatter_columns(keep, other):
+    shape = (4, 2) + keep.shape[1:]
+    keep, other = keep.reshape(shape), other.reshape(shape)
+    bit = bit_of(2)
+    send = added(pick(keep, 1 - bit, 1), pick(other, 1 - bit, 1)).astype(LOW)
+    return added(pick(keep, bit, 1), pick(other, bit, 1)).astype(LOW), flip(send, 2)
+
+
+def scatter_lines(keep, other):
+    line = lax.axis_index("clip") // 4
+    total = added(keep, other).astype(LOW)
+    parts = [flip(pick(total, line ^ step, 0), 4 * step) for step in range(1, 4)]
+    return (pick(total, line, 0), *parts)
+
+
+def scatter_frames(*parts):
+    total = added(*parts).astype(LOW)
+    total = total.reshape(2, total.shape[0] // 2, total.shape[1])
+    place = lax.axis_index("frame")
+    return pick(total, place, 0), swap_axis(pick(total, 1 - place, 0), "frame")
+
+
+def summed(values):
+    for mask in (1, 2, 4, 8):
+        values = values + flip(values, mask)
+    return values + swap_axis(values, "frame")
+
+
+def flat_rows(values):
+    return values.reshape(-1, values.shape[-1])
 
 
 def clip_local(
@@ -912,74 +1127,118 @@
 ):
     axes = ("clip", "frame")
     place = lax.axis_index("frame")
-    width = tokens.shape[-1]
-    collect = lambda item: lax.all_gather(item, axes, axis=0, tiled=True)
+    owners = lax.axis_size(axes)
+    me = lax.axis_index(axes)
+    share, width = space_out.shape
+    blocks = down_proj.shape[0] // share
+    core = bit_of(1).reshape(1)
+    spot = place.reshape(1)
 
     gains = jnp.stack([space_gain, time_gain, feed_gain], axis=1)
     gains = jnp.pad(gains, ((0, 0), (0, LANES - 3)))
-    space = collect(jnp.concatenate([space_proj, space_out, gains], axis=1))
-    time = collect(jnp.concatenate([time_proj, time_out], axis=1))
-    up = collect(up_proj)
-    down = collect(down_proj)
-    rest = swap_axis(lax.dynamic_index_in_dim(tokens, 1 - place, 0, keepdims=False), "frame")
-    g_rest = swap_axis(lax.dynamic_index_in_dim(cotangent, 1 - place, 0, keepdims=False), "frame")
-    own = lax.dynamic_index_in_dim(tokens, place, 0, keepdims=False)
-    g_own = lax.dynamic_index_in_dim(cotangent, place, 0, keepdims=False)
-
-    proj_width = 3 * width
-    table = space[:, 4 * width : 4 * width + 3].astype(WIDE).T
+    first = collect_start(space_proj[:, : 2 * width])
+    second = collect_start(
+        jnp.concatenate([space_proj[:, 2 * width :], space_out, gains], axis=1)
+    )
+    up_order = up_proj.reshape(share, owners, blocks, share).transpose(0, 2, 1, 3)
+    down_order = down_proj.reshape(blocks, share, width).transpose(1, 0, 2)
+    packed = jnp.concatenate(
+        [time_proj, time_out, up_order.reshape(share, -1), down_order.reshape(share, -1)], axis=1
+    )
+    first, second, by_place = tie(first, second, tokens.transpose(0, 2, 1, 3))
+    half = by_place.shape[1] // 2
+    send = pick(by_place, 1 - place, 0)
+    rest_a = swap_axis(send[:half], "frame")
+    first = collect_lines(first)
+    second, first, rest_a, send, packed = tie(second, first, rest_a, send, packed)
+    packed = lax.all_gather(packed, axes, axis=0, tiled=True)
+    rest_b = swap_axis(send[half:], "frame")
+    second = collect_lines(second)
+    first = collect_half(first, 2, 1)
+    first, second = tie(first, second)
+    second = collect_half(second, 2, 1)
+    second, rest_b, g_send = tie(second, rest_b, cotangent.transpose(0, 2, 1, 3))
+    g_rest = swap_axis(pick(g_send, 1 - place, 0), "frame")
+    first = merged(collect_half(first, 1, 2))
+    second = merged(collect_half(second, 1, 2))
+    rest = jnp.concatenate([rest_a, rest_b], axis=0).transpose(1, 0, 2)
+    own = pick(tokens, place, 0)
+    g_own = pick(cotangent, place, 0)
+    table = second[:, 2 * width : 2 * width + 3].astype(WIDE).T
     sgain, tgain, fgain = (table[index : index + 1] for index in range(3))
-    w_sproj, w_sout = space[:, :proj_width], space[:, proj_width : 4 * width]
-    w_tproj, w_tout = time[:, :proj_width], time[:, proj_width:]
-
-    in_o, qkv_o, o_o, after_o = space_forward(own, sgain, w_sproj, w_sout)
-    in_r, qkv_r, o_r, after_r = space_forward(rest, sgain, w_sproj, w_sout)
-    qkv_t, in_t, o_t, in_f, act, gh, gb, mixed_o, mixed_r, g_time, gain_f = middle(
-        after_o, after_r, g_own, g_rest, tgain, fgain, w_tproj, w_tout, up, down
+    in_o, qkv_o, o_o, after_o = space_forward(own, sgain, first, second)
+    rest, after_o = tie(rest, after_o)
+    in_r, qkv_r, o_r, after_r = space_forward(rest, sgain, first, second)
+    g_rest, after_r = tie(g_rest, after_r)
+    g_rest = g_rest.transpose(1, 0, 2)
+    qkv_t, in_t, o_t, in_f, act, gh, gb, mixed, mixed_r, g_time, gain_f = middle(
+        spot, after_o, after_r, g_own, g_rest, tgain, fgain, packed
     )
     mixed_other = swap_axis(mixed_r, "frame")
     scatter = lambda item: lax.psum_scatter(item, axes, scatter_dimension=0, tiled=True)
-    d_down = scatter(weight_gradient(act, gb)).astype(WIDE)
-    d_up = scatter(weight_gradient(in_f, gh)).astype(WIDE)
+    d_up = weight_gradient(([(in_f, gh)], 0, blocks, 1, 0))
+    d_up, act = tie(d_up, act)
+    d_up = scatter(d_up)
+    d_down = weight_gradient(([(act, gb)], 0, blocks, 0, 0))
+    d_down, g_time = tie(d_down, g_time)
     gq_t, tb, gs_o, gs_r, gain_t = time_backward(
-        qkv_t, g_time, after_o, after_r, tgain, w_tout, w_tproj
-    )
-    d_time = scatter(
-        jnp.concatenate([weight_gradient(in_t, gq_t), weight_gradient(o_t, tb)], axis=1)
-    ).astype(WIDE)
-    gq_r, sb_r, gx_r, gain_sr = space_backward(rest, gs_r, qkv_r, sgain, w_sout, w_sproj, LOW)
+        qkv_t, g_time, after_o, after_r, tgain, packed
+    )
+    d_time = split_gradient(
+        core, owners, ([(in_t, gq_t)], 0, 3, 1, 0), ([(o_t, tb)], 3, 4, 1, 0)
+    )
+    d_up, d_down, d_time, gs_r, mixed_other = tie(d_up, d_down, d_time, gs_r, mixed_other)
+    d_down = scatter(d_down)
+    d_time = scatter_columns(*scatter_core(*d_time))
+    gq_r, sb_r, gx_r, gain_sr = space_backward(spot, rest, gs_r, qkv_r, sgain, first, second, LOW)
     grad_other = swap_axis(gx_r, "frame")
-    gq_o, sb_o, gx_o, gain_so = space_backward(own, gs_o, qkv_o, sgain, w_sout, w_sproj, WIDE)
-    gain_grads = jnp.stack(
-        [jnp.sum(item, axis=0) for item in (gain_so + gain_sr, gain_t, gain_f)], axis=1
-    )
-    gain_grads = jnp.pad(gain_grads, ((0, 0), (0, LANES - 3))).astype(LOW)
-    d_space = scatter(
-        jnp.concatenate(
+    d_time, gs_o, sb_r = tie(d_time, gs_o, sb_r)
+    d_time = scatter_lines(*d_time)
+    gq_o, sb_o, grad_tokens, gain_so = space_backward(spot, own, gs_o, qkv_o, sgain, first, second, WIDE)
+    d_down, d_time, gq_o, sb_o = tie(d_down, d_time, gq_o, sb_o)
+    inputs = [(flat_rows(in_o), flat_rows(gq_o)), (flat_rows(in_r), flat_rows(gq_r))]
+    outputs = [(flat_rows(o_o), flat_rows(sb_o)), (flat_rows(o_r), flat_rows(sb_r))]
+    d_first = scatter_core(*split_gradient(core, owners, (inputs, 0, 2, 1, 0)))
+    d_second = split_gradient(core, owners, (inputs, 0, 1, 1, 2), (outputs, 1, 2, 1, 0))
+    gain_parts = tie(gain_so, gain_sr, gain_t, gain_f, d_first[0])
+    d_first = (gain_parts[4], d_first[1])
+    gain_grads = summed(
+        jnp.stack(
             [
-                weight_gradient(
-                    jnp.concatenate([in_o, in_r]), jnp.concatenate([gq_o, gq_r])
-                ),
-                weight_gradient(jnp.concatenate([o_o, o_r]), jnp.concatenate([sb_o, sb_r])),
-                gain_grads,
-            ],
-            axis=1,
+                jnp.sum(item, axis=0)
+                for item in (gain_parts[0] + gain_parts[1], gain_parts[2], gain_parts[3])
+            ]
         )
-    ).astype(WIDE)
-    mixed = own_first(mixed_o, mixed_other, place)
-    grad_tokens = own_first(gx_o, grad_other.astype(WIDE), place)
+    )
+    d_first, d_second = tie(d_first, d_second)
+    d_second = scatter_core(*d_second)
+    d_first = scatter_columns(*d_first)
+    d_second = scatter_columns(*d_second)
+    d_time = scatter_frames(*d_time)
+    d_first = scatter_frames(*scatter_lines(*d_first))
+    d_second = scatter_frames(*scatter_lines(*d_second))
+    d_first, d_second, d_time = (added(*item) for item in (d_first, d_second, d_time))
+    d_up, d_down = d_up.astype(WIDE), d_down.astype(WIDE)
+    d_up = d_up.reshape(share, blocks, owners, share).transpose(0, 2, 1, 3)
+    d_down = d_down.reshape(share, blocks, width).transpose(1, 0, 2)
+    gain_grads = lax.dynamic_slice_in_dim(gain_grads, me * share, share, axis=1)
+    mixed = lax.dynamic_update_index_in_dim(mixed, mixed_other, 1 - place, 0)
+    grad_tokens = lax.dynamic_update_index_in_dim(
+        grad_tokens, grad_other.astype(WIDE), 1 - place, 0
+    )
+    mixed, grad_tokens = mixed.transpose(0, 2, 1, 3), grad_tokens.transpose(0, 2, 1, 3)
     return (
         mixed,
         grad_tokens,
-        d_space[:, 4 * width],
-        d_space[:, 4 * width + 1],
-        d_space[:, 4 * width + 2],
-        d_space[:, :proj_width],
-        d_space[:, proj_width : 4 * width],
-        d_time[:, :proj_width],
-        d_time[:, proj_width:],
-        d_up,
-        d_down,
+        gain_grads[0],
+        gain_grads[1],
+        gain_grads[2],
+        jnp.concatenate([d_first, d_second[:, :width]], axis=1),
+        d_second[:, width:],
+        d_time[:, : 3 * width],
+        d_time[:, 3 * width :],
+        d_up.reshape(up_proj.shape),
+        d_down.reshape(down_proj.shape),
     )
 
 

time: 995 us -> 711 us (0.71)
  waiting for transfers between devices: 428 us -> 84.8 us
  Pallas kernels: 375 us -> 479 us
  matrix products: 91 us -> 0 us
  starting transfers between devices: 6.15 us -> 46.7 us
  other arithmetic: 19.1 us -> 30.9 us
    ppermute x4 -> x11, waiting for transfers between devices: 224 us -> 16.9 us  [swap_axis(): lax.ppermute(values, axis, [(index, size - 1 - index) for index in range(...]
    unnamed x9 -> x3, waiting for transfers between devices: 109 us -> 0.05 us
    pallas_call x3 -> x8, Pallas kernels: 240 us -> 343 us  [the longest x1 128 us: middle(): pl.pallas_call(functools.partial(middle_kernel, places), grid_spec=pltpu....]
    dot_general x6 -> x0, matrix products: 91 us -> none  [dot(): return lax.dot_general(first, second, numbers, preferred_element_type=WIDE)]
    all_gather x4 -> x1, waiting for transfers between devices: 72.5 us -> 8.44 us  [clip_local(): packed = lax.all_gather(packed, axes, axis=0, tiled=True)]
    ppermute x0 -> x29, waiting for transfers between devices: none -> 59.4 us  [flip(): lax.ppermute(values, 'clip', [(index, index ^ mask) for index in range(si...]
    ppermute x0 -> x29, starting transfers between devices: none -> 30.9 us  [flip(): lax.ppermute(values, 'clip', [(index, index ^ mask) for index in range(si...]
    reduce_scatter x3 -> x2, waiting for transfers between devices: 22.2 us -> 0.03 us  [clip_local(): lax.psum_scatter(item, axes, scatter_dimension=0, tiled=True)]
  transfers between devices with their start and end apart: 12 -> 43, of which waited for: 8 -> 17; matrix products, arithmetic and copies ran while one was open for 13% -> 10% of each run, Pallas kernels for 17% -> 47%
where the time goes in v2:
time: 711 us; the launch traced here: 704 us
  Pallas kernels  479 us (67%)
  waiting for transfers between devices  84.8 us (12%)
  local copies, waits for them, and re-layouts  47.6 us (7%)
  starting transfers between devices  46.7 us (7%)
  other arithmetic  30.9 us (4%)
  between operations  14.9 us (2%)
    pallas_call x1, Pallas kernels, middle(): pl.pallas_call(functools.partial(middle_kernel, places), grid_spec=pltpu....  128 us
    pallas_call x2, Pallas kernels, space_backward(): pl.pallas_call(functools.partial(space_backward_kernel, places), grid_spe...  113 us
    pallas_call x1, Pallas kernels, time_backward(): pl.pallas_call(time_backward_kernel, grid=(groups // 2,), in_specs=[by_ro...  76.7 us
    ppermute x29, waiting for transfers between devices, flip(): lax.ppermute(values, 'clip', [(index, index ^ mask) for index in range(si...  59.4 us
    pallas_call x2, Pallas kernels, space_forward(): pl.pallas_call(functools.partial(space_forward_kernel, places), grid=(fra...  59.1 us
    pallas_call x3, Pallas kernels, split_gradient(): pl.pallas_call(functools.partial(gradient_kernel, parts, tiles), grid_spe...  57.4 us
    pallas_call x2, Pallas kernels, weight_gradient(): pl.pallas_call(functools.partial(gradient_kernel, parts, tiles, None), gr...  44 us
    ppermute x29, starting transfers between devices, flip(): lax.ppermute(values, 'clip', [(index, index ^ mask) for index in range(si...  30.9 us
  transfers between devices with their start and end apart: 43, of which 17 were waited for; matrix products, arithmetic and copies ran while one was open for 10% of the time, Pallas kernels for 47%

profile of v2, /device:TPU:0, one launch (start us, length us, event | category | flops | bytes accessed | tf_op | source)
XLA Modules:
  0.0 704.0 jit_solution(8992683176049123058)
XLA Ops:
  8.2 3.0 collective-permute-start
  13.6 2.1 reshape.161
  18.1 2.4 dynamic-slice_bitcast_fusion.2
  22.6 1.6 collective-permute-start.2
  24.2 2.6 collective-permute-start.3
  27.0 1.8 dynamic-slice_bitcast_fusion.1
  29.5 8.0 %collective-permute-done.3 = bf16[2,24,1536]{2,1,0:T(8,128)(2,1)S(1)} collective-permute-done((bf16[2,24,1536]{2,1,0:T(8,128)(2,1)S(1)}, bf16[2,24,1536]{2,1,0:T(8,128)(2,1)S(1)}, u32[]{:S(2)}, u32[]{:S(2)}) %collective-permute-start.3) | collective-permute-done | bytes 147488 | tf_op jit(solution)/shard_map/ppermute | solution.py:1033
  37.6 10.4 %collective-permute-done.5 = bf16[98,8,768]{2,1,0:T(8,128)(2,1)} collective-permute-done((bf16[98,8,768]{2,1,0:T(8,128)(2,1)}, bf16[98,8,768]{2,1,0:T(8,128)(2,1)}, u32[]{:S(2)}, u32[]{:S(2)}) %collective-permute-start.5) | collective-permute-done | bytes 1204256 | tf_op jit(solution)/shard_map/ppermute | solution.py:1028
  48.1 1.9 collective-permute-start.7
  50.0 2.6 collective-permute-start.8
  52.6 1.7 collective-permute-start.6
  54.4 1.6 collective-permute-start.11
  55.9 9.9 %collective-permute-done.8 = bf16[2,24,1664]{2,1,0:T(8,128)(2,1)S(1)} collective-permute-done((bf16[2,24,1664]{2,1,0:T(8,128)(2,1)S(1)}, bf16[2,24,1664]{2,1,0:T(8,128)(2,1)S(1)}, u32[]{:S(2)}, u32[]{:S(2)}) %collective-permute-start.8) | collective-permute-done | bytes 159776 | tf_op jit(solution)/shard_map/ppermute | solution.py:1033
  67.0 3.7 collective-permute-done.6
  72.3 10.2 %collective-permute-done.10 = bf16[4,2,24,1664]{3,2,1,0:T(8,128)(2,1)S(1)} collective-permute-done((bf16[4,2,24,1664]{3,2,1,0:T(8,128)(2,1)S(1)}, bf16[4,2,24,1664]{3,2,1,0:T(8,128)(2,1)S(1)}, u32[]{:S(2)}, u32[]{:S(2)}) %collective-permute-start.10) | collective-permute-done | bytes 639008 | tf_op jit(solution)/shard_map/ppermute | solution.py:1033
  82.7 2.7 collective-permute-done.11
  86.5 3.3 dynamic-slice_bitcast_fusion
  89.7 2.5 collective-permute-start.14
  92.2 1.8 constant_dynamic-slice_fusion.3
  94.0 1.9 copy.108
  96.0 1.8 constant_dynamic-slice_fusion.2
  97.8 1.9 copy.107
  99.7 1.6 copy.73
  101.6 1.8 maximum_bitcast_fusion.x_ref
  103.4 2.0 maximum_select_fusion.1
  105.4 1.6 copy.77
  107.0 2.3 maximum_select_fusion
  110.7 1.7 copy.78.gain_ref.gain_row_ref
  112.5 30.3 %space_forward.2 = (bf16[8,208,768]{2,1,0:T(8,128)(2,1)}, bf16[8,208,2304]{2,1,0:T(8,128)(2,1)}, bf16[8,208,768]{2,1,0:T(8,128)(2,1)}, f32[26,8,8,768]{3,2,1,0:T(8,128)}) custom-call(bf16[8,196,768]{2,1,0:T(8,128)(2,1)} %bitcast.186, f32[1,768]{1,0:T(1,128)} %copy.78.gain_ref.gain_row_ref, bf16[768,1536]{1,0:T(8,128)(2,1)} %bitcast.178, ...), custom_call_target="tpu_custom_call" | custom-call | flops 1663041536 | bytes 4202496 | tf_op jit(solution)/shard_map/space_forward/pallas_call | solution.py:426
  144.2 28.8 %space_forward.3 = (bf16[8,208,768]{2,1,0:T(8,128)(2,1)}, bf16[8,208,2304]{2,1,0:T(8,128)(2,1)}, bf16[8,208,768]{2,1,0:T(8,128)(2,1)}, f32[26,8,8,768]{3,2,1,0:T(8,128)}) custom-call(bf16[8,196,768]{2,1,0:T(8,128)(2,1)} %maximum_bitcast_fusion.x_ref, f32[1,768]{1,0:T(1,128)} %copy.78.gain_ref.gain_row_ref, bf16[768,1536]{1,0:T(8,128)(2,1)} %bitcast.179, ...), custom_call_target="tpu_custom_call" | custom-call | flops 1663041536 | bytes 4202496 | tf_op jit(solution)/shard_map/space_forward/pallas_call | solution.py:426
  173.0 3.7 copy.106
  176.7 8.4 %all-gather.2.cloned.1.call-done.tproj_ref.tout_ref.up_ref.down_ref = bf16[768,9216]{1,0:T(8,128)(2,1)} async-done(((bf16[24,9216]{1,0:T(8,128)(2,1)}), bf16[768,9216]{1,0:T(8,128)(2,1)}) %all-gather.2.cloned.1.call-update) | async-done | bytes 14155792 | tf_op jit(solution)/shard_map/all_gather | solution.py:1154
  185.1 128.4 %middle.1 = (bf16[3328,2304]{1,0:T(8,128)(2,1)}, bf16[3328,768]{1,0:T(8,128)(2,1)}, bf16[3328,768]{1,0:T(8,128)(2,1)}, bf16[3328,768]{1,0:T(8,128)(2,1)}, bf16[3...) custom-call(s32[1]{0:T(128)} %bitcast.place_ref, ...), custom_call_target="tpu_custom_call" | custom-call | flops 13522436096 | bytes 18198528 | tf_op jit(solution)/shard_map/middle/pallas_call | solution.py:475
  313.5 21.9 %weight_gradient.2 = bf16[768,3072]{1,0:T(8,128)(2,1)} custom-call(bf16[3328,768]{1,0:T(8,128)(2,1)} %get-tuple-element.116.refs_0_, bf16[3328,3072]{1,0:T(8,128)(2,1)} %get-tuple-element.117.refs_1_), custom_call_target="tpu_custom_call" | custom-call | flops 2617245696 | bytes 5046272 | tf_op jit(solution)/shard_map/weight_gradient/pallas_call | solution.py:655
  336.2 22.1 %weight_gradient.3 = bf16[768,3072]{1,0:T(8,128)(2,1)} custom-call(bf16[3328,3072]{1,0:T(8,128)(2,1)} %get-tuple-element.120.refs_0_, bf16[3328,768]{1,0:T(8,128)(2,1)} %get-tuple-element.121.refs_1_), custom_call_target="tpu_custom_call" | custom-call | flops 2617245696 | bytes 5046272 | tf_op jit(solution)/shard_map/weight_gradient/pallas_call | solution.py:655
  358.4 76.7 %time_backward.1 = (bf16[3328,2304]{1,0:T(8,128)(2,1)}, bf16[3328,768]{1,0:T(8,128)(2,1)}, f32[8,208,768]{2,1,0:T(8,128)}, f32[8,208,768]{2,1,0:T(8,128)}, f32[8,768]{1,0:T(8,128)}) custom-call(bf16[3328,2304]{1,0:T(8,128)(2,1)} %get-tuple-element.125.qkv_ref, f32[3328,768]{1,0:T(8,128)} %get-tuple-element.126.gt_ref, ...), custom_call_target="tpu_custom_call" | custom-call | flops 3707764736 | bytes 11079680 | tf_op jit(solution)/shard_map/time_backward/pallas_call | solution.py:527
  435.1 25.4 %split_gradient.3 = (bf16[8,48,3072]{2,1,0:T(8,128)(2,1)}, bf16[8,48,3072]{2,1,0:T(8,128)(2,1)}) custom-call(s32[1]{0:T(128)} %bitcast.39.core_ref, bf16[3328,768]{1,0:T(8,128)(2,1)} %get-tuple-element.124.refs_0_, bf16[3328,2304]{1,0:T(8,128)(2,1)} %get-tuple-element.127.refs_1_, bf16[3328,768]{1,0:T(8,128)(2,1)} %get-tuple-element.128.refs_2_, ...), custom_call_target="tpu_custom_call" | custom-call | flops 2617245696 | bytes 5898240 | tf_op jit(solution)/shard_map/split_gradient/pallas_call | solution.py:672
  460.6 4.9 collective-permute-done.16
  465.5 3.2 fusion.1
  470.0 56.4 %space_backward.2 = (bf16[8,208,2304]{2,1,0:T(8,128)(2,1)}, bf16[8,208,768]{2,1,0:T(8,128)(2,1)}, bf16[196,8,768]{2,1,0:T(8,128)(2,1)}, f32[8,768]{1,0:T(8,128)}) custom-call(s32[1]{0:T(128)} %bitcast.place_ref, bf16[8,196,768]{2,1,0:T(8,128)(2,1)} %maximum_bitcast_fusion.x_ref, f32[8,208,768]{2,1,0:T(8,128)} %get-tuple-element.138.gs_ref, ...), custom_call_target="tpu_custom_call" | custom-call | flops 2194669568 | bytes 4640768 | tf_op jit(solution)/shard_map/space_backward/pallas_call | solution.py:560
  526.4 1.5 collective-permute-start.18
  527.9 2.0 fusion
  529.9 1.7 add_convert_fusion
  533.0 1.5 collective-permute-start.20
  534.5 2.5 collective-permute-start.21
  537.0 57.0 %space_backward.3 = (bf16[8,208,2304]{2,1,0:T(8,128)(2,1)}, bf16[8,208,768]{2,1,0:T(8,128)(2,1)}, f32[2,196,8,768]{3,2,1,0:T(8,128)}, f32[8,768]{1,0:T(8,128)}) custom-call(s32[1]{0:T(128)} %bitcast.place_ref, bf16[8,196,768]{2,1,0:T(8,128)(2,1)} %bitcast.187, f32[8,208,768]{2,1,0:T(8,128)} %get-tuple-element.141.gs_ref, ...), custom_call_target="tpu_custom_call" | custom-call | flops 2194669568 | bytes 5844992 | tf_op jit(solution)/shard_map/space_backward/pallas_call | solution.py:560
  594.2 14.6 %split_gradient.4 = (bf16[8,48,1536]{2,1,0:T(8,128)(2,1)}, bf16[8,48,1536]{2,1,0:T(8,128)(2,1)}) custom-call(s32[1]{0:T(128)} %bitcast.39.core_ref, bf16[1664,768]{1,0:T(8,128)(2,1)} %bitcast.188, bf16[1664,2304]{1,0:T(8,128)(2,1)} %bitcast.184, bf16[1664,768]{1,0:T(8,128)(2,1)} %bitcast.190, bf16[1664,2304]{1,0:T(8,128)(2,1)} %bitcast.182), custom_call_target="tpu_custom_call" | custom-call | flops 1308622848 | bytes 3801088 | tf_op jit(solution)/shard_map/split_gradient/pallas_call | solution.py:672
  609.6 1.6 bitcast_dynamic-update-slice_fusion
  613.6 2.6 reshape.198
  618.1 4.4 convert_dynamic-update-slice_fusion
  623.4 3.5 collective-permute-done.24
  627.5 17.4 %split_gradient.5 = (bf16[8,48,1536]{2,1,0:T(8,128)(2,1)}, bf16[8,48,1536]{2,1,0:T(8,128)(2,1)}) custom-call(s32[1]{0:T(128)} %bitcast.39.core_ref, bf16[1664,768]{1,0:T(8,128)(2,1)} %bitcast.189, bf16[1664,2304]{1,0:T(8,128)(2,1)} %bitcast.185, bf16[1664,768]{1,0:T(8,128)(2,1)} %bitcast.191, bf16[1664,2304]{1,0:T(8,128)(2,1)} %bitcast.183, ...), custom_call_target="tpu_custom_call" | custom-call | flops 1308622848 | bytes 5505024 | tf_op jit(solution)/shard_map/split_gradient/pallas_call | solution.py:672
  648.6 1.5 collective-permute-start.39
  650.1 1.8 reshape.206
  651.9 1.7 copy.94
  654.9 5.4 collective-permute-done.28
  664.2 1.8 collective-permute-start.31
  670.9 3.3 collective-permute-done.30
  674.2 4.6 collective-permute-done.34
  680.4 2.6 collective-permute-start.36
  683.1 1.5 collective-permute-start.37
  685.8 1.5 collective-permute-done.35
  687.3 3.7 collective-permute-done.36
  692.5 3.1 collective-permute-done.38
  (163 shorter events, 45.7 us)
Async XLA Ops:
  7.2 10.0 %copy-start.14 = (bf16[96,768]{1,0:T(8,128)(2,1)S(1)}, bf16[96,768]{1,0:T(8,128)(2,1)}, u32[]{:S(2)}) copy-start(bf16[96,768]{1,0:T(8,128)(2,1)} %param.21) | copy-start | bytes 442372
  7.2 177.9 %all-gather.2.cloned.1.call-start = ((), (), s32[]{:S(2)}) async-start(), calls=%async_computation.2 | async-start | bytes 14598144 | tf_op jit(solution)/shard_map/all_gather | solution.py:1154
  8.2 9.1 %collective-permute-start = (bf16[24,1536]{1,0:T(8,128)(2,1)S(1)}, bf16[24,1536]{1,0:T(8,128)(2,1)S(1)}, u32[]{:S(2)}, u32[]{:S(2)}) collective-permute-start(bf16[24,1536]{1,0:T(8,128)(2,1)S(1)} %get-tuple-element.205), channel_id=1, source_target_pairs={{0,1},{1,0},{2,3},{3,2},{4,5},{5,4},{6,7},{7,6},{8,9},{9,8},{10,11... | collective-permute-start | bytes 221192 | tf_op jit(solution)/shard_map/ppermute | solution.py:1028
  13.5 4.5 collective-permute-start.1
  15.9 5.9 copy-start.16
  15.9 5.9 copy-start.17
  20.4 27.6 %collective-permute-start.5 = (bf16[98,8,768]{2,1,0:T(8,128)(2,1)}, bf16[98,8,768]{2,1,0:T(8,128)(2,1)}, u32[]{:S(2)}, u32[]{:S(2)}) collective-permute-start(bf16[98,8,768]{2,1,0:T(8,128)(2,1)} %dynamic-slice_bitcast_fusion.2), channel_id=1, source_target_pairs={{0,1},{1,0},{2,3},{3,2},{4,5},{5,4},{6,7},{7,6},{8,9},{9,8},{10,11... | collective-permute-start | bytes 3612680 | tf_op jit(solution)/shard_map/ppermute | solution.py:1028
  22.6 6.9 collective-permute-start.2
  24.2 13.3 %collective-permute-start.3 = (bf16[2,24,1536]{2,1,0:T(8,128)(2,1)S(1)}, bf16[2,24,1536]{2,1,0:T(8,128)(2,1)S(1)}, u32[]{:S(2)}, u32[]{:S(2)}) collective-permute-start(bf16[2,24,1536]{2,1,0:T(8,128)(2,1)S(1)} %maximum_select_fusion.5), channel_id=1, source_target_pairs={{0,16},{2,18},{4,20},{6,22},{8,24},{10,26},{12,28},{14,30},{16,0},... | collective-permute-start | bytes 442376 | tf_op jit(solution)/shard_map/ppermute | solution.py:1033
  26.8 10.7 %collective-permute-start.4 = (bf16[2,24,1536]{2,1,0:T(8,128)(2,1)S(1)}, bf16[2,24,1536]{2,1,0:T(8,128)(2,1)S(1)}, u32[]{:S(2)}, u32[]{:S(2)}) collective-permute-start(bf16[2,24,1536]{2,1,0:T(8,128)(2,1)S(1)} %maximum_select_fusion.5), channel_id=1, source_target_pairs={{0,24},{2,26},{4,28},{6,30},{8,16},{10,18},{12,20},{14,22},{16,8},... | collective-permute-start | bytes 442376 | tf_op jit(solution)/shard_map/ppermute | solution.py:1033
  48.1 412.5 %reduce-scatter.3.cloned.1.call-start = ((), (), s32[]{:S(2)}) async-start(), calls=%async_computation.3 | async-start | bytes 4866048 | tf_op jit(solution)/shard_map/reduce_scatter | solution.py:1178
  48.1 7.8 %collective-permute-start.7 = (bf16[2,24,1664]{2,1,0:T(8,128)(2,1)S(1)}, bf16[2,24,1664]{2,1,0:T(8,128)(2,1)S(1)}, u32[]{:S(2)}, u32[]{:S(2)}) collective-permute-start(bf16[2,24,1664]{2,1,0:T(8,128)(2,1)S(1)} %maximum_select_fusion.4), channel_id=1, source_target_pairs={{0,8},{2,10},{4,12},{6,14},{8,0},{10,2},{12,4},{14,6},{16,24},{18,... | collective-permute-start | bytes 479240 | tf_op jit(solution)/shard_map/ppermute | solution.py:1033
  50.0 15.9 %collective-permute-start.8 = (bf16[2,24,1664]{2,1,0:T(8,128)(2,1)S(1)}, bf16[2,24,1664]{2,1,0:T(8,128)(2,1)S(1)}, u32[]{:S(2)}, u32[]{:S(2)}) collective-permute-start(bf16[2,24,1664]{2,1,0:T(8,128)(2,1)S(1)} %maximum_select_fusion.4), channel_id=1, source_target_pairs={{0,16},{2,18},{4,20},{6,22},{8,24},{10,26},{12,28},{14,30},{16,0},... | collective-permute-start | bytes 479240 | tf_op jit(solution)/shard_map/ppermute | solution.py:1033
  52.6 13.3 %collective-permute-start.9 = (bf16[2,24,1664]{2,1,0:T(8,128)(2,1)S(1)}, bf16[2,24,1664]{2,1,0:T(8,128)(2,1)}, u32[]{:S(2)}, u32[]{:S(2)}) collective-permute-start(bf16[2,24,1664]{2,1,0:T(8,128)(2,1)S(1)} %maximum_select_fusion.4), channel_id=1, source_target_pairs={{0,24},{2,26},{4,28},{6,30},{8,16},{10,18},{12,20},{14,22},{16,8},... | collective-permute-start | bytes 479240 | tf_op jit(solution)/shard_map/ppermute | solution.py:1033
  52.6 18.1 %collective-permute-start.6 = (bf16[4,2,24,1536]{3,2,1,0:T(8,128)(2,1)S(1)}, bf16[4,2,24,1536]{3,2,1,0:T(8,128)(2,1)S(1)}, u32[]{:S(2)}, u32[]{:S(2)}) collective-permute-start(bf16[4,2,24,1536]{3,2,1,0:T(8,128)(2,1)S(1)} %pad_maximum_fusion.1), channel_id=1, source_target_pairs={{0,4},{2,6},{4,0},{6,2},{8,12},{10,14},{12,8},{14,10},{16,20},{18,... | collective-permute-start | bytes 1769480 | tf_op jit(solution)/shard_map/ppermute | solution.py:1033
  54.4 31.0 %collective-permute-start.11 = (bf16[98,8,768]{2,1,0:T(8,128)(2,1)S(1)}, bf16[98,8,768]{2,1,0:T(8,128)(2,1)S(1)}, u32[]{:S(2)}, u32[]{:S(2)}) collective-permute-start(bf16[98,8,768]{2,1,0:T(8,128)(2,1)S(1)} %slice.52), channel_id=1, source_target_pairs={{0,1},{1,0},{2,3},{3,2},{4,5},{5,4},{6,7},{7,6},{8,9},{9,8},{10,11... | collective-permute-start | bytes 3612680 | tf_op jit(solution)/shard_map/ppermute | solution.py:1028
  70.9 11.6 %collective-permute-start.10 = (bf16[4,2,24,1664]{3,2,1,0:T(8,128)(2,1)S(1)}, bf16[4,2,24,1664]{3,2,1,0:T(8,128)(2,1)S(1)}, u32[]{:S(2)}, u32[]{:S(2)}) collective-permute-start(bf16[4,2,24,1664]{3,2,1,0:T(8,128)(2,1)S(1)} %pad_maximum_fusion), channel_id=1, source_target_pairs={{0,4},{2,6},{4,0},{6,2},{8,12},{10,14},{12,8},{14,10},{16,20},{18,... | collective-permute-start | bytes 1916936 | tf_op jit(solution)/shard_map/ppermute | solution.py:1033
  72.3 31.1 %collective-permute-start.13 = (bf16[4,2,2,24,1536]{4,3,2,0,1:T(8,128)(2,1)S(1)}, bf16[4,2,2,24,1536]{4,3,2,0,1:T(8,128)(2,1)}, u32[]{:S(2)}, u32[]{:S(2)}) collective-permute-start(bf16[4,2,2,24,1536]{4,3,2,0,1:T(8,128)(2,1)S(1)} %maximum_select_fusion.3), channel_id=1, source_target_pairs={{0,2},{2,0},{4,6},{6,4},{8,10},{10,8},{12,14},{14,12},{16,18},{18,... | collective-permute-start | bytes 3538952 | tf_op jit(solution)/shard_map/ppermute | solution.py:1033
  86.5 20.5 %collective-permute-start.12 = (bf16[4,2,2,24,1664]{4,3,2,0,1:T(8,128)(2,1)S(1)}, bf16[4,2,2,24,1664]{4,3,2,0,1:T(8,128)(2,1)}, u32[]{:S(2)}, u32[]{:S(2)}) collective-permute-start(bf16[4,2,2,24,1664]{4,3,2,0,1:T(8,128)(2,1)S(1)} %maximum_select_fusion.2), channel_id=1, source_target_pairs={{0,2},{2,0},{4,6},{6,4},{8,10},{10,8},{12,14},{14,12},{16,18},{18,... | collective-permute-start | bytes 3833864 | tf_op jit(solution)/shard_map/ppermute | solution.py:1033
  89.7 83.3 %collective-permute-start.14 = (bf16[196,8,768]{2,1,0:T(8,128)(2,1)}, bf16[196,8,768]{2,1,0:T(8,128)(2,1)}, u32[]{:S(2)}, u32[]{:S(2)}) collective-permute-start(bf16[196,8,768]{2,1,0:T(8,128)(2,1)} %dynamic-slice_bitcast_fusion), channel_id=1, source_target_pairs={{0,1},{1,0},{2,3},{3,2},{4,5},{5,4},{6,7},{7,6},{8,9},{9,8},{10,11... | collective-permute-start | bytes 7225352 | tf_op jit(solution)/shard_map/ppermute | solution.py:1028
  99.7 1.6 copy-start.2
  109.5 3.0 copy-start
  335.4 258.8 %reduce-scatter.5.cloned.1.call-start = ((), (), s32[]{:S(2)}) async-start(), calls=%async_computation.4 | async-start | bytes 4866048 | tf_op jit(solution)/shard_map/reduce_scatter | solution.py:1178
  335.4 125.1 %collective-permute-start.15 = (bf16[196,8,768]{2,1,0:T(8,128)(2,1)}, bf16[196,8,768]{2,1,0:T(8,128)(2,1)S(1)}, u32[]{:S(2)}, u32[]{:S(2)}) collective-permute-start(bf16[196,8,768]{2,1,0:T(8,128)(2,1)} %get-tuple-element.133), channel_id=1, source_target_pairs={{0,1},{1,0},{2,3},{3,2},{4,5},{5,4},{6,7},{7,6},{8,9},{9,8},{10,11... | collective-permute-start | bytes 7225352 | tf_op jit(solution)/shard_map/ppermute | solution.py:1028
  460.6 4.9 collective-permute-start.16
  468.7 61.3 %collective-permute-start.17 = (bf16[4,48,3072]{2,1,0:T(8,128)(2,1)}, bf16[4,48,3072]{2,1,0:T(8,128)(2,1)}, u32[]{:S(2)}, u32[]{:S(2)}) collective-permute-start(bf16[4,48,3072]{2,1,0:T(8,128)(2,1)} %fusion.1), channel_id=1, source_target_pairs={{0,4},{2,6},{4,0},{6,2},{8,12},{10,14},{12,8},{14,10},{16,20},{18,... | collective-permute-start | bytes 3538952 | tf_op jit(solution)/shard_map/ppermute | solution.py:1033
  526.4 91.7 %collective-permute-start.18 = (bf16[196,8,768]{2,1,0:T(8,128)(2,1)}, bf16[196,8,768]{2,1,0:T(8,128)(2,1)}, u32[]{:S(2)}, u32[]{:S(2)}) collective-permute-start(bf16[196,8,768]{2,1,0:T(8,128)(2,1)} %get-tuple-element.144), channel_id=1, source_target_pairs={{0,1},{1,0},{2,3},{3,2},{4,5},{5,4},{6,7},{7,6},{8,9},{9,8},{10,11... | collective-permute-start | bytes 7225352 | tf_op jit(solution)/shard_map/ppermute | solution.py:1028
  532.7 61.4 %collective-permute-start.19 = (bf16[48,3072]{1,0:T(8,128)(2,1)}, bf16[48,3072]{1,0:T(8,128)(2,1)S(1)}, u32[]{:S(2)}, u32[]{:S(2)}) collective-permute-start(bf16[48,3072]{1,0:T(8,128)(2,1)} %get-tuple-element.183), channel_id=1, source_target_pairs={{0,8},{2,10},{4,12},{6,14},{8,0},{10,2},{12,4},{14,6},{16,24},{18,... | collective-permute-start | bytes 884744 | tf_op jit(solution)/shard_map/ppermute | solution.py:1033
  533.0 61.1 %collective-permute-start.20 = (bf16[48,3072]{1,0:T(8,128)(2,1)}, bf16[48,3072]{1,0:T(8,128)(2,1)S(1)}, u32[]{:S(2)}, u32[]{:S(2)}) collective-permute-start(bf16[48,3072]{1,0:T(8,128)(2,1)} %get-tuple-element.182), channel_id=1, source_target_pairs={{0,16},{2,18},{4,20},{6,22},{8,24},{10,26},{12,28},{14,30},{16,0},... | collective-permute-start | bytes 884744 | tf_op jit(solution)/shard_map/ppermute | solution.py:1033
  534.5 59.6 %collective-permute-start.21 = (bf16[48,3072]{1,0:T(8,128)(2,1)}, bf16[48,3072]{1,0:T(8,128)(2,1)S(1)}, u32[]{:S(2)}, u32[]{:S(2)}) collective-permute-start(bf16[48,3072]{1,0:T(8,128)(2,1)} %get-tuple-element.181), channel_id=1, source_target_pairs={{0,24},{2,26},{4,28},{6,30},{8,16},{10,18},{12,20},{14,22},{16,8},... | collective-permute-start | bytes 884744 | tf_op jit(solution)/shard_map/ppermute | solution.py:1033
  594.1 14.8 %copy-start.8 = (bf16[48,3072]{1,0:T(8,128)(2,1)}, bf16[48,3072]{1,0:T(8,128)(2,1)S(1)}, u32[]{:S(2)}) copy-start(bf16[48,3072]{1,0:T(8,128)(2,1)S(1)} %collective-permute-done.19) | copy-start | bytes 884740
  594.1 14.8 %copy-start.10 = (bf16[48,3072]{1,0:T(8,128)(2,1)}, bf16[48,3072]{1,0:T(8,128)(2,1)S(1)}, u32[]{:S(2)}) copy-start(bf16[48,3072]{1,0:T(8,128)(2,1)S(1)} %collective-permute-done.20) | copy-start | bytes 884740
  594.1 14.8 %copy-start.12 = (bf16[48,3072]{1,0:T(8,128)(2,1)}, bf16[48,3072]{1,0:T(8,128)(2,1)S(1)}, u32[]{:S(2)}) copy-start(bf16[48,3072]{1,0:T(8,128)(2,1)S(1)} %collective-permute-done.21) | copy-start | bytes 884740
  594.2 14.7 %copy-start.20 = (f32[8,768]{1,0:T(8,128)S(1)}, f32[8,768]{1,0:T(8,128)}, u32[]{:S(2)}) copy-start(f32[8,768]{1,0:T(8,128)} %get-tuple-element.160) | copy-start | bytes 73732
  594.2 14.7 %copy-start.21 = (f32[8,768]{1,0:T(8,128)S(1)}, f32[8,768]{1,0:T(8,128)}, u32[]{:S(2)}) copy-start(f32[8,768]{1,0:T(8,128)} %get-tuple-element.159) | copy-start | bytes 73732
  594.2 14.7 %copy-start.19 = (f32[8,768]{1,0:T(8,128)S(1)}, f32[8,768]{1,0:T(8,128)}, u32[]{:S(2)}) copy-start(f32[8,768]{1,0:T(8,128)} %get-tuple-element.161) | copy-start | bytes 73732
  594.2 14.8 %copy-start.18 = (f32[8,768]{1,0:T(8,128)S(1)}, f32[8,768]{1,0:T(8,128)}, u32[]{:S(2)}) copy-start(f32[8,768]{1,0:T(8,128)} %get-tuple-element.162) | copy-start | bytes 73732
  609.6 7.1 %collective-permute-start.22 = (f32[3,768]{1,0:T(4,128)}, f32[3,768]{1,0:T(4,128)}, u32[]{:S(2)}, u32[]{:S(2)}) collective-permute-start(f32[3,768]{1,0:T(4,128)} %pad_maximum_fusion.4), channel_id=1, source_target_pairs={{0,2},{2,0},{4,6},{6,4},{8,10},{10,8},{12,14},{14,12},{16,18},{18,... | collective-permute-start | bytes 27656 | tf_op jit(solution)/shard_map/ppermute | solution.py:1033
  609.6 1.6 copy-start.15
  616.2 29.6 %collective-permute-start.27 = (bf16[8,48,1536]{2,1,0:T(8,128)(2,1)}, bf16[8,48,1536]{2,1,0:T(8,128)(2,1)S(1)}, u32[]{:S(2)}, u32[]{:S(2)}) collective-permute-start(bf16[8,48,1536]{2,1,0:T(8,128)(2,1)} %get-tuple-element.164), channel_id=1, source_target_pairs={{0,2},{2,0},{4,6},{6,4},{8,10},{10,8},{12,14},{14,12},{16,18},{18,... | collective-permute-start | bytes 3538952 | tf_op jit(solution)/shard_map/ppermute | solution.py:1033
  617.4 5.0 collective-permute-start.23
  618.0 5.2 copy-start.7
  618.0 5.2 copy-start.9
  618.0 5.2 copy-start.11
  618.0 5.2 copy-start.13
  623.1 3.8 collective-permute-start.24
  623.4 24.5 %copy-start.5 = (bf16[48,3072]{1,0:T(8,128)(2,1)}, bf16[48,3072]{1,0:T(8,128)(2,1)S(1)}, u32[]{:S(2)}) copy-start(bf16[48,3072]{1,0:T(8,128)(2,1)S(1)} %add_convert_fusion.7) | copy-start | bytes 884740
  626.9 17.9 %collective-permute-start.25 = (f32[3,768]{1,0:T(4,128)S(1)}, f32[3,768]{1,0:T(4,128)S(1)}, u32[]{:S(2)}, u32[]{:S(2)}) collective-permute-start(f32[3,768]{1,0:T(4,128)S(1)} %add.201), channel_id=1, source_target_pairs={{0,16},{2,18},{4,20},{6,22},{8,24},{10,26},{12,28},{14,30},{16,0},... | collective-permute-start | bytes 27656 | tf_op jit(solution)/shard_map/ppermute | solution.py:1033
  627.5 18.3 %copy-start.3 = (bf16[8,48,1536]{2,1,0:T(8,128)(2,1)S(1)}, bf16[8,48,1536]{2,1,0:T(8,128)(2,1)}, u32[]{:S(2)}) copy-start(bf16[8,48,1536]{2,1,0:T(8,128)(2,1)} %get-tuple-element.171) | copy-start | bytes 3538948
  644.9 8.7 %collective-permute-start.26 = (f32[3,768]{1,0:T(4,128)S(1)}, f32[3,768]{1,0:T(4,128)}, u32[]{:S(2)}, u32[]{:S(2)}) collective-permute-start(f32[3,768]{1,0:T(4,128)S(1)} %add.202), channel_id=1, source_target_pairs={{0,1},{1,0},{2,3},{3,2},{4,5},{5,4},{6,7},{7,6},{8,9},{9,8},{10,11... | collective-permute-start | bytes 27656 | tf_op jit(solution)/shard_map/ppermute | solution.py:1028
  646.7 19.3 %copy-start.4 = (bf16[8,48,1536]{2,1,0:T(8,128)(2,1)S(1)}, bf16[8,48,1536]{2,1,0:T(8,128)(2,1)}, u32[]{:S(2)}) copy-start(bf16[8,48,1536]{2,1,0:T(8,128)(2,1)} %get-tuple-element.173) | copy-start | bytes 3538948
  646.7 13.6 %collective-permute-start.28 = (bf16[4,48,1536]{2,1,0:T(8,128)(2,1)}, bf16[4,48,1536]{2,1,0:T(8,128)(2,1)}, u32[]{:S(2)}, u32[]{:S(2)}) collective-permute-start(bf16[4,48,1536]{2,1,0:T(8,128)(2,1)} %fusion.5), channel_id=1, source_target_pairs={{0,4},{2,6},{4,0},{6,2},{8,12},{10,14},{12,8},{14,10},{16,20},{18,... | collective-permute-start | bytes 1769480 | tf_op jit(solution)/shard_map/ppermute | solution.py:1033
  647.9 18.1 %collective-permute-start.33 = (bf16[8,48,1536]{2,1,0:T(8,128)(2,1)}, bf16[8,48,1536]{2,1,0:T(8,128)(2,1)}, u32[]{:S(2)}, u32[]{:S(2)}) collective-permute-start(bf16[8,48,1536]{2,1,0:T(8,128)(2,1)} %get-tuple-element.174), channel_id=1, source_target_pairs={{0,2},{2,0},{4,6},{6,4},{8,10},{10,8},{12,14},{14,12},{16,18},{18,... | collective-permute-start | bytes 3538952 | tf_op jit(solution)/shard_map/ppermute | solution.py:1033
  648.6 19.9 %collective-permute-start.39 = (bf16[24,3072]{1,0:T(8,128)(2,1)}, bf16[24,3072]{1,0:T(8,128)(2,1)}, u32[]{:S(2)}, u32[]{:S(2)}) collective-permute-start(bf16[24,3072]{1,0:T(8,128)(2,1)} %dynamic-slice_bitcast_fusion.7), channel_id=1, source_target_pairs={{0,1},{1,0},{2,3},{3,2},{4,5},{5,4},{6,7},{7,6},{8,9},{9,8},{10,11... | collective-permute-start | bytes 442376 | tf_op jit(solution)/shard_map/ppermute | solution.py:1028
  654.9 13.7 %copy-start.6 = (bf16[48,3072]{1,0:T(8,128)(2,1)S(1)}, bf16[48,3072]{1,0:T(8,128)(2,1)}, u32[]{:S(2)}) copy-start(bf16[48,3072]{1,0:T(8,128)(2,1)} %copy-done.5) | copy-start | bytes 884740
  661.6 9.3 %collective-permute-start.29 = (bf16[48,1536]{1,0:T(8,128)(2,1)S(1)}, bf16[48,1536]{1,0:T(8,128)(2,1)S(1)}, u32[]{:S(2)}, u32[]{:S(2)}) collective-permute-start(bf16[48,1536]{1,0:T(8,128)(2,1)S(1)} %get-tuple-element.189), channel_id=1, source_target_pairs={{0,8},{2,10},{4,12},{6,14},{8,0},{10,2},{12,4},{14,6},{16,24},{18,... | collective-permute-start | bytes 442376 | tf_op jit(solution)/shard_map/ppermute | solution.py:1033
  662.8 11.4 %collective-permute-start.30 = (bf16[48,1536]{1,0:T(8,128)(2,1)S(1)}, bf16[48,1536]{1,0:T(8,128)(2,1)S(1)}, u32[]{:S(2)}, u32[]{:S(2)}) collective-permute-start(bf16[48,1536]{1,0:T(8,128)(2,1)S(1)} %get-tuple-element.191), channel_id=1, source_target_pairs={{0,16},{2,18},{4,20},{6,22},{8,24},{10,26},{12,28},{14,30},{16,0},... | collective-permute-start | bytes 442376 | tf_op jit(solution)/shard_map/ppermute | solution.py:1033
  664.2 9.9 %collective-permute-start.31 = (bf16[48,1536]{1,0:T(8,128)(2,1)S(1)}, bf16[48,1536]{1,0:T(8,128)(2,1)S(1)}, u32[]{:S(2)}, u32[]{:S(2)}) collective-permute-start(bf16[48,1536]{1,0:T(8,128)(2,1)S(1)} %get-tuple-element.190), channel_id=1, source_target_pairs={{0,24},{2,26},{4,28},{6,30},{8,16},{10,18},{12,20},{14,22},{16,8},... | collective-permute-start | bytes 442376 | tf_op jit(solution)/shard_map/ppermute | solution.py:1033
  667.3 11.5 %collective-permute-start.34 = (bf16[4,48,1536]{2,1,0:T(8,128)(2,1)S(1)}, bf16[4,48,1536]{2,1,0:T(8,128)(2,1)S(1)}, u32[]{:S(2)}, u32[]{:S(2)}) collective-permute-start(bf16[4,48,1536]{2,1,0:T(8,128)(2,1)S(1)} %fusion.7), channel_id=1, source_target_pairs={{0,4},{2,6},{4,0},{6,2},{8,12},{10,14},{12,8},{14,10},{16,20},{18,... | collective-permute-start | bytes 1769480 | tf_op jit(solution)/shard_map/ppermute | solution.py:1033
  680.1 7.2 %collective-permute-start.35 = (bf16[48,1536]{1,0:T(8,128)(2,1)S(1)}, bf16[48,1536]{1,0:T(8,128)(2,1)S(1)}, u32[]{:S(2)}, u32[]{:S(2)}) collective-permute-start(bf16[48,1536]{1,0:T(8,128)(2,1)S(1)} %get-tuple-element.192), channel_id=1, source_target_pairs={{0,8},{2,10},{4,12},{6,14},{8,0},{10,2},{12,4},{14,6},{16,24},{18,... | collective-permute-start | bytes 442376 | tf_op jit(solution)/shard_map/ppermute | solution.py:1033
  680.4 10.6 %collective-permute-start.36 = (bf16[48,1536]{1,0:T(8,128)(2,1)S(1)}, bf16[48,1536]{1,0:T(8,128)(2,1)S(1)}, u32[]{:S(2)}, u32[]{:S(2)}) collective-permute-start(bf16[48,1536]{1,0:T(8,128)(2,1)S(1)} %get-tuple-element.194), channel_id=1, source_target_pairs={{0,16},{2,18},{4,20},{6,22},{8,24},{10,26},{12,28},{14,30},{16,0},... | collective-permute-start | bytes 442376 | tf_op jit(solution)/shard_map/ppermute | solution.py:1033
  683.1 8.0 %collective-permute-start.37 = (bf16[48,1536]{1,0:T(8,128)(2,1)S(1)}, bf16[48,1536]{1,0:T(8,128)(2,1)S(1)}, u32[]{:S(2)}, u32[]{:S(2)}) collective-permute-start(bf16[48,1536]{1,0:T(8,128)(2,1)S(1)} %get-tuple-element.193), channel_id=1, source_target_pairs={{0,24},{2,26},{4,28},{6,30},{8,16},{10,18},{12,20},{14,22},{16,8},... | collective-permute-start | bytes 442376 | tf_op jit(solution)/shard_map/ppermute | solution.py:1033
  684.6 7.9 %collective-permute-start.32 = (bf16[24,1536]{1,0:T(8,128)(2,1)S(1)}, bf16[24,1536]{1,0:T(8,128)(2,1)S(1)}, u32[]{:S(2)}, u32[]{:S(2)}) collective-permute-start(bf16[24,1536]{1,0:T(8,128)(2,1)S(1)} %dynamic-slice_bitcast_fusion.15), channel_id=1, source_target_pairs={{0,1},{1,0},{2,3},{3,2},{4,5},{5,4},{6,7},{7,6},{8,9},{9,8},{10,11... | collective-permute-start | bytes 221192 | tf_op jit(solution)/shard_map/ppermute | solution.py:1028
  691.2 4.4 collective-permute-start.38
  (1 other events, 1.0 us)
Sparse Core Ops, SparseCore 0:
  48.2 136.8 all-gather.1
  335.5 109.7 reduce-scatter.2
  460.7 118.6 reduce-scatter.4

commit v3 on v2

--- a/solution.py
+++ b/solution.py
@@ -25,6 +25,8 @@
 STEP = 2 * GROUP
 LIMIT = 60 << 20
 SHRINK = 6
+TIME_BATCH = 12
+SPACE_BATCH = 6
 
 
 def dot(first, second, numbers=NN):
@@ -70,6 +72,31 @@
 def pair(ref, rows, part, index):
     start = (part * PAIRS + index) * LANES
     return ref[rows, start : start + LANES]
+
+
+def batches(count, size):
+    return [range(start, min(start + size, count)) for start in range(0, count, size)]
+
+
+def time_batches(block):
+    spots = [
+        (slice(group * block, (group + 1) * block), index)
+        for group in range(2)
+        for index in range(PAIRS)
+    ]
+    return [spots[start : start + TIME_BATCH] for start in range(0, len(spots), TIME_BATCH)]
+
+
+def shares(scores, axis):
+    highest = [jnp.max(item, axis=axis, keepdims=True) for item in scores]
+    powers = [jnp.exp2((item - top) * POWER) for item, top in zip(scores, highest)]
+    totals = [jnp.sum(item, axis=axis, keepdims=True) for item in powers]
+    return [item * (1.0 / total) for item, total in zip(powers, totals)]
+
+
+def score_grads(chances, grads, axis):
+    means = [jnp.sum(p * g, axis=axis, keepdims=True) for p, g in zip(chances, grads)]
+    return [(p * (g - mean)).astype(LOW) for p, g, mean in zip(chances, grads, means)]
 
 
 def load_padded(x_ref, pad_ref):
@@ -96,27 +123,34 @@
         qkv_ref[:, :, start : start + part.shape[1]] = part.reshape(frames, padded, -1)
     real = lax.broadcasted_iota(jnp.int32, (padded, padded), 1) < places
 
-    def one_frame(frame, carry):
-        for index in range(PAIRS):
-            queries = qkv_ref[frame, :, index * LANES : (index + 1) * LANES]
-            start = width + index * LANES
-            keys = split_heads(qkv_ref[frame, :, start : start + LANES])
-            start = 2 * width + index * LANES
-            value_block = qkv_ref[frame, :, start : start + LANES]
-            outs = []
-            for head in range(2):
-                scores = jnp.where(real, dot(queries, keys[head], NT), NEVER)
-                powers = jnp.exp2((scores - jnp.max(scores, axis=1, keepdims=True)) * POWER)
-                chances = powers * (1.0 / jnp.sum(powers, axis=1, keepdims=True))
-                outs.append(dot(chances.astype(LOW), value_block))
-            o_ref[frame, :, index * LANES : (index + 1) * LANES] = join_heads(*outs).astype(LOW)
-        return carry
-
-    lax.fori_loop(0, frames, one_frame, 0)
+    def one_frame(frame):
+        for batch in batches(PAIRS, SPACE_BATCH):
+            part = lambda number, index: qkv_ref[
+                frame, :, number * width + index * LANES : number * width + (index + 1) * LANES
+            ]
+            keys = [split_heads(part(1, index)) for index in batch]
+            scores = [
+                jnp.where(real, dot(part(0, index), key, NT), NEVER)
+                for index, both in zip(batch, keys)
+                for key in both
+            ]
+            chances = [item.astype(LOW) for item in shares(scores, 1)]
+            outs = [
+                dot(chances[2 * slot + head], part(2, index))
+                for slot, index in enumerate(batch)
+                for head in range(2)
+            ]
+            for slot, index in enumerate(batch):
+                o_ref[frame, :, index * LANES : (index + 1) * LANES] = join_heads(
+                    *outs[2 * slot : 2 * slot + 2]
+                ).astype(LOW)
+
+    for frame in range(frames):
+        one_frame(frame)
     after = values + dot(o_ref[...].reshape(frames * padded, width), out_ref[...])
     after = after.reshape(frames, padded // GROUP, GROUP, width)
     for frame in range(frames):
-        after_ref[:, frame] = after[frame]
+        after_ref[:, frame] = after[frame].astype(after_ref.dtype)
 
 
 def middle_kernel(
@@ -149,27 +183,30 @@
     width = ao_ref.shape[3]
     rows = 2 * frames * GROUP
     block = frames * GROUP
-    values = jnp.concatenate([ao_ref[...], ar_ref[...]], axis=1).reshape(rows, width)
+    values = jnp.concatenate([ao_ref[...].astype(WIDE), ar_ref[...].astype(WIDE)], axis=1).reshape(rows, width)
     in_time = norm_rows(values, tgain_ref[...])[0].astype(LOW)
     int_ref[...] = in_time
     qkv_ref[...] = dot(in_time, tproj_ref[...]).astype(LOW)
     across = lax.broadcasted_iota(jnp.int32, (block, block), 0)
     down = lax.broadcasted_iota(jnp.int32, (block, block), 1)
     bias = jnp.where(((across ^ down) & (GROUP - 1)) == 0, 0.0, NEVER)
-    for group in range(2):
-        own = slice(group * block, (group + 1) * block)
-        for index in range(PAIRS):
-            queries = pair(qkv_ref, own, 0, index)
-            keys = stack_heads(pair(qkv_ref, own, 1, index))
-            value_block = stack_heads(pair(qkv_ref, own, 2, index))
-            both = dot(queries, keys, NT)
-            chances = []
-            for head in range(2):
-                scores = both[:, head * block : (head + 1) * block] + bias
-                powers = jnp.exp2((scores - jnp.max(scores, axis=1, keepdims=True)) * POWER)
-                total = jnp.sum(powers, axis=1, keepdims=True)
-                chances.append((powers * (1.0 / total)).astype(LOW))
-            result = dot(jnp.concatenate(chances, axis=1), value_block)
+    for batch in time_batches(block):
+        both = [
+            dot(pair(qkv_ref, own, 0, index), stack_heads(pair(qkv_ref, own, 1, index)), NT)
+            for own, index in batch
+        ]
+        scores = [
+            item[:, head * block : (head + 1) * block] + bias for item in both for head in range(2)
+        ]
+        chances = [item.astype(LOW) for item in shares(scores, 1)]
+        results = [
+            dot(
+                jnp.concatenate(chances[2 * slot : 2 * slot + 2], axis=1),
+                stack_heads(pair(qkv_ref, own, 2, index)),
+            )
+            for slot, (own, index) in enumerate(batch)
+        ]
+        for result, (own, index) in zip(results, batch):
             ot_ref[own, index * LANES : (index + 1) * LANES] = result.astype(LOW)
     values = values + dot(ot_ref[...], tout_ref[...])
     feed_gain = fgain_ref[...]
@@ -187,29 +224,34 @@
     grad_low = gradient.astype(LOW)
     gb_ref[...] = grad_low
     hidden_width = up_ref.shape[1]
-    piece = width
     root = math.sqrt(2.0 / math.pi)
-    for start in range(0, hidden_width, piece):
-        cut = slice(start, start + piece)
-        hidden = dot(in_feed, up_ref[:, cut])
-        back = dot(grad_low, down_ref[:, cut], NT)
+    cuts = [slice(start, start + width) for start in range(0, hidden_width, width)]
+
+    def products(cut):
+        return dot(in_feed, up_ref[:, cut]), dot(grad_low, down_ref[:, cut], NT)
+
+    mixed = values
+    ready = products(cuts[0])
+    for number, cut in enumerate(cuts):
+        hidden, grad_active = ready
+        if number + 1 < len(cuts):
+            ready = products(cuts[number + 1])
         square = hidden * hidden
-        slope = jnp.tanh(hidden * (root + (root * 0.044715) * square))
-        plus = 0.5 * slope + 0.5
-        act_ref[:, cut] = (hidden * plus).astype(LOW)
-        inner = hidden * (0.5 * root + (1.5 * root * 0.044715) * square)
-        gh_ref[:, cut] = (back * (plus + inner * (1.0 - slope * slope))).astype(LOW)
-    mixed = values
-    for start in range(0, hidden_width, piece):
-        cut = slice(start, start + piece)
+        plus = 0.5 * jnp.tanh(hidden * (root + (root * 0.044715) * square)) + 0.5
+        active = hidden * plus
+        act_ref[:, cut] = active.astype(LOW)
+        inner = 2.0 * root + (6.0 * root * 0.044715) * square
+        gh_ref[:, cut] = (grad_active * (plus + active * (1.0 - plus) * inner)).astype(LOW)
+    for cut in cuts:
         mixed = mixed + dot(act_ref[:, cut], down_ref[:, cut])
+    back = dot(gh_ref[...], up_ref[...], NT)
     mixed = mixed.reshape(2, frames, GROUP, width)
     for group in range(2):
         cut = slice(group * GROUP, (group + 1) * GROUP)
         mo_ref[0, cut] = jnp.swapaxes(mixed[group, :half], 0, 1).astype(LOW)
         mr_ref[cut] = jnp.swapaxes(mixed[group, half:], 0, 1).astype(LOW)
-    back = dot(gh_ref[...], up_ref[...], NT)
-    gt_ref[...] = gradient + norm_back(back, normed, inverse, feed_gain)
+    g_time = gradient + norm_back(back, normed, inverse, feed_gain)
+    gt_ref[...] = g_time.astype(gt_ref.dtype)
 
     @pl.when(pl.program_id(0) == 0)
     def _():
@@ -244,40 +286,42 @@
     across = lax.broadcasted_iota(jnp.int32, (block, block), 0)
     down = lax.broadcasted_iota(jnp.int32, (block, block), 1)
     bias = jnp.where(((across ^ down) & (GROUP - 1)) == 0, 0.0, NEVER)
-    for group in range(2):
-        own = slice(group * block, (group + 1) * block)
-        for index in range(PAIRS):
-            queries = pair(qkv_ref, own, 0, index)
-            keys = stack_heads(pair(qkv_ref, own, 1, index))
-            value_block = stack_heads(pair(qkv_ref, own, 2, index))
-            grad = pair(d_ref, own, 0, index)
-            both = dot(keys, queries, NT)
-            grad_both = dot(value_block, grad, NT)
-            chances, grads = [], []
-            for head in range(2):
-                cut = slice(head * block, (head + 1) * block)
-                scores = both[cut] + bias
-                powers = jnp.exp2((scores - jnp.max(scores, axis=0, keepdims=True)) * POWER)
-                share = powers * (1.0 / jnp.sum(powers, axis=0, keepdims=True))
-                grad_share = grad_both[cut]
-                mean = jnp.sum(share * grad_share, axis=0, keepdims=True)
-                chances.append(share.astype(LOW))
-                grads.append((share * (grad_share - mean)).astype(LOW))
-            dv = dot(jnp.concatenate(chances, axis=1), stack_heads(grad))
-            dk = dot(jnp.concatenate(grads, axis=1), stack_heads(queries)) * SCALE
-            dq = dot(jnp.concatenate(grads, axis=0), keys, TN) * SCALE
-            for part, item in enumerate((dq, dk, dv)):
+    for batch in time_batches(block):
+        keys = [stack_heads(pair(qkv_ref, own, 1, index)) for own, index in batch]
+        both = [dot(key, pair(qkv_ref, own, 0, index), NT) for key, (own, index) in zip(keys, batch)]
+        grad_both = [
+            dot(stack_heads(pair(qkv_ref, own, 2, index)), pair(d_ref, own, 0, index), NT)
+            for own, index in batch
+        ]
+        cuts = [slice(0, block), slice(block, 2 * block)]
+        chances = shares([item[cut] + bias for item in both for cut in cuts], 0)
+        grads = score_grads(chances, [item[cut] for item in grad_both for cut in cuts], 0)
+        chances = [item.astype(LOW) for item in chances]
+        results = []
+        for slot, (own, index) in enumerate(batch):
+            two = slice(2 * slot, 2 * slot + 2)
+            grad = stack_heads(pair(d_ref, own, 0, index))
+            queries = stack_heads(pair(qkv_ref, own, 0, index))
+            results.append(
+                (
+                    dot(jnp.concatenate(grads[two], axis=0), keys[slot], TN) * SCALE,
+                    dot(jnp.concatenate(grads[two], axis=1), queries) * SCALE,
+                    dot(jnp.concatenate(chances[two], axis=1), grad),
+                )
+            )
+        for items, (own, index) in zip(results, batch):
+            for part, item in enumerate(items):
                 start = (part * PAIRS + index) * LANES
                 gq_ref[own, start : start + LANES] = item.astype(LOW)
-    values = jnp.concatenate([ao_ref[...], ar_ref[...]], axis=1).reshape(rows, width)
+    values = jnp.concatenate([ao_ref[...].astype(WIDE), ar_ref[...].astype(WIDE)], axis=1).reshape(rows, width)
     gain = tgain_ref[...]
     _, normed, inverse = norm_rows(values, gain)
     back = dot(gq_ref[...], tproj_ref[...], NT)
-    result = gt_ref[...] + norm_back(back, normed, inverse, gain)
+    result = gt_ref[...].astype(WIDE) + norm_back(back, normed, inverse, gain)
     for frame in range(frames):
         low = result[frame * GROUP : (frame + 1) * GROUP]
         high = result[block + frame * GROUP : block + (frame + 1) * GROUP]
-        tile = jnp.concatenate([low, high], axis=0)
+        tile = jnp.concatenate([low, high], axis=0).astype(gso_ref.dtype)
         if frame < half:
             gso_ref[frame] = tile
         else:
@@ -311,45 +355,41 @@
     frames, padded, width = pad_ref.shape
     stride = order_ref.shape[1] // padded
     values = load_padded(x_ref, pad_ref)
-    grad_space = gs_ref[...].reshape(frames * padded, width)
+    grad_space = gs_ref[...].astype(WIDE).reshape(frames * padded, width)
     sb = grad_space.astype(LOW)
     sb_ref[...] = sb.reshape(frames, padded, width)
     d_ref[...] = dot(sb, out_ref[...], NT).astype(LOW).reshape(frames, padded, width)
     real = lax.broadcasted_iota(jnp.int32, (padded, padded), 0) < places
 
-    def one_frame(frame, carry):
-        for index in range(PAIRS):
-            queries = qkv_ref[frame, :, index * LANES : (index + 1) * LANES]
-            start = width + index * LANES
-            key_block = qkv_ref[frame, :, start : start + LANES]
-            start = 2 * width + index * LANES
-            value_block = qkv_ref[frame, :, start : start + LANES]
-            grad = d_ref[frame, :, index * LANES : (index + 1) * LANES]
-            keys = split_heads(key_block)
-            vals = split_heads(value_block)
-            outs = []
-            for head in range(2):
-                scores = jnp.where(real, dot(keys[head], queries, NT), NEVER)
-                powers = jnp.exp2((scores - jnp.max(scores, axis=0, keepdims=True)) * POWER)
-                share = powers * (1.0 / jnp.sum(powers, axis=0, keepdims=True))
-                grad_share = dot(vals[head], grad, NT)
-                mean = jnp.sum(share * grad_share, axis=0, keepdims=True)
-                ds = (share * (grad_share - mean)).astype(LOW)
-                outs.append(
-                    (
-                        dot(ds, key_block, TN) * SCALE,
-                        dot(ds, queries) * SCALE,
-                        dot(share.astype(LOW), grad),
-                    )
-                )
-            for part in range(3):
-                start = part * width + index * LANES
-                gq_ref[frame, :, start : start + LANES] = join_heads(
-                    outs[0][part], outs[1][part]
-                ).astype(LOW)
-        return carry
-
-    lax.fori_loop(0, frames, one_frame, 0)
+    def one_frame(frame):
+        for batch in batches(PAIRS, SPACE_BATCH):
+            part = lambda number, index: qkv_ref[
+                frame, :, number * width + index * LANES : number * width + (index + 1) * LANES
+            ]
+            grad = lambda index: d_ref[frame, :, index * LANES : (index + 1) * LANES]
+            heads = [(index, head) for index in batch for head in range(2)]
+            scores = [
+                jnp.where(real, dot(split_heads(part(1, index))[head], part(0, index), NT), NEVER)
+                for index, head in heads
+            ]
+            grad_shares = [
+                dot(split_heads(part(2, index))[head], grad(index), NT) for index, head in heads
+            ]
+            chances = shares(scores, 0)
+            grads = score_grads(chances, grad_shares, 0)
+            chances = [item.astype(LOW) for item in chances]
+            dq = [dot(ds, part(1, index), TN) * SCALE for ds, (index, _) in zip(grads, heads)]
+            dk = [dot(ds, part(0, index)) * SCALE for ds, (index, _) in zip(grads, heads)]
+            dv = [dot(p, grad(index)) for p, (index, _) in zip(chances, heads)]
+            for number, items in enumerate((dq, dk, dv)):
+                for slot, index in enumerate(batch):
+                    start = number * width + index * LANES
+                    gq_ref[frame, :, start : start + LANES] = join_heads(
+                        items[2 * slot], items[2 * slot + 1]
+                    ).astype(LOW)
+
+    for frame in range(frames):
+        one_frame(frame)
     gain = gain_row_ref[...]
     _, normed, inverse = norm_rows(values, gain)
     back = dot(gq_ref[:, :, : 2 * width].reshape(frames * padded, 2 * width), qk_ref[...], NT)
@@ -1080,12 +1120,17 @@
     return keep, flip(send, 1)
 
 
-def scatter_columns(keep, other):
+def column_parts(keep, other):
     shape = (4, 2) + keep.shape[1:]
     keep, other = keep.reshape(shape), other.reshape(shape)
     bit = bit_of(2)
     send = added(pick(keep, 1 - bit, 1), pick(other, 1 - bit, 1)).astype(LOW)
-    return added(pick(keep, bit, 1), pick(other, bit, 1)).astype(LOW), flip(send, 2)
+    return added(pick(keep, bit, 1), pick(other, bit, 1)).astype(LOW), send
+
+
+def scatter_columns(keep, other):
+    keep, send = column_parts(keep, other)
+    return keep, flip(send, 2)
 
 
 def scatter_lines(keep, other):
@@ -1100,12 +1145,6 @@
     total = total.reshape(2, total.shape[0] // 2, total.shape[1])
     place = lax.axis_index("frame")
     return pick(total, place, 0), swap_axis(pick(total, 1 - place, 0), "frame")
-
-
-def summed(values):
-    for mask in (1, 2, 4, 8):
-        values = values + flip(values, mask)
-    return values + swap_axis(values, "frame")
 
 
 def flat_rows(values):
@@ -1128,7 +1167,6 @@
     axes = ("clip", "frame")
     place = lax.axis_index("frame")
     owners = lax.axis_size(axes)
-    me = lax.axis_index(axes)
     share, width = space_out.shape
     blocks = down_proj.shape[0] // share
     core = bit_of(1).reshape(1)
@@ -1145,25 +1183,24 @@
     packed = jnp.concatenate(
         [time_proj, time_out, up_order.reshape(share, -1), down_order.reshape(share, -1)], axis=1
     )
-    first, second, by_place = tie(first, second, tokens.transpose(0, 2, 1, 3))
+    first, second, by_place, packed = tie(first, second, tokens.transpose(0, 2, 1, 3), packed)
+    packed = lax.all_gather(packed, axes, axis=0, tiled=True)
     half = by_place.shape[1] // 2
     send = pick(by_place, 1 - place, 0)
     rest_a = swap_axis(send[:half], "frame")
     first = collect_lines(first)
-    second, first, rest_a, send, packed = tie(second, first, rest_a, send, packed)
-    packed = lax.all_gather(packed, axes, axis=0, tiled=True)
+    second, first, rest_a, send = tie(second, first, rest_a, send)
     rest_b = swap_axis(send[half:], "frame")
     second = collect_lines(second)
     first = collect_half(first, 2, 1)
-    first, second = tie(first, second)
+    own, g_own = pick(tokens, place, 0), pick(cotangent, place, 0)
+    first, second, own, g_own = tie(first, second, own, g_own)
     second = collect_half(second, 2, 1)
     second, rest_b, g_send = tie(second, rest_b, cotangent.transpose(0, 2, 1, 3))
     g_rest = swap_axis(pick(g_send, 1 - place, 0), "frame")
     first = merged(collect_half(first, 1, 2))
     second = merged(collect_half(second, 1, 2))
     rest = jnp.concatenate([rest_a, rest_b], axis=0).transpose(1, 0, 2)
-    own = pick(tokens, place, 0)
-    g_own = pick(cotangent, place, 0)
     table = second[:, 2 * width : 2 * width + 3].astype(WIDE).T
     sgain, tgain, fgain = (table[index : index + 1] for index in range(3))
     in_o, qkv_o, o_o, after_o = space_forward(own, sgain, first, second)
@@ -1176,69 +1213,76 @@
     )
     mixed_other = swap_axis(mixed_r, "frame")
     scatter = lambda item: lax.psum_scatter(item, axes, scatter_dimension=0, tiled=True)
-    d_up = weight_gradient(([(in_f, gh)], 0, blocks, 1, 0))
-    d_up, act = tie(d_up, act)
-    d_up = scatter(d_up)
-    d_down = weight_gradient(([(act, gb)], 0, blocks, 0, 0))
-    d_down, g_time = tie(d_down, g_time)
+    d_feed = weight_gradient(
+        ([(in_f, gh)], 0, blocks, 1, 0), ([(act, gb)], blocks, 2 * blocks, 0, 0)
+    )
+    d_feed, g_time = tie(d_feed, g_time)
+    d_feed = scatter(d_feed)
     gq_t, tb, gs_o, gs_r, gain_t = time_backward(
         qkv_t, g_time, after_o, after_r, tgain, packed
     )
     d_time = split_gradient(
         core, owners, ([(in_t, gq_t)], 0, 3, 1, 0), ([(o_t, tb)], 3, 4, 1, 0)
     )
-    d_up, d_down, d_time, gs_r, mixed_other = tie(d_up, d_down, d_time, gs_r, mixed_other)
-    d_down = scatter(d_down)
+    d_time, gs_r, mixed_other = tie(d_time, gs_r, mixed_other)
     d_time = scatter_columns(*scatter_core(*d_time))
     gq_r, sb_r, gx_r, gain_sr = space_backward(spot, rest, gs_r, qkv_r, sgain, first, second, LOW)
-    grad_other = swap_axis(gx_r, "frame")
+    grad_a = swap_axis(gx_r[:half], "frame")
+    grad_b = swap_axis(gx_r[half:], "frame")
     d_time, gs_o, sb_r = tie(d_time, gs_o, sb_r)
     d_time = scatter_lines(*d_time)
     gq_o, sb_o, grad_tokens, gain_so = space_backward(spot, own, gs_o, qkv_o, sgain, first, second, WIDE)
-    d_down, d_time, gq_o, sb_o = tie(d_down, d_time, gq_o, sb_o)
+    d_time, gq_o, sb_o, grad_a = tie(d_time, gq_o, sb_o, grad_a)
+    gain_grads = jnp.stack(
+        [jnp.sum(item, axis=0) for item in (gain_so + gain_sr, gain_t, gain_f)], axis=1
+    )
+    gain_grads = jnp.pad(gain_grads, ((0, 0), (0, LANES - 3))).astype(LOW)
+    gain_grads = gain_grads.reshape(owners // 4, 2, 2 * share, LANES)
+    gain_grads = [pick(gain_grads, side, 1) for side in (core[0], 1 - core[0])]
     inputs = [(flat_rows(in_o), flat_rows(gq_o)), (flat_rows(in_r), flat_rows(gq_r))]
+    d_first = scatter_core(*split_gradient(core, owners, (inputs, 0, 3, 1, 0)))
+    first_keep, first_send = column_parts(*d_first)
+    first_keep, first_send, o_o = tie(first_keep, first_send, o_o)
+    d_first = first_keep, flip(first_send, 2)
     outputs = [(flat_rows(o_o), flat_rows(sb_o)), (flat_rows(o_r), flat_rows(sb_r))]
-    d_first = scatter_core(*split_gradient(core, owners, (inputs, 0, 2, 1, 0)))
-    d_second = split_gradient(core, owners, (inputs, 0, 1, 1, 2), (outputs, 1, 2, 1, 0))
-    gain_parts = tie(gain_so, gain_sr, gain_t, gain_f, d_first[0])
-    d_first = (gain_parts[4], d_first[1])
-    gain_grads = summed(
-        jnp.stack(
-            [
-                jnp.sum(item, axis=0)
-                for item in (gain_parts[0] + gain_parts[1], gain_parts[2], gain_parts[3])
-            ]
-        )
-    )
-    d_first, d_second = tie(d_first, d_second)
+    d_second = split_gradient(core, owners, (outputs, 0, 1, 1, 0))
+    d_second = [
+        jnp.concatenate([item, gain], axis=2) for item, gain in zip(d_second, gain_grads)
+    ]
     d_second = scatter_core(*d_second)
-    d_first = scatter_columns(*d_first)
+    d_first, d_second, d_time, mixed_other, grad_a, grad_b, d_feed = tie(
+        d_first, d_second, d_time, mixed_other, grad_a, grad_b, d_feed
+    )
+    d_first = scatter_lines(*d_first)
     d_second = scatter_columns(*d_second)
     d_time = scatter_frames(*d_time)
-    d_first = scatter_frames(*scatter_lines(*d_first))
+    d_feed = d_feed.astype(WIDE)
+    d_up, d_down = d_feed[:, : blocks * width], d_feed[:, blocks * width :]
+    d_up = d_up.reshape(share, blocks, owners, share).transpose(0, 2, 1, 3)
+    d_up = d_up.reshape(up_proj.shape)
+    d_down = d_down.reshape(share, blocks, width).transpose(1, 0, 2).reshape(down_proj.shape)
+    mixed = lax.dynamic_update_index_in_dim(mixed, mixed_other, 1 - place, 0)
+    for start, item in ((0, grad_a), (half, grad_b)):
+        grad_tokens = lax.dynamic_update_slice(
+            grad_tokens, item.astype(WIDE)[None], (1 - place, start, 0, 0)
+        )
+    d_first, mixed, grad_tokens, d_up, d_down = tie(d_first, mixed, grad_tokens, d_up, d_down)
+    d_first = scatter_frames(*d_first)
     d_second = scatter_frames(*scatter_lines(*d_second))
     d_first, d_second, d_time = (added(*item) for item in (d_first, d_second, d_time))
-    d_up, d_down = d_up.astype(WIDE), d_down.astype(WIDE)
-    d_up = d_up.reshape(share, blocks, owners, share).transpose(0, 2, 1, 3)
-    d_down = d_down.reshape(share, blocks, width).transpose(1, 0, 2)
-    gain_grads = lax.dynamic_slice_in_dim(gain_grads, me * share, share, axis=1)
-    mixed = lax.dynamic_update_index_in_dim(mixed, mixed_other, 1 - place, 0)
-    grad_tokens = lax.dynamic_update_index_in_dim(
-        grad_tokens, grad_other.astype(WIDE), 1 - place, 0
-    )
     mixed, grad_tokens = mixed.transpose(0, 2, 1, 3), grad_tokens.transpose(0, 2, 1, 3)
     return (
         mixed,
         grad_tokens,
-        gain_grads[0],
-        gain_grads[1],
-        gain_grads[2],
-        jnp.concatenate([d_first, d_second[:, :width]], axis=1),
-        d_second[:, width:],
+        d_second[:, width],
+        d_second[:, width + 1],
+        d_second[:, width + 2],
+        d_first,
+        d_second[:, :width],
         d_time[:, : 3 * width],
         d_time[:, 3 * width :],
-        d_up.reshape(up_proj.shape),
-        d_down.reshape(down_proj.shape),
+        d_up,
+        d_down,
     )
 
 

time: 711 us -> 633 us (0.89)
  Pallas kernels: 479 us -> 397 us
    pallas_call x2, Pallas kernels: 113 us -> 77.9 us  [space_backward(): pl.pallas_call(functools.partial(space_backward_kernel, places), grid_spe...]
    pallas_call x1, Pallas kernels: 76.7 us -> 54.5 us  [time_backward(): pl.pallas_call(time_backward_kernel, grid=(groups // 2,), in_specs=[by_ro...]
    pallas_call x2, Pallas kernels: 59.1 us -> 45 us  [space_forward(): pl.pallas_call(functools.partial(space_forward_kernel, places), grid=(fra...]
    ppermute x11, waiting for transfers between devices: 16.9 us -> 26.8 us  [swap_axis(): lax.ppermute(values, axis, [(index, size - 1 - index) for index in range(...]
    all_gather x1, waiting for transfers between devices: 8.44 us -> 0.01 us  [clip_local(): packed = lax.all_gather(packed, axes, axis=0, tiled=True)]
    ppermute x29 -> x25, starting transfers between devices: 30.9 us -> 27.7 us  [flip(): lax.ppermute(values, 'clip', [(index, index ^ mask) for index in range(si...]
    pallas_call x2 -> x1, Pallas kernels: 44 us -> 41.9 us  [weight_gradient(): pl.pallas_call(functools.partial(gradient_kernel, parts, tiles, None), gr...]
    ppermute x29 -> x25, waiting for transfers between devices: 59.4 us -> 60.9 us  [flip(): lax.ppermute(values, 'clip', [(index, index ^ mask) for index in range(si...]
  transfers between devices with their start and end apart: 43 -> 38, of which waited for: 17 -> 14; matrix products, arithmetic and copies ran while one was open for 10% -> 12% of each run, Pallas kernels for 47% -> 37%
where the time goes in v3:
time: 633 us; the launch traced here: 625 us
  Pallas kernels  397 us (63%)
  waiting for transfers between devices  87.7 us (14%)
  local copies, waits for them, and re-layouts  50.6 us (8%)
  starting transfers between devices  41.6 us (7%)
  other arithmetic  33.5 us (5%)
  between operations  15 us (2%)
    pallas_call x1, Pallas kernels, middle(): pl.pallas_call(functools.partial(middle_kernel, places), grid_spec=pltpu....  124 us
    pallas_call x2, Pallas kernels, space_backward(): pl.pallas_call(functools.partial(space_backward_kernel, places), grid_spe...  77.9 us
    ppermute x25, waiting for transfers between devices, flip(): lax.ppermute(values, 'clip', [(index, index ^ mask) for index in range(si...  60.9 us
    pallas_call x1, Pallas kernels, time_backward(): pl.pallas_call(time_backward_kernel, grid=(groups // 2,), in_specs=[by_ro...  54.5 us
    pallas_call x3, Pallas kernels, split_gradient(): pl.pallas_call(functools.partial(gradient_kernel, parts, tiles), grid_spe...  53.5 us
    pallas_call x2, Pallas kernels, space_forward(): pl.pallas_call(functools.partial(space_forward_kernel, places), grid=(fra...  45 us
    pallas_call x1, Pallas kernels, weight_gradient(): pl.pallas_call(functools.partial(gradient_kernel, parts, tiles, None), gr...  41.9 us
    ppermute x25, starting transfers between devices, flip(): lax.ppermute(values, 'clip', [(index, index ^ mask) for index in range(si...  27.7 us
  transfers between devices with their start and end apart: 38, of which 14 were waited for; matrix products, arithmetic and copies ran while one was open for 12% of the time, Pallas kernels for 37%

profile of v3, /device:TPU:0, one launch (start us, length us, event | category | flops | bytes accessed | tf_op | source)
XLA Modules:
  0.0 625.2 jit_solution(12802493740532787028)
XLA Ops:
  9.6 3.0 collective-permute-start.1
  14.6 2.1 reshape.152
  19.1 1.4 dynamic-slice_bitcast_fusion.2
  20.5 2.1 collective-permute-start.5
  22.6 3.6 collective-permute-start.4
  26.9 1.9 dynamic-slice_bitcast_fusion.1
  28.8 2.3 collective-permute-done.4
  31.1 14.8 %collective-permute-done.3 = bf16[2,24,1536]{2,1,0:T(8,128)(2,1)S(1)} collective-permute-done((bf16[2,24,1536]{2,1,0:T(8,128)(2,1)S(1)}, bf16[2,24,1536]{2,1,0:T(8,128)(2,1)S(1)}, u32[]{:S(2)}, u32[]{:S(2)}) %collective-permute-start.3) | collective-permute-done | bytes 147488 | tf_op jit(solution)/shard_map/ppermute | solution.py:1073
  46.1 5.6 collective-permute-done.5
  51.7 3.8 collective-permute-start.9
  56.1 2.7 constant_dynamic-slice_fusion
  58.8 1.9 copy.110
  60.7 2.0 copy.111
  62.8 1.8 collective-permute-start.6
  64.6 1.5 collective-permute-start.11
  66.1 17.0 %collective-permute-done.8 = bf16[2,24,1664]{2,1,0:T(8,128)(2,1)S(1)} collective-permute-done((bf16[2,24,1664]{2,1,0:T(8,128)(2,1)S(1)}, bf16[2,24,1664]{2,1,0:T(8,128)(2,1)S(1)}, u32[]{:S(2)}, u32[]{:S(2)}) %collective-permute-start.8) | collective-permute-done | bytes 159776 | tf_op jit(solution)/shard_map/ppermute | solution.py:1073
  83.5 1.6 collective-permute-start.10
  85.1 13.7 %collective-permute-done.10 = bf16[4,2,24,1664]{3,2,1,0:T(8,128)(2,1)S(1)} collective-permute-done((bf16[4,2,24,1664]{3,2,1,0:T(8,128)(2,1)S(1)}, bf16[4,2,24,1664]{3,2,1,0:T(8,128)(2,1)S(1)}, u32[]{:S(2)}, u32[]{:S(2)}) %collective-permute-start.10) | collective-permute-done | bytes 639008 | tf_op jit(solution)/shard_map/ppermute | solution.py:1073
  99.1 1.7 dynamic-slice_bitcast_fusion
  101.9 1.6 copy.79
  103.8 1.8 maximum_bitcast_fusion.x_ref
  105.6 2.0 maximum_select_fusion.1
  107.6 1.6 copy.77
  109.2 2.3 maximum_select_fusion
  111.8 1.3 fusion.14
  113.1 1.7 copy.84.fgain_ref
  116.3 22.5 %space_forward.2 = (bf16[8,208,768]{2,1,0:T(8,128)(2,1)}, bf16[8,208,2304]{2,1,0:T(8,128)(2,1)}, bf16[8,208,768]{2,1,0:T(8,128)(2,1)}, f32[26,8,8,768]{3,2,1,0:T(8,128)}) custom-call(bf16[8,196,768]{2,1,0:T(8,128)(2,1)} %bitcast.180, f32[1,768]{1,0:T(1,128)} %copy.78.gain_ref.gain_row_ref, bf16[768,1536]{1,0:T(8,128)(2,1)} %bitcast.176, ...), custom_call_target="tpu_custom_call" | custom-call | flops 1663041536 | bytes 4202496 | tf_op jit(solution)/shard_map/space_forward/pallas_call | solution.py:466
  138.8 22.5 %space_forward.3 = (bf16[8,208,768]{2,1,0:T(8,128)(2,1)}, bf16[8,208,2304]{2,1,0:T(8,128)(2,1)}, bf16[8,208,768]{2,1,0:T(8,128)(2,1)}, f32[26,8,8,768]{3,2,1,0:T(8,128)}) custom-call(bf16[8,196,768]{2,1,0:T(8,128)(2,1)} %maximum_bitcast_fusion.x_ref, f32[1,768]{1,0:T(1,128)} %copy.78.gain_ref.gain_row_ref, bf16[768,1536]{1,0:T(8,128)(2,1)} %bitcast.177, ...), custom_call_target="tpu_custom_call" | custom-call | flops 1663041536 | bytes 4202496 | tf_op jit(solution)/shard_map/space_forward/pallas_call | solution.py:466
  161.3 10.3 %collective-permute-done.14 = bf16[196,8,768]{2,1,0:T(8,128)(2,1)} collective-permute-done((bf16[196,8,768]{2,1,0:T(8,128)(2,1)}, bf16[196,8,768]{2,1,0:T(8,128)(2,1)}, u32[]{:S(2)}, u32[]{:S(2)}) %collective-permute-start.14) | collective-permute-done | bytes 2408480 | tf_op jit(solution)/shard_map/ppermute | solution.py:1068
  171.6 3.6 copy.109
  175.3 124.0 %middle.1 = (bf16[3328,2304]{1,0:T(8,128)(2,1)}, bf16[3328,768]{1,0:T(8,128)(2,1)}, bf16[3328,768]{1,0:T(8,128)(2,1)}, bf16[3328,768]{1,0:T(8,128)(2,1)}, bf16[3...) custom-call(s32[1]{0:T(128)} %bitcast.37.place_ref, ...), custom_call_target="tpu_custom_call" | custom-call | flops 13522436096 | bytes 18198528 | tf_op jit(solution)/shard_map/middle/pallas_call | solution.py:515
  299.3 41.9 %weight_gradient.1 = bf16[768,6144]{1,0:T(8,128)(2,1)} custom-call(bf16[3328,768]{1,0:T(8,128)(2,1)} %get-tuple-element.132.refs_0_, bf16[3328,3072]{1,0:T(8,128)(2,1)} %get-tuple-element.133.refs_1_, bf16[3328,3072]{1,0:T(8,128)(2,1)} %get-tuple-element.134.refs_2_, bf16[3328,768]{1,0:T(8,128)(2,1)} %get-tuple-element.135.refs_3_), custom_call_target="tpu_custom_call" | custom-call | flops 5234491392 | bytes 10092544 | tf_op jit(solution)/shard_map/weight_gradient/pallas_call | solution.py:695
  341.2 1.7 copy-done.20
  343.2 54.5 %time_backward.1 = (bf16[3328,2304]{1,0:T(8,128)(2,1)}, bf16[3328,768]{1,0:T(8,128)(2,1)}, f32[8,208,768]{2,1,0:T(8,128)}, f32[8,208,768]{2,1,0:T(8,128)}, f32[8,768]{1,0:T(8,128)}) custom-call(bf16[3328,2304]{1,0:T(8,128)(2,1)} %get-tuple-element.131.qkv_ref, f32[3328,768]{1,0:T(8,128)} %get-tuple-element.137.gt_ref, ...), custom_call_target="tpu_custom_call" | custom-call | flops 3707764736 | bytes 11079680 | tf_op jit(solution)/shard_map/time_backward/pallas_call | solution.py:567
  397.7 25.1 %split_gradient.3 = (bf16[8,48,3072]{2,1,0:T(8,128)(2,1)}, bf16[8,48,3072]{2,1,0:T(8,128)(2,1)}) custom-call(s32[1]{0:T(128)} %bitcast.core_ref, bf16[3328,768]{1,0:T(8,128)(2,1)} %get-tuple-element.130.refs_0_, bf16[3328,2304]{1,0:T(8,128)(2,1)} %get-tuple-element.138.refs_1_, bf16[3328,768]{1,0:T(8,128)(2,1)} %get-tuple-element.139.refs_2_, ...), custom_call_target="tpu_custom_call" | custom-call | flops 2617245696 | bytes 5898240 | tf_op jit(solution)/shard_map/split_gradient/pallas_call | solution.py:712
  422.9 4.7 collective-permute-done.16
  427.6 2.7 fusion.1
  430.3 1.6 collective-permute-start.17
  431.9 38.6 %space_backward.2 = (bf16[8,208,2304]{2,1,0:T(8,128)(2,1)}, bf16[8,208,768]{2,1,0:T(8,128)(2,1)}, bf16[196,8,768]{2,1,0:T(8,128)(2,1)}, f32[8,768]{1,0:T(8,128)}) custom-call(s32[1]{0:T(128)} %bitcast.37.place_ref, bf16[8,196,768]{2,1,0:T(8,128)(2,1)} %maximum_bitcast_fusion.x_ref, f32[8,208,768]{2,1,0:T(8,128)} %get-tuple-element.148.gs_ref, ...), custom_call_target="tpu_custom_call" | custom-call | flops 2194669568 | bytes 4640768 | tf_op jit(solution)/shard_map/space_backward/pallas_call | solution.py:600
  470.5 3.7 fusion.13
  474.2 1.5 collective-permute-start.21
  476.7 3.4 collective-permute-start.20
  481.2 39.3 %space_backward.3 = (bf16[8,208,2304]{2,1,0:T(8,128)(2,1)}, bf16[8,208,768]{2,1,0:T(8,128)(2,1)}, f32[2,196,8,768]{3,2,1,0:T(8,128)}, f32[8,768]{1,0:T(8,128)}) custom-call(s32[1]{0:T(128)} %bitcast.37.place_ref, bf16[8,196,768]{2,1,0:T(8,128)(2,1)} %bitcast.181, f32[8,208,768]{2,1,0:T(8,128)} %get-tuple-element.153.gs_ref, ...), custom_call_target="tpu_custom_call" | custom-call | flops 2194669568 | bytes 5844992 | tf_op jit(solution)/shard_map/space_backward/pallas_call | solution.py:600
  521.4 18.8 %split_gradient.4 = (bf16[8,48,2304]{2,1,0:T(8,128)(2,1)}, bf16[8,48,2304]{2,1,0:T(8,128)(2,1)}) custom-call(s32[1]{0:T(128)} %bitcast.core_ref, bf16[1664,768]{1,0:T(8,128)(2,1)} %bitcast.199, bf16[1664,2304]{1,0:T(8,128)(2,1)} %bitcast.185, bf16[1664,768]{1,0:T(8,128)(2,1)} %bitcast.200, bf16[1664,2304]{1,0:T(8,128)(2,1)} %bitcast.184), custom_call_target="tpu_custom_call" | custom-call | flops 1962934272 | bytes 3997696 | tf_op jit(solution)/shard_map/split_gradient/pallas_call | solution.py:712
  541.3 3.0 collective-permute-done.22
  544.3 2.6 fusion.3
  546.9 1.4 fusion.2
  548.8 9.5 %split_gradient.5 = (bf16[8,48,768]{2,1,0:T(8,128)(2,1)}, bf16[8,48,768]{2,1,0:T(8,128)(2,1)}) custom-call(s32[1]{0:T(128)} %bitcast.core_ref, bf16[1664,768]{1,0:T(8,128)(2,1)} %bitcast.197, bf16[1664,768]{1,0:T(8,128)(2,1)} %bitcast.202, bf16[1664,768]{1,0:T(8,128)(2,1)} %bitcast.198, bf16[1664,768]{1,0:T(8,128)(2,1)} %bitcast.201), custom_call_target="tpu_custom_call" | custom-call | flops 654311424 | bytes 1900544 | tf_op jit(solution)/shard_map/split_gradient/pallas_call | solution.py:712
  560.6 9.1 %collective-permute-done.25 = bf16[98,8,768]{2,1,0:T(8,128)(2,1)} collective-permute-done((bf16[98,8,768]{2,1,0:T(8,128)(2,1)}, bf16[98,8,768]{2,1,0:T(8,128)(2,1)}, u32[]{:S(2)}, u32[]{:S(2)}) %collective-permute-start.25) | collective-permute-done | bytes 1204256 | tf_op jit(solution)/shard_map/ppermute | solution.py:1068
  571.2 1.4 add_convert_fusion.3
  573.5 3.3 collective-permute-start.28
  577.9 1.3 add_convert_fusion.8
  580.4 1.8 fusion.6
  582.5 2.9 convert_dynamic-update-slice_fusion.1
  585.4 3.3 bitcast_dynamic-update-slice_fusion
  588.6 2.9 convert_dynamic-update-slice_fusion
  594.8 2.6 reshape.171
  599.7 1.3 add_convert_fusion.9
  603.4 2.4 collective-permute-start.32
  606.3 1.6 collective-permute-start.34
  608.2 1.8 collective-permute-done.32
  610.0 2.6 collective-permute-done.31
  612.7 1.6 collective-permute-start.33
  615.0 1.8 collective-permute-done.33
  (156 shorter events, 35.0 us)
Async XLA Ops:
  7.2 11.0 %copy-start.15 = (bf16[24,768]{1,0:T(8,128)(2,1)S(1)}, bf16[24,768]{1,0:T(8,128)(2,1)}, u32[]{:S(2)}) copy-start(bf16[24,768]{1,0:T(8,128)(2,1)} %param.19) | copy-start | bytes 110596
  7.2 11.0 %copy-start.14 = (bf16[24,2304]{1,0:T(8,128)(2,1)S(1)}, bf16[24,2304]{1,0:T(8,128)(2,1)}, u32[]{:S(2)}) copy-start(bf16[24,2304]{1,0:T(8,128)(2,1)} %param.18) | copy-start | bytes 331780
  7.2 168.1 %all-gather.2.cloned.1.call-start = ((), (), s32[]{:S(2)}) async-start(), calls=%async_computation.1 | async-start | bytes 14598144 | tf_op jit(solution)/shard_map/all_gather | solution.py:1187
  9.6 9.4 %collective-permute-start.1 = (bf16[24,1664]{1,0:T(8,128)(2,1)S(1)}, bf16[24,1664]{1,0:T(8,128)(2,1)S(1)}, u32[]{:S(2)}, u32[]{:S(2)}) collective-permute-start(bf16[24,1664]{1,0:T(8,128)(2,1)S(1)} %get-tuple-element.239), channel_id=1, source_target_pairs={{0,1},{1,0},{2,3},{3,2},{4,5},{5,4},{6,7},{7,6},{8,9},{9,8},{10,11... | collective-permute-start | bytes 239624 | tf_op jit(solution)/shard_map/ppermute | solution.py:1068
  13.5 5.4 collective-permute-start
  19.1 552.1 %reduce-scatter.2.cloned.1.call-start = ((), (), s32[]{:S(2)}) async-start(), calls=%async_computation.2 | async-start | bytes 9732096 | tf_op jit(solution)/shard_map/reduce_scatter | solution.py:1215
  20.5 31.2 %collective-permute-start.5 = (bf16[98,8,768]{2,1,0:T(8,128)(2,1)S(1)}, bf16[98,8,768]{2,1,0:T(8,128)(2,1)S(1)}, u32[]{:S(2)}, u32[]{:S(2)}) collective-permute-start(bf16[98,8,768]{2,1,0:T(8,128)(2,1)S(1)} %dynamic-slice_bitcast_fusion.2), channel_id=1, source_target_pairs={{0,1},{1,0},{2,3},{3,2},{4,5},{5,4},{6,7},{7,6},{8,9},{9,8},{10,11... | collective-permute-start | bytes 3612680 | tf_op jit(solution)/shard_map/ppermute | solution.py:1068
  22.6 8.6 %collective-permute-start.4 = (bf16[2,24,1536]{2,1,0:T(8,128)(2,1)S(1)}, bf16[2,24,1536]{2,1,0:T(8,128)(2,1)S(1)}, u32[]{:S(2)}, u32[]{:S(2)}) collective-permute-start(bf16[2,24,1536]{2,1,0:T(8,128)(2,1)S(1)} %maximum_select_fusion.5), channel_id=1, source_target_pairs={{0,24},{2,26},{4,28},{6,30},{8,16},{10,18},{12,20},{14,22},{16,8},... | collective-permute-start | bytes 442376 | tf_op jit(solution)/shard_map/ppermute | solution.py:1073
  26.2 19.8 %collective-permute-start.3 = (bf16[2,24,1536]{2,1,0:T(8,128)(2,1)S(1)}, bf16[2,24,1536]{2,1,0:T(8,128)(2,1)S(1)}, u32[]{:S(2)}, u32[]{:S(2)}) collective-permute-start(bf16[2,24,1536]{2,1,0:T(8,128)(2,1)S(1)} %maximum_select_fusion.5), channel_id=1, source_target_pairs={{0,16},{2,18},{4,20},{6,22},{8,24},{10,26},{12,28},{14,30},{16,0},... | collective-permute-start | bytes 442376 | tf_op jit(solution)/shard_map/ppermute | solution.py:1073
  26.2 19.8 %collective-permute-start.2 = (bf16[2,24,1536]{2,1,0:T(8,128)(2,1)S(1)}, bf16[2,24,1536]{2,1,0:T(8,128)(2,1)S(1)}, u32[]{:S(2)}, u32[]{:S(2)}) collective-permute-start(bf16[2,24,1536]{2,1,0:T(8,128)(2,1)S(1)} %maximum_select_fusion.5), channel_id=1, source_target_pairs={{0,8},{2,10},{4,12},{6,14},{8,0},{10,2},{12,4},{14,6},{16,24},{18,... | collective-permute-start | bytes 442376 | tf_op jit(solution)/shard_map/ppermute | solution.py:1073
  51.7 7.1 %copy-start.5 = (bf16[98,8,768]{2,1,0:T(8,128)(2,1)}, bf16[98,8,768]{2,1,0:T(8,128)(2,1)S(1)}, u32[]{:S(2)}) copy-start(bf16[98,8,768]{2,1,0:T(8,128)(2,1)S(1)} %collective-permute-done.5) | copy-start | bytes 3612676
  51.7 14.4 %collective-permute-start.9 = (bf16[2,24,1664]{2,1,0:T(8,128)(2,1)S(1)}, bf16[2,24,1664]{2,1,0:T(8,128)(2,1)S(1)}, u32[]{:S(2)}, u32[]{:S(2)}) collective-permute-start(bf16[2,24,1664]{2,1,0:T(8,128)(2,1)S(1)} %maximum_select_fusion.4), channel_id=1, source_target_pairs={{0,24},{2,26},{4,28},{6,30},{8,16},{10,18},{12,20},{14,22},{16,8},... | collective-permute-start | bytes 479240 | tf_op jit(solution)/shard_map/ppermute | solution.py:1073
  55.5 27.6 %collective-permute-start.8 = (bf16[2,24,1664]{2,1,0:T(8,128)(2,1)S(1)}, bf16[2,24,1664]{2,1,0:T(8,128)(2,1)S(1)}, u32[]{:S(2)}, u32[]{:S(2)}) collective-permute-start(bf16[2,24,1664]{2,1,0:T(8,128)(2,1)S(1)} %maximum_select_fusion.4), channel_id=1, source_target_pairs={{0,16},{2,18},{4,20},{6,22},{8,24},{10,26},{12,28},{14,30},{16,0},... | collective-permute-start | bytes 479240 | tf_op jit(solution)/shard_map/ppermute | solution.py:1073
  55.5 27.6 %collective-permute-start.7 = (bf16[2,24,1664]{2,1,0:T(8,128)(2,1)S(1)}, bf16[2,24,1664]{2,1,0:T(8,128)(2,1)S(1)}, u32[]{:S(2)}, u32[]{:S(2)}) collective-permute-start(bf16[2,24,1664]{2,1,0:T(8,128)(2,1)S(1)} %maximum_select_fusion.4), channel_id=1, source_target_pairs={{0,8},{2,10},{4,12},{6,14},{8,0},{10,2},{12,4},{14,6},{16,24},{18,... | collective-permute-start | bytes 479240 | tf_op jit(solution)/shard_map/ppermute | solution.py:1073
  58.8 40.3 %slice-start = ((s8[4816896]{0:T(1024)(128)(4,1)}), s8[4194304]{0:T(1024)(128)(4,1)S(1)}, s32[]{:S(2)}) async-start(s8[4816896]{0:T(1024)(128)(4,1)} %bitcast.190), calls=%async_computation.3 | async-start | bytes 8388608
  62.7 36.4 %slice-start.1 = ((s8[4816896]{0:T(1024)(128)(4,1)}), s8[622592]{0:T(1024)(128)(4,1)S(1)}, s32[]{:S(2)}) async-start(s8[4816896]{0:T(1024)(128)(4,1)} %bitcast.190), calls=%async_computation.4 | async-start | bytes 1245184
  62.8 20.5 %collective-permute-start.6 = (bf16[4,2,24,1536]{3,2,1,0:T(8,128)(2,1)S(1)}, bf16[4,2,24,1536]{3,2,1,0:T(8,128)(2,1)S(1)}, u32[]{:S(2)}, u32[]{:S(2)}) collective-permute-start(bf16[4,2,24,1536]{3,2,1,0:T(8,128)(2,1)S(1)} %pad_maximum_fusion.3), channel_id=1, source_target_pairs={{0,4},{2,6},{4,0},{6,2},{8,12},{10,14},{12,8},{14,10},{16,20},{18,... | collective-permute-start | bytes 1769480 | tf_op jit(solution)/shard_map/ppermute | solution.py:1073
  64.6 34.4 %collective-permute-start.11 = (bf16[98,8,768]{2,1,0:T(8,128)(2,1)S(1)}, bf16[98,8,768]{2,1,0:T(8,128)(2,1)S(1)}, u32[]{:S(2)}, u32[]{:S(2)}) collective-permute-start(bf16[98,8,768]{2,1,0:T(8,128)(2,1)S(1)} %slice.61), channel_id=1, source_target_pairs={{0,1},{1,0},{2,3},{3,2},{4,5},{5,4},{6,7},{7,6},{8,9},{9,8},{10,11... | collective-permute-start | bytes 3612680 | tf_op jit(solution)/shard_map/ppermute | solution.py:1068
  83.5 15.2 %collective-permute-start.10 = (bf16[4,2,24,1664]{3,2,1,0:T(8,128)(2,1)S(1)}, bf16[4,2,24,1664]{3,2,1,0:T(8,128)(2,1)S(1)}, u32[]{:S(2)}, u32[]{:S(2)}) collective-permute-start(bf16[4,2,24,1664]{3,2,1,0:T(8,128)(2,1)S(1)} %pad_maximum_fusion.2), channel_id=1, source_target_pairs={{0,4},{2,6},{4,0},{6,2},{8,12},{10,14},{12,8},{14,10},{16,20},{18,... | collective-permute-start | bytes 1916936 | tf_op jit(solution)/shard_map/ppermute | solution.py:1073
  85.1 20.5 %collective-permute-start.13 = (bf16[4,2,2,24,1536]{4,3,2,0,1:T(8,128)(2,1)S(1)}, bf16[4,2,2,24,1536]{4,3,2,0,1:T(8,128)(2,1)}, u32[]{:S(2)}, u32[]{:S(2)}) collective-permute-start(bf16[4,2,2,24,1536]{4,3,2,0,1:T(8,128)(2,1)S(1)} %maximum_select_fusion.3), channel_id=1, source_target_pairs={{0,2},{2,0},{4,6},{6,4},{8,10},{10,8},{12,14},{14,12},{16,18},{18,... | collective-permute-start | bytes 3538952 | tf_op jit(solution)/shard_map/ppermute | solution.py:1073
  99.0 1.8 copy-start.6
  99.0 10.2 %collective-permute-start.12 = (bf16[4,2,2,24,1664]{4,3,2,0,1:T(8,128)(2,1)S(1)}, bf16[4,2,2,24,1664]{4,3,2,0,1:T(8,128)(2,1)}, u32[]{:S(2)}, u32[]{:S(2)}) collective-permute-start(bf16[4,2,2,24,1664]{4,3,2,0,1:T(8,128)(2,1)S(1)} %maximum_select_fusion.2), channel_id=1, source_target_pairs={{0,2},{2,0},{4,6},{6,4},{8,10},{10,8},{12,14},{14,12},{16,18},{18,... | collective-permute-start | bytes 3833864 | tf_op jit(solution)/shard_map/ppermute | solution.py:1073
  100.8 70.8 %collective-permute-start.14 = (bf16[196,8,768]{2,1,0:T(8,128)(2,1)}, bf16[196,8,768]{2,1,0:T(8,128)(2,1)}, u32[]{:S(2)}, u32[]{:S(2)}) collective-permute-start(bf16[196,8,768]{2,1,0:T(8,128)(2,1)} %dynamic-slice_bitcast_fusion), channel_id=1, source_target_pairs={{0,1},{1,0},{2,3},{3,2},{4,5},{5,4},{6,7},{7,6},{8,9},{9,8},{10,11... | collective-permute-start | bytes 7225352 | tf_op jit(solution)/shard_map/ppermute | solution.py:1068
  101.9 1.7 copy-start.7
  111.8 4.5 copy-start
  341.2 1.7 copy-start.20
  342.8 80.0 %collective-permute-start.15 = (bf16[196,8,768]{2,1,0:T(8,128)(2,1)S(1)}, bf16[196,8,768]{2,1,0:T(8,128)(2,1)}, u32[]{:S(2)}, u32[]{:S(2)}) collective-permute-start(bf16[196,8,768]{2,1,0:T(8,128)(2,1)S(1)} %copy-done.20), channel_id=1, source_target_pairs={{0,1},{1,0},{2,3},{3,2},{4,5},{5,4},{6,7},{7,6},{8,9},{9,8},{10,11... | collective-permute-start | bytes 7225352 | tf_op jit(solution)/shard_map/ppermute | solution.py:1068
  422.8 4.7 collective-permute-start.16
  430.3 45.9 %collective-permute-start.17 = (bf16[4,48,3072]{2,1,0:T(8,128)(2,1)}, bf16[4,48,3072]{2,1,0:T(8,128)(2,1)S(1)}, u32[]{:S(2)}, u32[]{:S(2)}) collective-permute-start(bf16[4,48,3072]{2,1,0:T(8,128)(2,1)} %fusion.1), channel_id=1, source_target_pairs={{0,4},{2,6},{4,0},{6,2},{8,12},{10,14},{12,8},{14,10},{16,20},{18,... | collective-permute-start | bytes 3538952 | tf_op jit(solution)/shard_map/ppermute | solution.py:1073
  470.5 5.2 copy-start.3
  474.2 46.2 %collective-permute-start.21 = (bf16[98,8,768]{2,1,0:T(8,128)(2,1)}, bf16[98,8,768]{2,1,0:T(8,128)(2,1)}, u32[]{:S(2)}, u32[]{:S(2)}) collective-permute-start(bf16[98,8,768]{2,1,0:T(8,128)(2,1)} %get-tuple-element.209), channel_id=1, source_target_pairs={{0,1},{1,0},{2,3},{3,2},{4,5},{5,4},{6,7},{7,6},{8,9},{9,8},{10,11... | collective-permute-start | bytes 3612680 | tf_op jit(solution)/shard_map/ppermute | solution.py:1068
  476.7 43.8 %collective-permute-start.20 = (bf16[48,3072]{1,0:T(8,128)(2,1)S(1)}, bf16[48,3072]{1,0:T(8,128)(2,1)S(1)}, u32[]{:S(2)}, u32[]{:S(2)}) collective-permute-start(bf16[48,3072]{1,0:T(8,128)(2,1)S(1)} %get-tuple-element.210), channel_id=1, source_target_pairs={{0,24},{2,26},{4,28},{6,30},{8,16},{10,18},{12,20},{14,22},{16,8},... | collective-permute-start | bytes 884744 | tf_op jit(solution)/shard_map/ppermute | solution.py:1073
  480.1 40.4 %collective-permute-start.19 = (bf16[48,3072]{1,0:T(8,128)(2,1)S(1)}, bf16[48,3072]{1,0:T(8,128)(2,1)S(1)}, u32[]{:S(2)}, u32[]{:S(2)}) collective-permute-start(bf16[48,3072]{1,0:T(8,128)(2,1)S(1)} %get-tuple-element.211), channel_id=1, source_target_pairs={{0,16},{2,18},{4,20},{6,22},{8,24},{10,26},{12,28},{14,30},{16,0},... | collective-permute-start | bytes 884744 | tf_op jit(solution)/shard_map/ppermute | solution.py:1073
  480.1 40.4 %collective-permute-start.18 = (bf16[48,3072]{1,0:T(8,128)(2,1)S(1)}, bf16[48,3072]{1,0:T(8,128)(2,1)S(1)}, u32[]{:S(2)}, u32[]{:S(2)}) collective-permute-start(bf16[48,3072]{1,0:T(8,128)(2,1)S(1)} %get-tuple-element.212), channel_id=1, source_target_pairs={{0,8},{2,10},{4,12},{6,14},{8,0},{10,2},{12,4},{14,6},{16,24},{18,... | collective-permute-start | bytes 884744 | tf_op jit(solution)/shard_map/ppermute | solution.py:1073
  520.5 19.7 %copy-start.11 = (bf16[48,3072]{1,0:T(8,128)(2,1)}, bf16[48,3072]{1,0:T(8,128)(2,1)S(1)}, u32[]{:S(2)}) copy-start(bf16[48,3072]{1,0:T(8,128)(2,1)S(1)} %collective-permute-done.20) | copy-start | bytes 884740
  520.5 0.8 copy-start.12
  520.5 0.9 copy-start.13
  521.4 19.0 %copy-start.18 = (f32[8,768]{1,0:T(8,128)S(1)}, f32[8,768]{1,0:T(8,128)}, u32[]{:S(2)}) copy-start(f32[8,768]{1,0:T(8,128)} %get-tuple-element.174) | copy-start | bytes 73732
  521.4 19.0 %copy-start.19 = (f32[8,768]{1,0:T(8,128)S(1)}, f32[8,768]{1,0:T(8,128)}, u32[]{:S(2)}) copy-start(f32[8,768]{1,0:T(8,128)} %get-tuple-element.173) | copy-start | bytes 73732
  521.4 19.6 %copy-start.16 = (f32[8,768]{1,0:T(8,128)S(1)}, f32[8,768]{1,0:T(8,128)}, u32[]{:S(2)}) copy-start(f32[8,768]{1,0:T(8,128)} %get-tuple-element.172) | copy-start | bytes 73732
  521.4 19.6 %copy-start.17 = (f32[8,768]{1,0:T(8,128)S(1)}, f32[8,768]{1,0:T(8,128)}, u32[]{:S(2)}) copy-start(f32[8,768]{1,0:T(8,128)} %get-tuple-element.171) | copy-start | bytes 73732
  540.2 6.7 %copy-start.4 = (bf16[8,48,2304]{2,1,0:T(8,128)(2,1)S(1)}, bf16[8,48,2304]{2,1,0:T(8,128)(2,1)}, u32[]{:S(2)}) copy-start(bf16[8,48,2304]{2,1,0:T(8,128)(2,1)} %get-tuple-element.161) | copy-start | bytes 5308420
  540.2 4.1 collective-permute-start.22
  540.4 29.3 %collective-permute-start.25 = (bf16[98,8,768]{2,1,0:T(8,128)(2,1)}, bf16[98,8,768]{2,1,0:T(8,128)(2,1)}, u32[]{:S(2)}, u32[]{:S(2)}) collective-permute-start(bf16[98,8,768]{2,1,0:T(8,128)(2,1)} %get-tuple-element.208), channel_id=1, source_target_pairs={{0,1},{1,0},{2,3},{3,2},{4,5},{5,4},{6,7},{7,6},{8,9},{9,8},{10,11... | collective-permute-start | bytes 3612680 | tf_op jit(solution)/shard_map/ppermute | solution.py:1068
  548.3 22.0 %collective-permute-start.23 = (bf16[4,48,2304]{2,1,0:T(8,128)(2,1)}, bf16[4,48,2304]{2,1,0:T(8,128)(2,1)S(1)}, u32[]{:S(2)}, u32[]{:S(2)}) collective-permute-start(bf16[4,48,2304]{2,1,0:T(8,128)(2,1)} %fusion.3), channel_id=1, source_target_pairs={{0,4},{2,6},{4,0},{6,2},{8,12},{10,14},{12,8},{14,10},{16,20},{18,... | collective-permute-start | bytes 2654216 | tf_op jit(solution)/shard_map/ppermute | solution.py:1073
  559.4 10.3 %collective-permute-start.24 = (bf16[8,48,896]{2,1,0:T(8,128)(2,1)S(1)}, bf16[8,48,896]{2,1,0:T(8,128)(2,1)}, u32[]{:S(2)}, u32[]{:S(2)}) collective-permute-start(bf16[8,48,896]{2,1,0:T(8,128)(2,1)S(1)} %pad_maximum_fusion.1), channel_id=1, source_target_pairs={{0,2},{2,0},{4,6},{6,4},{8,10},{10,8},{12,14},{14,12},{16,18},{18,... | collective-permute-start | bytes 2064392 | tf_op jit(solution)/shard_map/ppermute | solution.py:1073
  560.6 19.8 %copy-start.1 = (bf16[8,48,896]{2,1,0:T(8,128)(2,1)}, bf16[8,48,896]{2,1,0:T(8,128)(2,1)S(1)}, u32[]{:S(2)}) copy-start(bf16[8,48,896]{2,1,0:T(8,128)(2,1)S(1)} %pad_maximum_fusion) | copy-start | bytes 2064388
  570.2 0.9 copy-start.9
  572.5 9.9 %copy-start.8 = (bf16[24,6144]{1,0:T(8,128)(2,1)S(1)}, bf16[24,6144]{1,0:T(8,128)(2,1)}, u32[]{:S(2)}) copy-start(bf16[24,6144]{1,0:T(8,128)(2,1)} %reduce-scatter.2.cloned.1.call-done) | copy-start | bytes 884740
  573.5 26.2 %collective-permute-start.28 = (bf16[48,2304]{1,0:T(8,128)(2,1)}, bf16[48,2304]{1,0:T(8,128)(2,1)}, u32[]{:S(2)}, u32[]{:S(2)}) collective-permute-start(bf16[48,2304]{1,0:T(8,128)(2,1)} %get-tuple-element.214), channel_id=1, source_target_pairs={{0,24},{2,26},{4,28},{6,30},{8,16},{10,18},{12,20},{14,22},{16,8},... | collective-permute-start | bytes 663560 | tf_op jit(solution)/shard_map/ppermute | solution.py:1073
  576.8 22.9 %collective-permute-start.27 = (bf16[48,2304]{1,0:T(8,128)(2,1)}, bf16[48,2304]{1,0:T(8,128)(2,1)}, u32[]{:S(2)}, u32[]{:S(2)}) collective-permute-start(bf16[48,2304]{1,0:T(8,128)(2,1)} %get-tuple-element.215), channel_id=1, source_target_pairs={{0,16},{2,18},{4,20},{6,22},{8,24},{10,26},{12,28},{14,30},{16,0},... | collective-permute-start | bytes 663560 | tf_op jit(solution)/shard_map/ppermute | solution.py:1073
  576.8 22.9 %collective-permute-start.26 = (bf16[48,2304]{1,0:T(8,128)(2,1)}, bf16[48,2304]{1,0:T(8,128)(2,1)}, u32[]{:S(2)}, u32[]{:S(2)}) collective-permute-start(bf16[48,2304]{1,0:T(8,128)(2,1)} %get-tuple-element.216), channel_id=1, source_target_pairs={{0,8},{2,10},{4,12},{6,14},{8,0},{10,2},{12,4},{14,6},{16,24},{18,... | collective-permute-start | bytes 663560 | tf_op jit(solution)/shard_map/ppermute | solution.py:1073
  579.8 17.5 %collective-permute-start.35 = (bf16[24,3072]{1,0:T(8,128)(2,1)}, bf16[24,3072]{1,0:T(8,128)(2,1)}, u32[]{:S(2)}, u32[]{:S(2)}) collective-permute-start(bf16[24,3072]{1,0:T(8,128)(2,1)} %dynamic-slice_bitcast_fusion.11), channel_id=1, source_target_pairs={{0,1},{1,0},{2,3},{3,2},{4,5},{5,4},{6,7},{7,6},{8,9},{9,8},{10,11... | collective-permute-start | bytes 442376 | tf_op jit(solution)/shard_map/ppermute | solution.py:1068
  582.2 18.8 %collective-permute-start.29 = (bf16[4,48,896]{2,1,0:T(8,128)(2,1)}, bf16[4,48,896]{2,1,0:T(8,128)(2,1)}, u32[]{:S(2)}, u32[]{:S(2)}) collective-permute-start(bf16[4,48,896]{2,1,0:T(8,128)(2,1)} %fusion.6), channel_id=1, source_target_pairs={{0,4},{2,6},{4,0},{6,2},{8,12},{10,14},{12,8},{14,10},{16,20},{18,... | collective-permute-start | bytes 1032200 | tf_op jit(solution)/shard_map/ppermute | solution.py:1073
  594.8 4.9 copy-start.10
  594.8 6.2 copy-start.2
  602.2 6.0 collective-permute-start.30
  603.4 6.6 %collective-permute-start.32 = (bf16[48,896]{1,0:T(8,128)(2,1)S(1)}, bf16[48,896]{1,0:T(8,128)(2,1)S(1)}, u32[]{:S(2)}, u32[]{:S(2)}) collective-permute-start(bf16[48,896]{1,0:T(8,128)(2,1)S(1)} %get-tuple-element.230), channel_id=1, source_target_pairs={{0,24},{2,26},{4,28},{6,30},{8,16},{10,18},{12,20},{14,22},{16,8},... | collective-permute-start | bytes 258056 | tf_op jit(solution)/shard_map/ppermute | solution.py:1073
  605.8 6.8 %collective-permute-start.31 = (bf16[48,896]{1,0:T(8,128)(2,1)S(1)}, bf16[48,896]{1,0:T(8,128)(2,1)S(1)}, u32[]{:S(2)}, u32[]{:S(2)}) collective-permute-start(bf16[48,896]{1,0:T(8,128)(2,1)S(1)} %get-tuple-element.231), channel_id=1, source_target_pairs={{0,16},{2,18},{4,20},{6,22},{8,24},{10,26},{12,28},{14,30},{16,0},... | collective-permute-start | bytes 258056 | tf_op jit(solution)/shard_map/ppermute | solution.py:1073
  606.3 7.9 %collective-permute-start.34 = (bf16[24,2304]{1,0:T(8,128)(2,1)S(1)}, bf16[24,2304]{1,0:T(8,128)(2,1)S(1)}, u32[]{:S(2)}, u32[]{:S(2)}) collective-permute-start(bf16[24,2304]{1,0:T(8,128)(2,1)S(1)} %dynamic-slice_bitcast_fusion.12), channel_id=1, source_target_pairs={{0,1},{1,0},{2,3},{3,2},{4,5},{5,4},{6,7},{7,6},{8,9},{9,8},{10,11... | collective-permute-start | bytes 331784 | tf_op jit(solution)/shard_map/ppermute | solution.py:1068
  612.7 4.1 collective-permute-start.33
Sparse Core Ops, SparseCore 0:
  19.2 135.4 all-gather.1
  341.3 156.8 reduce-scatter.1

commit v4 on v3

--- a/solution.py
+++ b/solution.py
@@ -67,6 +67,11 @@
 
 def stack_heads(values):
     return jnp.concatenate(split_heads(values), axis=0)
+
+
+def halves(ref):
+    middle_column = ref.shape[1] // 2
+    return ref.at[:, :middle_column], ref.at[:, middle_column:]
 
 
 def pair(ref, rows, part, index):
@@ -167,12 +172,9 @@
     up_ref,
     down_ref,
     qkv_ref,
-    int_ref,
-    ot_ref,
-    inf_ref,
-    act_ref,
-    gh_ref,
-    gb_ref,
+    time_ref,
+    feed_ref,
+    hidden_ref,
     mo_ref,
     mr_ref,
     gt_ref,
@@ -181,6 +183,9 @@
     half = ao_ref.shape[1]
     frames = half + ar_ref.shape[1]
     width = ao_ref.shape[3]
+    int_ref, ot_ref = halves(time_ref)
+    inf_ref, gb_ref = halves(feed_ref)
+    gh_ref, act_ref = halves(hidden_ref)
     rows = 2 * frames * GROUP
     block = frames * GROUP
     values = jnp.concatenate([ao_ref[...].astype(WIDE), ar_ref[...].astype(WIDE)], axis=1).reshape(rows, width)
@@ -213,14 +218,16 @@
     in_feed, normed, inverse = norm_rows(values, feed_gain)
     in_feed = in_feed.astype(LOW)
     inf_ref[...] = in_feed
-    place = pl.program_id(0) * STEP + lax.broadcasted_iota(jnp.int32, (STEP, width), 0)
-    lows, highs = [], []
-    for ref in (go_ref, gr_ref):
-        for frame in range(half):
-            tile = jnp.where(place < places, ref[frame].astype(WIDE), 0.0)
-            lows.append(tile[:GROUP])
-            highs.append(tile[GROUP:])
-    gradient = jnp.concatenate(lows + highs, axis=0)
+    place = pl.program_id(0) * STEP + lax.broadcasted_iota(jnp.int32, (STEP, half, width), 0)
+    sides = [jnp.where(place < places, ref[...].astype(WIDE), 0.0) for ref in (go_ref, gr_ref)]
+    gradient = jnp.concatenate(
+        [
+            jnp.swapaxes(side[start : start + GROUP], 0, 1).reshape(half * GROUP, width)
+            for start in (0, GROUP)
+            for side in sides
+        ],
+        axis=0,
+    )
     grad_low = gradient.astype(LOW)
     gb_ref[...] = grad_low
     hidden_width = up_ref.shape[1]
@@ -268,8 +275,7 @@
     tgain_ref,
     tout_ref,
     tproj_ref,
-    gq_ref,
-    tb_ref,
+    grad_ref,
     gso_ref,
     gsr_ref,
     gain_ref,
@@ -280,6 +286,7 @@
     width = ao_ref.shape[3]
     rows = 2 * frames * GROUP
     block = frames * GROUP
+    gq_ref, tb_ref = grad_ref.at[:, : 3 * width], grad_ref.at[:, 3 * width :]
     tb = gt_ref[...].astype(LOW)
     tb_ref[...] = tb
     d_ref[...] = dot(tb, tout_ref[...], NT).astype(LOW)
@@ -489,7 +496,7 @@
 
 def middle(place, after_own, after_rest, g_own, g_rest, tgain, fgain, packed):
     groups, half, _, width = after_own.shape
-    places = g_own.shape[1]
+    places = g_own.shape[0]
     frames = 2 * half
     rows = groups * frames * GROUP
     block = 2 * frames * GROUP
@@ -497,12 +504,9 @@
     padded = groups * GROUP
     outs = (
         jax.ShapeDtypeStruct((rows, 3 * width), LOW),
-        jax.ShapeDtypeStruct((rows, width), LOW),
-        jax.ShapeDtypeStruct((rows, width), LOW),
-        jax.ShapeDtypeStruct((rows, width), LOW),
-        jax.ShapeDtypeStruct((rows, hidden), LOW),
-        jax.ShapeDtypeStruct((rows, hidden), LOW),
-        jax.ShapeDtypeStruct((rows, width), LOW),
+        jax.ShapeDtypeStruct((rows, 2 * width), LOW),
+        jax.ShapeDtypeStruct((rows, 2 * width), LOW),
+        jax.ShapeDtypeStruct((rows, 2 * hidden), LOW),
         jax.ShapeDtypeStruct((2, places, half, width), LOW),
         jax.ShapeDtypeStruct((places, half, width), LOW),
         jax.ShapeDtypeStruct((rows, width), WIDE),
@@ -510,7 +514,7 @@
     )
     by_row = lambda size: pl.BlockSpec((block, size), lambda step, place: (step, 0))
     by_group = pl.BlockSpec((2, half, GROUP, width), lambda step, place: (step, 0, 0, 0))
-    by_place = pl.BlockSpec((half, STEP, width), lambda step, place: (0, step, 0))
+    by_place = pl.BlockSpec((STEP, half, width), lambda step, place: (step, 0, 0))
     flops = 2 * rows * width * (4 * width + 4 * hidden) + 8 * rows * frames * GROUP * width
     return pl.pallas_call(
         functools.partial(middle_kernel, places),
@@ -528,14 +532,11 @@
             ],
             out_specs=[
                 by_row(3 * width),
-                by_row(width),
-                by_row(width),
-                by_row(width),
-                by_row(hidden),
-                by_row(hidden),
-                by_row(width),
+                by_row(2 * width),
+                by_row(2 * width),
+                by_row(2 * hidden),
                 pl.BlockSpec((1, STEP, half, width), lambda step, place: (place[0], step, 0, 0)),
-                pl.BlockSpec((STEP, half, width), lambda step, place: (step, 0, 0)),
+                by_place,
                 by_row(width),
                 pl.BlockSpec((8, width), lambda step, place: (0, 0)),
             ],
@@ -554,8 +555,7 @@
     block = 2 * frames * GROUP
     padded = groups * GROUP
     outs = (
-        jax.ShapeDtypeStruct((rows, 3 * width), LOW),
-        jax.ShapeDtypeStruct((rows, width), LOW),
+        jax.ShapeDtypeStruct((rows, 4 * width), LOW),
         jax.ShapeDtypeStruct((half, padded, width), WIDE),
         jax.ShapeDtypeStruct((half, padded, width), WIDE),
         jax.ShapeDtypeStruct((8, width), WIDE),
@@ -570,8 +570,7 @@
         in_specs=[by_row(3 * width), by_row(width), by_group, by_group]
         + [whole(tgain.shape), columns(packed, width, 3), columns(packed, 3 * width, 0)],
         out_specs=[
-            by_row(3 * width),
-            by_row(width),
+            by_row(4 * width),
             by_place,
             by_place,
             pl.BlockSpec((8, width), lambda step: (0, 0)),
@@ -639,15 +638,7 @@
         total = dot(pairs[0][0][...], pairs[0][1][...], TN)
         for first, second in pairs[1:]:
             total = total + dot(first[...], second[...], TN)
-        if core_ref is None:
-            refs[-1][...] = total.astype(LOW)
-            return
-        keep_ref, send_ref = refs[-2:]
-        total = total.reshape(keep_ref.shape[0], 2, keep_ref.shape[1], keep_ref.shape[2])
-        total = total.astype(LOW)
-        keep = core_ref[0] == 0
-        keep_ref[...] = jnp.where(keep, total[:, 0], total[:, 1])
-        send_ref[...] = jnp.where(keep, total[:, 1], total[:, 0])
+        split_owners(core_ref, total, *refs[-2:])
 
     start = 0
     for (first, last), count in zip(tiles, parts):
@@ -689,19 +680,67 @@
     return width, count, specs, arrays, parts, tiles, flops
 
 
-def weight_gradient(*groups):
-    width, count, specs, arrays, parts, tiles, flops = plan_gradient(groups)
+def paired_specs(narrow, wide, width, turns):
+    count = wide.shape[1] // width
+    return count, [
+        pl.BlockSpec((narrow.shape[0], width), lambda step, *_: (0, step // turns)),
+        pl.BlockSpec((wide.shape[0], width), lambda step, *_: (0, step)),
+    ]
+
+
+def feed_gradient_kernel(turns, narrow_ref, wide_ref, out_ref):
+    @pl.when(pl.program_id(0) < turns)
+    def _():
+        out_ref[...] = dot(narrow_ref[...], wide_ref[...], TN).astype(LOW)
+
+    @pl.when(pl.program_id(0) >= turns)
+    def _():
+        out_ref[...] = dot(wide_ref[...], narrow_ref[...], TN).astype(LOW)
+
+
+def feed_gradient(feed, hidden, width):
+    turns = hidden.shape[1] // width // 2
+    count, specs = paired_specs(feed, hidden, width, turns)
     out = jax.ShapeDtypeStruct((width, count * width), LOW)
     return pl.pallas_call(
-        functools.partial(gradient_kernel, parts, tiles, None),
+        functools.partial(feed_gradient_kernel, turns),
         grid=(count,),
         in_specs=specs,
         out_specs=pl.BlockSpec((width, width), lambda step: (0, step)),
         out_shape=out,
         compiler_params=params(),
-        cost_estimate=cost(flops, *arrays, out),
-        name="weight_gradient",
-    )(*arrays)
+        cost_estimate=cost(2 * feed.shape[0] * width * width * count, feed, hidden, out),
+        name="feed_gradient",
+    )(feed, hidden)
+
+
+def split_owners(core_ref, total, keep_ref, send_ref):
+    total = total.reshape(keep_ref.shape[0], 2, keep_ref.shape[1], keep_ref.shape[2])
+    total = total.astype(LOW)
+    keep = core_ref[0] == 0
+    keep_ref[...] = jnp.where(keep, total[:, 0], total[:, 1])
+    send_ref[...] = jnp.where(keep, total[:, 1], total[:, 0])
+
+
+def time_gradient_kernel(core_ref, narrow_ref, wide_ref, keep_ref, send_ref):
+    split_owners(core_ref, dot(narrow_ref[...], wide_ref[...], TN), keep_ref, send_ref)
+
+
+def time_gradient(core, owners, inputs, grads, width):
+    count, specs = paired_specs(inputs, grads, width, 3)
+    blocks, rows = owners // 4, 2 * (width // owners)
+    out = jax.ShapeDtypeStruct((blocks, rows, count * width), LOW)
+    out_spec = pl.BlockSpec((blocks, rows, width), lambda step, core: (0, 0, step))
+    return pl.pallas_call(
+        time_gradient_kernel,
+        grid_spec=pltpu.PrefetchScalarGridSpec(
+            num_scalar_prefetch=1, grid=(count,), in_specs=specs, out_specs=[out_spec, out_spec]
+        ),
+        out_shape=[out, out],
+        compiler_params=params(),
+        cost_estimate=cost(2 * inputs.shape[0] * width * width * count, inputs, grads, out, out),
+        name="time_gradient",
+    )(core, inputs, grads)
 
 
 def split_gradient(core, owners, *groups):
@@ -1193,7 +1232,8 @@
     rest_b = swap_axis(send[half:], "frame")
     second = collect_lines(second)
     first = collect_half(first, 2, 1)
-    own, g_own = pick(tokens, place, 0), pick(cotangent, place, 0)
+    own = pick(tokens, place, 0)
+    g_own = pick(cotangent.transpose(0, 2, 1, 3), place, 0)
     first, second, own, g_own = tie(first, second, own, g_own)
     second = collect_half(second, 2, 1)
     second, rest_b, g_send = tie(second, rest_b, cotangent.transpose(0, 2, 1, 3))
@@ -1207,23 +1247,18 @@
     rest, after_o = tie(rest, after_o)
     in_r, qkv_r, o_r, after_r = space_forward(rest, sgain, first, second)
     g_rest, after_r = tie(g_rest, after_r)
-    g_rest = g_rest.transpose(1, 0, 2)
-    qkv_t, in_t, o_t, in_f, act, gh, gb, mixed, mixed_r, g_time, gain_f = middle(
+    qkv_t, time_in, feed_in, hidden, mixed, mixed_r, g_time, gain_f = middle(
         spot, after_o, after_r, g_own, g_rest, tgain, fgain, packed
     )
     mixed_other = swap_axis(mixed_r, "frame")
     scatter = lambda item: lax.psum_scatter(item, axes, scatter_dimension=0, tiled=True)
-    d_feed = weight_gradient(
-        ([(in_f, gh)], 0, blocks, 1, 0), ([(act, gb)], blocks, 2 * blocks, 0, 0)
-    )
+    d_feed = feed_gradient(feed_in, hidden, width)
     d_feed, g_time = tie(d_feed, g_time)
     d_feed = scatter(d_feed)
-    gq_t, tb, gs_o, gs_r, gain_t = time_backward(
+    grads_t, gs_o, gs_r, gain_t = time_backward(
         qkv_t, g_time, after_o, after_r, tgain, packed
     )
-    d_time = split_gradient(
-        core, owners, ([(in_t, gq_t)], 0, 3, 1, 0), ([(o_t, tb)], 3, 4, 1, 0)
-    )
+    d_time = time_gradient(core, owners, time_in, grads_t, width)
     d_time, gs_r, mixed_other = tie(d_time, gs_r, mixed_other)
     d_time = scatter_columns(*scatter_core(*d_time))
     gq_r, sb_r, gx_r, gain_sr = space_backward(spot, rest, gs_r, qkv_r, sgain, first, second, LOW)

time: 633 us -> 625 us (0.987)
  local copies, waits for them, and re-layouts: 50.6 us -> 44.1 us
    pallas_call x3 -> x2, Pallas kernels: 53.5 us -> 28.3 us  [split_gradient(): pl.pallas_call(functools.partial(gradient_kernel, parts, tiles), grid_spe...]
    pallas_call x1 -> x2, Pallas kernels: 41.9 us -> 61.7 us  [the longest x1 39.2 us: feed_gradient(): pl.pallas_call(functools.partial(feed_gradient_kernel, turns), grid=(coun...]
  transfers between devices with their start and end apart: 38 -> 38, of which waited for: 14 -> 16; matrix products, arithmetic and copies ran while one was open for 12% -> 11% of each run, Pallas kernels for 37% -> 37%
where the time goes in v4:
time: 625 us; the launch traced here: 618 us
  Pallas kernels  392 us (63%)
  waiting for transfers between devices  93.9 us (15%)
  local copies, waits for them, and re-layouts  44.1 us (7%)
  starting transfers between devices  40.4 us (6%)
  other arithmetic  32.4 us (5%)
  between operations  15.1 us (2%)
    pallas_call x1, Pallas kernels, middle(): pl.pallas_call(functools.partial(middle_kernel, places), grid_spec=pltpu....  125 us
    pallas_call x2, Pallas kernels, space_backward(): pl.pallas_call(functools.partial(space_backward_kernel, places), grid_spe...  77.7 us
    ppermute x25, waiting for transfers between devices, flip(): lax.ppermute(values, 'clip', [(index, index ^ mask) for index in range(si...  65.4 us
    pallas_call x1, Pallas kernels, time_backward(): pl.pallas_call(time_backward_kernel, grid=(groups // 2,), in_specs=[by_ro...  54.4 us
    pallas_call x2, Pallas kernels, space_forward(): pl.pallas_call(functools.partial(space_forward_kernel, places), grid=(fra...  45 us
    pallas_call x1, Pallas kernels, feed_gradient(): pl.pallas_call(functools.partial(feed_gradient_kernel, turns), grid=(coun...  39.2 us
    ppermute x11, waiting for transfers between devices, swap_axis(): lax.ppermute(values, axis, [(index, size - 1 - index) for index in range(...  28.4 us
    pallas_call x2, Pallas kernels, split_gradient(): pl.pallas_call(functools.partial(gradient_kernel, parts, tiles), grid_spe...  28.3 us
  transfers between devices with their start and end apart: 38, of which 16 were waited for; matrix products, arithmetic and copies ran while one was open for 11% of the time, Pallas kernels for 37%

profile of v4, /device:TPU:0, one launch (start us, length us, event | category | flops | bytes accessed | tf_op | source)
XLA Modules:
  0.0 617.9 jit_solution(12131899216492787844)
XLA Ops:
  9.6 3.0 collective-permute-start.1
  14.6 2.1 reshape.152
  16.9 1.3 reshape.153
  19.1 1.4 dynamic-slice_bitcast_fusion.3
  20.6 2.1 collective-permute-start.5
  22.6 2.0 constant_dynamic-slice_fusion
  24.6 2.0 copy.101
  26.6 3.6 collective-permute-start.4
  31.1 6.0 collective-permute-done.4
  37.1 14.2 %collective-permute-done.3 = bf16[2,24,1536]{2,1,0:T(8,128)(2,1)S(1)} collective-permute-done((bf16[2,24,1536]{2,1,0:T(8,128)(2,1)S(1)}, bf16[2,24,1536]{2,1,0:T(8,128)(2,1)S(1)}, u32[]{:S(2)}, u32[]{:S(2)}) %collective-permute-start.3) | collective-permute-done | bytes 147488 | tf_op jit(solution)/shard_map/ppermute | solution.py:1112
  51.7 3.8 collective-permute-start.9
  56.2 1.5 dynamic-slice_bitcast_fusion.1.go_ref
  57.8 1.8 collective-permute-start.6
  59.6 1.5 collective-permute-start.11
  61.1 2.1 collective-permute-done.9
  63.1 17.2 %collective-permute-done.8 = bf16[2,24,1664]{2,1,0:T(8,128)(2,1)S(1)} collective-permute-done((bf16[2,24,1664]{2,1,0:T(8,128)(2,1)S(1)}, bf16[2,24,1664]{2,1,0:T(8,128)(2,1)S(1)}, u32[]{:S(2)}, u32[]{:S(2)}) %collective-permute-start.8) | collective-permute-done | bytes 159776 | tf_op jit(solution)/shard_map/ppermute | solution.py:1112
  81.6 12.5 %collective-permute-done.10 = bf16[4,2,24,1664]{3,2,1,0:T(8,128)(2,1)S(1)} collective-permute-done((bf16[4,2,24,1664]{3,2,1,0:T(8,128)(2,1)S(1)}, bf16[4,2,24,1664]{3,2,1,0:T(8,128)(2,1)S(1)}, u32[]{:S(2)}, u32[]{:S(2)}) %collective-permute-start.10) | collective-permute-done | bytes 639008 | tf_op jit(solution)/shard_map/ppermute | solution.py:1112
  94.4 1.8 collective-permute-done.11
  97.2 1.6 dynamic-slice_bitcast_fusion
  99.2 1.6 copy.74
  101.1 1.8 maximum_bitcast_fusion.x_ref
  102.9 2.0 maximum_select_fusion.1
  104.9 1.6 copy.72
  106.5 2.3 maximum_select_fusion
  109.0 1.2 fusion.14
  110.3 1.7 copy.78.fgain_ref
  113.5 22.5 %space_forward.2 = (bf16[8,208,768]{2,1,0:T(8,128)(2,1)}, bf16[8,208,2304]{2,1,0:T(8,128)(2,1)}, bf16[8,208,768]{2,1,0:T(8,128)(2,1)}, f32[26,8,8,768]{3,2,1,0:T(8,128)}) custom-call(bf16[8,196,768]{2,1,0:T(8,128)(2,1)} %bitcast.178, f32[1,768]{1,0:T(1,128)} %copy.73.gain_ref.gain_row_ref, bf16[768,1536]{1,0:T(8,128)(2,1)} %bitcast.174, ...), custom_call_target="tpu_custom_call" | custom-call | flops 1663041536 | bytes 4202496 | tf_op jit(solution)/shard_map/space_forward/pallas_call | solution.py:473
  136.0 22.5 %space_forward.3 = (bf16[8,208,768]{2,1,0:T(8,128)(2,1)}, bf16[8,208,2304]{2,1,0:T(8,128)(2,1)}, bf16[8,208,768]{2,1,0:T(8,128)(2,1)}, f32[26,8,8,768]{3,2,1,0:T(8,128)}) custom-call(bf16[8,196,768]{2,1,0:T(8,128)(2,1)} %maximum_bitcast_fusion.x_ref, f32[1,768]{1,0:T(1,128)} %copy.73.gain_ref.gain_row_ref, bf16[768,1536]{1,0:T(8,128)(2,1)} %bitcast.175, ...), custom_call_target="tpu_custom_call" | custom-call | flops 1663041536 | bytes 4202496 | tf_op jit(solution)/shard_map/space_forward/pallas_call | solution.py:473
  158.5 15.6 %collective-permute-done.14.gr_ref = bf16[196,8,768]{2,1,0:T(8,128)(2,1)} collective-permute-done((bf16[196,8,768]{2,1,0:T(8,128)(2,1)}, bf16[196,8,768]{2,1,0:T(8,128)(2,1)}, u32[]{:S(2)}, u32[]{:S(2)}) %collective-permute-start.14) | collective-permute-done | bytes 2408480 | tf_op jit(solution)/shard_map/ppermute | solution.py:1107
  174.1 124.9 %middle.1 = (bf16[3328,2304]{1,0:T(8,128)(2,1)}, bf16[3328,1536]{1,0:T(8,128)(2,1)}, bf16[3328,1536]{1,0:T(8,128)(2,1)}, bf16[3328,6144]{1,0:T(8,128)(2,1)}, bf1...) custom-call(s32[1]{0:T(128)} %bitcast.38.place_ref, ...), custom_call_target="tpu_custom_call" | custom-call | flops 13522436096 | bytes 18198528 | tf_op jit(solution)/shard_map/middle/pallas_call | solution.py:519
  299.0 39.2 %feed_gradient.1 = bf16[768,6144]{1,0:T(8,128)(2,1)} custom-call(bf16[3328,1536]{1,0:T(8,128)(2,1)} %get-tuple-element.128.narrow_ref, bf16[3328,6144]{1,0:T(8,128)(2,1)} %get-tuple-element.129.wide_ref), custom_call_target="tpu_custom_call" | custom-call | flops 5234491392 | bytes 10092544 | tf_op jit(solution)/shard_map/feed_gradient/pallas_call | solution.py:705
  338.2 1.7 copy-done.22
  340.2 54.4 %time_backward.1 = (bf16[3328,3072]{1,0:T(8,128)(2,1)}, f32[8,208,768]{2,1,0:T(8,128)}, f32[8,208,768]{2,1,0:T(8,128)}, f32[8,768]{1,0:T(8,128)}) custom-call(bf16[3328,2304]{1,0:T(8,128)(2,1)} %get-tuple-element.127.qkv_ref, f32[3328,768]{1,0:T(8,128)} %get-tuple-element.131.gt_ref, f32[26,8,8,768]{3,2,1,0:T(8,128)} %get-tuple-element.118.ao_ref, ...), custom_call_target="tpu_custom_call" | custom-call | flops 3707764736 | bytes 11079680 | tf_op jit(solution)/shard_map/time_backward/pallas_call | solution.py:567
  394.6 22.4 %time_gradient.1 = (bf16[8,48,3072]{2,1,0:T(8,128)(2,1)}, bf16[8,48,3072]{2,1,0:T(8,128)(2,1)}) custom-call(s32[1]{0:T(128)} %bitcast.core_ref, bf16[3328,1536]{1,0:T(8,128)(2,1)} %get-tuple-element.126.narrow_ref, bf16[3328,3072]{1,0:T(8,128)(2,1)} %get-tuple-element.132.wide_ref), custom_call_target="tpu_custom_call" | custom-call | flops 2617245696 | bytes 5898240 | tf_op jit(solution)/shard_map/time_gradient/pallas_call | solution.py:734
  417.1 4.7 collective-permute-done.16
  421.8 2.7 fusion.1
  424.6 1.6 collective-permute-start.17
  426.2 38.6 %space_backward.2 = (bf16[8,208,2304]{2,1,0:T(8,128)(2,1)}, bf16[8,208,768]{2,1,0:T(8,128)(2,1)}, bf16[196,8,768]{2,1,0:T(8,128)(2,1)}, f32[8,768]{1,0:T(8,128)}) custom-call(s32[1]{0:T(128)} %bitcast.38.place_ref, bf16[8,196,768]{2,1,0:T(8,128)(2,1)} %maximum_bitcast_fusion.x_ref, f32[8,208,768]{2,1,0:T(8,128)} %get-tuple-element.140.gs_ref, ...), custom_call_target="tpu_custom_call" | custom-call | flops 2194669568 | bytes 4640768 | tf_op jit(solution)/shard_map/space_backward/pallas_call | solution.py:599
  464.8 3.4 fusion.13
  468.2 1.5 collective-permute-start.21
  470.6 3.3 collective-permute-start.20
  473.9 1.2 collective-permute-start.18
  475.0 39.1 %space_backward.3 = (bf16[8,208,2304]{2,1,0:T(8,128)(2,1)}, bf16[8,208,768]{2,1,0:T(8,128)(2,1)}, f32[2,196,8,768]{3,2,1,0:T(8,128)}, f32[8,768]{1,0:T(8,128)}) custom-call(s32[1]{0:T(128)} %bitcast.38.place_ref, bf16[8,196,768]{2,1,0:T(8,128)(2,1)} %bitcast.179, f32[8,208,768]{2,1,0:T(8,128)} %get-tuple-element.145.gs_ref, ...), custom_call_target="tpu_custom_call" | custom-call | flops 2194669568 | bytes 5844992 | tf_op jit(solution)/shard_map/space_backward/pallas_call | solution.py:599
  515.0 18.9 %split_gradient.2 = (bf16[8,48,2304]{2,1,0:T(8,128)(2,1)}, bf16[8,48,2304]{2,1,0:T(8,128)(2,1)}) custom-call(s32[1]{0:T(128)} %bitcast.core_ref, bf16[1664,768]{1,0:T(8,128)(2,1)} %bitcast.197, bf16[1664,2304]{1,0:T(8,128)(2,1)} %bitcast.181, bf16[1664,768]{1,0:T(8,128)(2,1)} %bitcast.198, bf16[1664,2304]{1,0:T(8,128)(2,1)} %bitcast.180), custom_call_target="tpu_custom_call" | custom-call | flops 1962934272 | bytes 3997696 | tf_op jit(solution)/shard_map/split_gradient/pallas_call | solution.py:751
  535.0 3.0 collective-permute-done.22
  538.0 2.6 fusion.3
  540.6 1.4 fusion.2
  542.6 9.5 %split_gradient.3 = (bf16[8,48,768]{2,1,0:T(8,128)(2,1)}, bf16[8,48,768]{2,1,0:T(8,128)(2,1)}) custom-call(s32[1]{0:T(128)} %bitcast.core_ref, bf16[1664,768]{1,0:T(8,128)(2,1)} %bitcast.195, bf16[1664,768]{1,0:T(8,128)(2,1)} %bitcast.200, bf16[1664,768]{1,0:T(8,128)(2,1)} %bitcast.196, bf16[1664,768]{1,0:T(8,128)(2,1)} %bitcast.199), custom_call_target="tpu_custom_call" | custom-call | flops 654311424 | bytes 1900544 | tf_op jit(solution)/shard_map/split_gradient/pallas_call | solution.py:751
  554.4 8.9 %collective-permute-done.25 = bf16[98,8,768]{2,1,0:T(8,128)(2,1)} collective-permute-done((bf16[98,8,768]{2,1,0:T(8,128)(2,1)}, bf16[98,8,768]{2,1,0:T(8,128)(2,1)}, u32[]{:S(2)}, u32[]{:S(2)}) %collective-permute-start.25) | collective-permute-done | bytes 1204256 | tf_op jit(solution)/shard_map/ppermute | solution.py:1107
  564.2 1.4 add_convert_fusion.3
  566.6 3.3 collective-permute-start.28
  571.0 1.3 add_convert_fusion.8
  574.9 2.9 convert_dynamic-update-slice_fusion.1
  577.7 3.3 bitcast_dynamic-update-slice_fusion
  581.0 2.9 convert_dynamic-update-slice_fusion
  585.9 1.2 copy.87
  587.2 2.6 reshape.171
  592.1 1.3 add_convert_fusion.9
  595.6 2.4 collective-permute-start.32
  598.5 1.5 collective-permute-start.34
  600.5 1.9 collective-permute-done.32
  602.4 2.7 collective-permute-done.31
  605.1 1.5 collective-permute-start.33
  607.4 1.8 collective-permute-done.33
  (164 shorter events, 33.7 us)
Async XLA Ops:
  7.2 11.0 %copy-start.17 = (bf16[24,768]{1,0:T(8,128)(2,1)S(1)}, bf16[24,768]{1,0:T(8,128)(2,1)}, u32[]{:S(2)}) copy-start(bf16[24,768]{1,0:T(8,128)(2,1)} %param.19) | copy-start | bytes 110596
  7.2 11.0 %copy-start.16 = (bf16[24,2304]{1,0:T(8,128)(2,1)S(1)}, bf16[24,2304]{1,0:T(8,128)(2,1)}, u32[]{:S(2)}) copy-start(bf16[24,2304]{1,0:T(8,128)(2,1)} %param.18) | copy-start | bytes 331780
  7.2 166.9 %all-gather.2.cloned.1.call-start = ((), (), s32[]{:S(2)}) async-start(), calls=%async_computation.1 | async-start | bytes 14598144 | tf_op jit(solution)/shard_map/all_gather | solution.py:1226
  9.6 9.3 %collective-permute-start.1 = (bf16[24,1664]{1,0:T(8,128)(2,1)S(1)}, bf16[24,1664]{1,0:T(8,128)(2,1)S(1)}, u32[]{:S(2)}, u32[]{:S(2)}) collective-permute-start(bf16[24,1664]{1,0:T(8,128)(2,1)S(1)} %get-tuple-element.231), channel_id=1, source_target_pairs={{0,1},{1,0},{2,3},{3,2},{4,5},{5,4},{6,7},{7,6},{8,9},{9,8},{10,11... | collective-permute-start | bytes 239624 | tf_op jit(solution)/shard_map/ppermute | solution.py:1107
  13.5 5.4 collective-permute-start
  19.1 545.2 %reduce-scatter.2.cloned.1.call-start = ((), (), s32[]{:S(2)}) async-start(), calls=%async_computation.2 | async-start | bytes 9732096 | tf_op jit(solution)/shard_map/reduce_scatter | solution.py:1254
  19.1 11.9 %slice-start = ((s8[4816896]{0:T(1024)(128)(4,1)}), s8[622592]{0:T(1024)(128)(4,1)S(1)}, s32[]{:S(2)}) async-start(s8[4816896]{0:T(1024)(128)(4,1)} %bitcast.183), calls=%async_computation.3 | async-start | bytes 1245184
  20.6 31.2 %collective-permute-start.5 = (bf16[98,8,768]{2,1,0:T(8,128)(2,1)S(1)}, bf16[98,8,768]{2,1,0:T(8,128)(2,1)S(1)}, u32[]{:S(2)}, u32[]{:S(2)}) collective-permute-start(bf16[98,8,768]{2,1,0:T(8,128)(2,1)S(1)} %dynamic-slice_bitcast_fusion.3), channel_id=1, source_target_pairs={{0,1},{1,0},{2,3},{3,2},{4,5},{5,4},{6,7},{7,6},{8,9},{9,8},{10,11... | collective-permute-start | bytes 3612680 | tf_op jit(solution)/shard_map/ppermute | solution.py:1107
  22.6 8.4 %slice-start.1 = ((s8[4816896]{0:T(1024)(128)(4,1)}), s8[4194304]{0:T(1024)(128)(4,1)S(1)}, s32[]{:S(2)}) async-start(s8[4816896]{0:T(1024)(128)(4,1)} %bitcast.183), calls=%async_computation.4 | async-start | bytes 8388608
  22.6 33.5 %slice-start.2 = ((s8[4816896]{0:T(1024)(128)(4,1)}), s8[4194304]{0:T(1024)(128)(4,1)S(1)}, s32[]{:S(2)}) async-start(s8[4816896]{0:T(1024)(128)(4,1)} %bitcast.188), calls=%async_computation.5 | async-start | bytes 8388608
  24.6 31.5 %slice-start.3 = ((s8[4816896]{0:T(1024)(128)(4,1)}), s8[622592]{0:T(1024)(128)(4,1)S(1)}, s32[]{:S(2)}) async-start(s8[4816896]{0:T(1024)(128)(4,1)} %bitcast.188), calls=%async_computation.6 | async-start | bytes 1245184
  26.6 10.5 %collective-permute-start.4 = (bf16[2,24,1536]{2,1,0:T(8,128)(2,1)S(1)}, bf16[2,24,1536]{2,1,0:T(8,128)(2,1)S(1)}, u32[]{:S(2)}, u32[]{:S(2)}) collective-permute-start(bf16[2,24,1536]{2,1,0:T(8,128)(2,1)S(1)} %maximum_select_fusion.5), channel_id=1, source_target_pairs={{0,24},{2,26},{4,28},{6,30},{8,16},{10,18},{12,20},{14,22},{16,8},... | collective-permute-start | bytes 442376 | tf_op jit(solution)/shard_map/ppermute | solution.py:1112
  30.2 21.1 %collective-permute-start.3 = (bf16[2,24,1536]{2,1,0:T(8,128)(2,1)S(1)}, bf16[2,24,1536]{2,1,0:T(8,128)(2,1)S(1)}, u32[]{:S(2)}, u32[]{:S(2)}) collective-permute-start(bf16[2,24,1536]{2,1,0:T(8,128)(2,1)S(1)} %maximum_select_fusion.5), channel_id=1, source_target_pairs={{0,16},{2,18},{4,20},{6,22},{8,24},{10,26},{12,28},{14,30},{16,0},... | collective-permute-start | bytes 442376 | tf_op jit(solution)/shard_map/ppermute | solution.py:1112
  30.2 21.1 %collective-permute-start.2 = (bf16[2,24,1536]{2,1,0:T(8,128)(2,1)S(1)}, bf16[2,24,1536]{2,1,0:T(8,128)(2,1)S(1)}, u32[]{:S(2)}, u32[]{:S(2)}) collective-permute-start(bf16[2,24,1536]{2,1,0:T(8,128)(2,1)S(1)} %maximum_select_fusion.5), channel_id=1, source_target_pairs={{0,8},{2,10},{4,12},{6,14},{8,0},{10,2},{12,4},{14,6},{16,24},{18,... | collective-permute-start | bytes 442376 | tf_op jit(solution)/shard_map/ppermute | solution.py:1112
  51.7 6.0 copy-start.5
  51.7 11.4 %collective-permute-start.9 = (bf16[2,24,1664]{2,1,0:T(8,128)(2,1)S(1)}, bf16[2,24,1664]{2,1,0:T(8,128)(2,1)S(1)}, u32[]{:S(2)}, u32[]{:S(2)}) collective-permute-start(bf16[2,24,1664]{2,1,0:T(8,128)(2,1)S(1)} %maximum_select_fusion.4), channel_id=1, source_target_pairs={{0,24},{2,26},{4,28},{6,30},{8,16},{10,18},{12,20},{14,22},{16,8},... | collective-permute-start | bytes 479240 | tf_op jit(solution)/shard_map/ppermute | solution.py:1112
  55.6 24.8 %collective-permute-start.8 = (bf16[2,24,1664]{2,1,0:T(8,128)(2,1)S(1)}, bf16[2,24,1664]{2,1,0:T(8,128)(2,1)S(1)}, u32[]{:S(2)}, u32[]{:S(2)}) collective-permute-start(bf16[2,24,1664]{2,1,0:T(8,128)(2,1)S(1)} %maximum_select_fusion.4), channel_id=1, source_target_pairs={{0,16},{2,18},{4,20},{6,22},{8,24},{10,26},{12,28},{14,30},{16,0},... | collective-permute-start | bytes 479240 | tf_op jit(solution)/shard_map/ppermute | solution.py:1112
  55.6 24.8 %collective-permute-start.7 = (bf16[2,24,1664]{2,1,0:T(8,128)(2,1)S(1)}, bf16[2,24,1664]{2,1,0:T(8,128)(2,1)S(1)}, u32[]{:S(2)}, u32[]{:S(2)}) collective-permute-start(bf16[2,24,1664]{2,1,0:T(8,128)(2,1)S(1)} %maximum_select_fusion.4), channel_id=1, source_target_pairs={{0,8},{2,10},{4,12},{6,14},{8,0},{10,2},{12,4},{14,6},{16,24},{18,... | collective-permute-start | bytes 479240 | tf_op jit(solution)/shard_map/ppermute | solution.py:1112
  57.8 22.8 %collective-permute-start.6 = (bf16[4,2,24,1536]{3,2,1,0:T(8,128)(2,1)S(1)}, bf16[4,2,24,1536]{3,2,1,0:T(8,128)(2,1)S(1)}, u32[]{:S(2)}, u32[]{:S(2)}) collective-permute-start(bf16[4,2,24,1536]{3,2,1,0:T(8,128)(2,1)S(1)} %pad_maximum_fusion.3), channel_id=1, source_target_pairs={{0,4},{2,6},{4,0},{6,2},{8,12},{10,14},{12,8},{14,10},{16,20},{18,... | collective-permute-start | bytes 1769480 | tf_op jit(solution)/shard_map/ppermute | solution.py:1112
  59.6 36.6 %collective-permute-start.11 = (bf16[98,8,768]{2,1,0:T(8,128)(2,1)S(1)}, bf16[98,8,768]{2,1,0:T(8,128)(2,1)S(1)}, u32[]{:S(2)}, u32[]{:S(2)}) collective-permute-start(bf16[98,8,768]{2,1,0:T(8,128)(2,1)S(1)} %slice.61), channel_id=1, source_target_pairs={{0,1},{1,0},{2,3},{3,2},{4,5},{5,4},{6,7},{7,6},{8,9},{9,8},{10,11... | collective-permute-start | bytes 3612680 | tf_op jit(solution)/shard_map/ppermute | solution.py:1107
  80.8 13.4 %collective-permute-start.10 = (bf16[4,2,24,1664]{3,2,1,0:T(8,128)(2,1)S(1)}, bf16[4,2,24,1664]{3,2,1,0:T(8,128)(2,1)S(1)}, u32[]{:S(2)}, u32[]{:S(2)}) collective-permute-start(bf16[4,2,24,1664]{3,2,1,0:T(8,128)(2,1)S(1)} %pad_maximum_fusion.2), channel_id=1, source_target_pairs={{0,4},{2,6},{4,0},{6,2},{8,12},{10,14},{12,8},{14,10},{16,20},{18,... | collective-permute-start | bytes 1916936 | tf_op jit(solution)/shard_map/ppermute | solution.py:1112
  81.6 21.3 %collective-permute-start.13 = (bf16[4,2,2,24,1536]{4,3,2,0,1:T(8,128)(2,1)S(1)}, bf16[4,2,2,24,1536]{4,3,2,0,1:T(8,128)(2,1)}, u32[]{:S(2)}, u32[]{:S(2)}) collective-permute-start(bf16[4,2,2,24,1536]{4,3,2,0,1:T(8,128)(2,1)S(1)} %maximum_select_fusion.3), channel_id=1, source_target_pairs={{0,2},{2,0},{4,6},{6,4},{8,10},{10,8},{12,14},{14,12},{16,18},{18,... | collective-permute-start | bytes 3538952 | tf_op jit(solution)/shard_map/ppermute | solution.py:1112
  96.1 1.0 copy-start.6
  97.2 9.3 %collective-permute-start.12 = (bf16[4,2,2,24,1664]{4,3,2,0,1:T(8,128)(2,1)S(1)}, bf16[4,2,2,24,1664]{4,3,2,0,1:T(8,128)(2,1)}, u32[]{:S(2)}, u32[]{:S(2)}) collective-permute-start(bf16[4,2,2,24,1664]{4,3,2,0,1:T(8,128)(2,1)S(1)} %maximum_select_fusion.2), channel_id=1, source_target_pairs={{0,2},{2,0},{4,6},{6,4},{8,10},{10,8},{12,14},{14,12},{16,18},{18,... | collective-permute-start | bytes 3833864 | tf_op jit(solution)/shard_map/ppermute | solution.py:1112
  98.7 75.4 %collective-permute-start.14 = (bf16[196,8,768]{2,1,0:T(8,128)(2,1)}, bf16[196,8,768]{2,1,0:T(8,128)(2,1)}, u32[]{:S(2)}, u32[]{:S(2)}) collective-permute-start(bf16[196,8,768]{2,1,0:T(8,128)(2,1)} %dynamic-slice_bitcast_fusion), channel_id=1, source_target_pairs={{0,1},{1,0},{2,3},{3,2},{4,5},{5,4},{6,7},{7,6},{8,9},{9,8},{10,11... | collective-permute-start | bytes 7225352 | tf_op jit(solution)/shard_map/ppermute | solution.py:1107
  99.2 1.6 copy-start.7
  109.0 4.5 copy-start
  338.2 1.7 copy-start.22
  339.9 77.2 %collective-permute-start.15 = (bf16[196,8,768]{2,1,0:T(8,128)(2,1)S(1)}, bf16[196,8,768]{2,1,0:T(8,128)(2,1)}, u32[]{:S(2)}, u32[]{:S(2)}) collective-permute-start(bf16[196,8,768]{2,1,0:T(8,128)(2,1)S(1)} %copy-done.22), channel_id=1, source_target_pairs={{0,1},{1,0},{2,3},{3,2},{4,5},{5,4},{6,7},{7,6},{8,9},{9,8},{10,11... | collective-permute-start | bytes 7225352 | tf_op jit(solution)/shard_map/ppermute | solution.py:1107
  417.1 4.7 collective-permute-start.16
  424.6 45.5 %collective-permute-start.17 = (bf16[4,48,3072]{2,1,0:T(8,128)(2,1)}, bf16[4,48,3072]{2,1,0:T(8,128)(2,1)S(1)}, u32[]{:S(2)}, u32[]{:S(2)}) collective-permute-start(bf16[4,48,3072]{2,1,0:T(8,128)(2,1)} %fusion.1), channel_id=1, source_target_pairs={{0,4},{2,6},{4,0},{6,2},{8,12},{10,14},{12,8},{14,10},{16,20},{18,... | collective-permute-start | bytes 3538952 | tf_op jit(solution)/shard_map/ppermute | solution.py:1112
  464.8 4.9 copy-start.3
  468.2 46.0 %collective-permute-start.21 = (bf16[98,8,768]{2,1,0:T(8,128)(2,1)}, bf16[98,8,768]{2,1,0:T(8,128)(2,1)}, u32[]{:S(2)}, u32[]{:S(2)}) collective-permute-start(bf16[98,8,768]{2,1,0:T(8,128)(2,1)} %get-tuple-element.201), channel_id=1, source_target_pairs={{0,1},{1,0},{2,3},{3,2},{4,5},{5,4},{6,7},{7,6},{8,9},{9,8},{10,11... | collective-permute-start | bytes 3612680 | tf_op jit(solution)/shard_map/ppermute | solution.py:1107
  470.6 43.6 %collective-permute-start.20 = (bf16[48,3072]{1,0:T(8,128)(2,1)S(1)}, bf16[48,3072]{1,0:T(8,128)(2,1)S(1)}, u32[]{:S(2)}, u32[]{:S(2)}) collective-permute-start(bf16[48,3072]{1,0:T(8,128)(2,1)S(1)} %get-tuple-element.202), channel_id=1, source_target_pairs={{0,24},{2,26},{4,28},{6,30},{8,16},{10,18},{12,20},{14,22},{16,8},... | collective-permute-start | bytes 884744 | tf_op jit(solution)/shard_map/ppermute | solution.py:1112
  473.8 40.3 %collective-permute-start.19 = (bf16[48,3072]{1,0:T(8,128)(2,1)S(1)}, bf16[48,3072]{1,0:T(8,128)(2,1)S(1)}, u32[]{:S(2)}, u32[]{:S(2)}) collective-permute-start(bf16[48,3072]{1,0:T(8,128)(2,1)S(1)} %get-tuple-element.203), channel_id=1, source_target_pairs={{0,16},{2,18},{4,20},{6,22},{8,24},{10,26},{12,28},{14,30},{16,0},... | collective-permute-start | bytes 884744 | tf_op jit(solution)/shard_map/ppermute | solution.py:1112
  473.9 40.4 %collective-permute-start.18 = (bf16[48,3072]{1,0:T(8,128)(2,1)S(1)}, bf16[48,3072]{1,0:T(8,128)(2,1)S(1)}, u32[]{:S(2)}, u32[]{:S(2)}) collective-permute-start(bf16[48,3072]{1,0:T(8,128)(2,1)S(1)} %get-tuple-element.204), channel_id=1, source_target_pairs={{0,8},{2,10},{4,12},{6,14},{8,0},{10,2},{12,4},{14,6},{16,24},{18,... | collective-permute-start | bytes 884744 | tf_op jit(solution)/shard_map/ppermute | solution.py:1112
  514.2 19.7 %copy-start.13 = (bf16[48,3072]{1,0:T(8,128)(2,1)}, bf16[48,3072]{1,0:T(8,128)(2,1)S(1)}, u32[]{:S(2)}) copy-start(bf16[48,3072]{1,0:T(8,128)(2,1)S(1)} %collective-permute-done.20) | copy-start | bytes 884740
  514.2 0.8 copy-start.15
  515.0 19.0 %copy-start.20 = (f32[8,768]{1,0:T(8,128)S(1)}, f32[8,768]{1,0:T(8,128)}, u32[]{:S(2)}) copy-start(f32[8,768]{1,0:T(8,128)} %get-tuple-element.166) | copy-start | bytes 73732
  515.0 19.0 %copy-start.21 = (f32[8,768]{1,0:T(8,128)S(1)}, f32[8,768]{1,0:T(8,128)}, u32[]{:S(2)}) copy-start(f32[8,768]{1,0:T(8,128)} %get-tuple-element.165) | copy-start | bytes 73732
  515.0 19.7 %copy-start.18 = (f32[8,768]{1,0:T(8,128)S(1)}, f32[8,768]{1,0:T(8,128)}, u32[]{:S(2)}) copy-start(f32[8,768]{1,0:T(8,128)} %get-tuple-element.164) | copy-start | bytes 73732
  515.0 19.7 %copy-start.19 = (f32[8,768]{1,0:T(8,128)S(1)}, f32[8,768]{1,0:T(8,128)}, u32[]{:S(2)}) copy-start(f32[8,768]{1,0:T(8,128)} %get-tuple-element.163) | copy-start | bytes 73732
  533.9 6.7 %copy-start.4 = (bf16[8,48,2304]{2,1,0:T(8,128)(2,1)S(1)}, bf16[8,48,2304]{2,1,0:T(8,128)(2,1)}, u32[]{:S(2)}) copy-start(bf16[8,48,2304]{2,1,0:T(8,128)(2,1)} %get-tuple-element.153) | copy-start | bytes 5308420
  533.9 4.1 collective-permute-start.22
  534.1 29.3 %collective-permute-start.25 = (bf16[98,8,768]{2,1,0:T(8,128)(2,1)}, bf16[98,8,768]{2,1,0:T(8,128)(2,1)}, u32[]{:S(2)}, u32[]{:S(2)}) collective-permute-start(bf16[98,8,768]{2,1,0:T(8,128)(2,1)} %get-tuple-element.200), channel_id=1, source_target_pairs={{0,1},{1,0},{2,3},{3,2},{4,5},{5,4},{6,7},{7,6},{8,9},{9,8},{10,11... | collective-permute-start | bytes 3612680 | tf_op jit(solution)/shard_map/ppermute | solution.py:1107
  542.0 22.1 %collective-permute-start.23 = (bf16[4,48,2304]{2,1,0:T(8,128)(2,1)}, bf16[4,48,2304]{2,1,0:T(8,128)(2,1)}, u32[]{:S(2)}, u32[]{:S(2)}) collective-permute-start(bf16[4,48,2304]{2,1,0:T(8,128)(2,1)} %fusion.3), channel_id=1, source_target_pairs={{0,4},{2,6},{4,0},{6,2},{8,12},{10,14},{12,8},{14,10},{16,20},{18,... | collective-permute-start | bytes 2654216 | tf_op jit(solution)/shard_map/ppermute | solution.py:1112
  553.2 10.1 %collective-permute-start.24 = (bf16[8,48,896]{2,1,0:T(8,128)(2,1)S(1)}, bf16[8,48,896]{2,1,0:T(8,128)(2,1)S(1)}, u32[]{:S(2)}, u32[]{:S(2)}) collective-permute-start(bf16[8,48,896]{2,1,0:T(8,128)(2,1)S(1)} %pad_maximum_fusion.1), channel_id=1, source_target_pairs={{0,2},{2,0},{4,6},{6,4},{8,10},{10,8},{12,14},{14,12},{16,18},{18,... | collective-permute-start | bytes 2064392 | tf_op jit(solution)/shard_map/ppermute | solution.py:1112
  554.4 19.1 %copy-start.1 = (bf16[8,48,896]{2,1,0:T(8,128)(2,1)}, bf16[8,48,896]{2,1,0:T(8,128)(2,1)S(1)}, u32[]{:S(2)}) copy-start(bf16[8,48,896]{2,1,0:T(8,128)(2,1)S(1)} %pad_maximum_fusion) | copy-start | bytes 2064388
  563.4 0.9 copy-start.10
  565.6 7.9 %copy-start.11 = (bf16[8,48,896]{2,1,0:T(8,128)(2,1)S(1)}, bf16[8,48,896]{2,1,0:T(8,128)(2,1)}, u32[]{:S(2)}) copy-start(bf16[8,48,896]{2,1,0:T(8,128)(2,1)} %copy-done.10) | copy-start | bytes 2064388
  565.6 9.2 %copy-start.8 = (bf16[24,6144]{1,0:T(8,128)(2,1)S(1)}, bf16[24,6144]{1,0:T(8,128)(2,1)}, u32[]{:S(2)}) copy-start(bf16[24,6144]{1,0:T(8,128)(2,1)} %reduce-scatter.2.cloned.1.call-done) | copy-start | bytes 884740
  566.6 25.5 %collective-permute-start.28 = (bf16[48,2304]{1,0:T(8,128)(2,1)}, bf16[48,2304]{1,0:T(8,128)(2,1)}, u32[]{:S(2)}, u32[]{:S(2)}) collective-permute-start(bf16[48,2304]{1,0:T(8,128)(2,1)} %get-tuple-element.206), channel_id=1, source_target_pairs={{0,24},{2,26},{4,28},{6,30},{8,16},{10,18},{12,20},{14,22},{16,8},... | collective-permute-start | bytes 663560 | tf_op jit(solution)/shard_map/ppermute | solution.py:1112
  569.8 22.3 %collective-permute-start.27 = (bf16[48,2304]{1,0:T(8,128)(2,1)}, bf16[48,2304]{1,0:T(8,128)(2,1)}, u32[]{:S(2)}, u32[]{:S(2)}) collective-permute-start(bf16[48,2304]{1,0:T(8,128)(2,1)} %get-tuple-element.207), channel_id=1, source_target_pairs={{0,16},{2,18},{4,20},{6,22},{8,24},{10,26},{12,28},{14,30},{16,0},... | collective-permute-start | bytes 663560 | tf_op jit(solution)/shard_map/ppermute | solution.py:1112
  569.8 22.3 %collective-permute-start.26 = (bf16[48,2304]{1,0:T(8,128)(2,1)}, bf16[48,2304]{1,0:T(8,128)(2,1)}, u32[]{:S(2)}, u32[]{:S(2)}) collective-permute-start(bf16[48,2304]{1,0:T(8,128)(2,1)} %get-tuple-element.208), channel_id=1, source_target_pairs={{0,8},{2,10},{4,12},{6,14},{8,0},{10,2},{12,4},{14,6},{16,24},{18,... | collective-permute-start | bytes 663560 | tf_op jit(solution)/shard_map/ppermute | solution.py:1112
  572.9 16.8 %collective-permute-start.35 = (bf16[24,3072]{1,0:T(8,128)(2,1)}, bf16[24,3072]{1,0:T(8,128)(2,1)}, u32[]{:S(2)}, u32[]{:S(2)}) collective-permute-start(bf16[24,3072]{1,0:T(8,128)(2,1)} %dynamic-slice_bitcast_fusion.12), channel_id=1, source_target_pairs={{0,1},{1,0},{2,3},{3,2},{4,5},{5,4},{6,7},{7,6},{8,9},{9,8},{10,11... | collective-permute-start | bytes 442376 | tf_op jit(solution)/shard_map/ppermute | solution.py:1107
  574.3 19.1 %collective-permute-start.29 = (bf16[4,48,896]{2,1,0:T(8,128)(2,1)}, bf16[4,48,896]{2,1,0:T(8,128)(2,1)}, u32[]{:S(2)}, u32[]{:S(2)}) collective-permute-start(bf16[4,48,896]{2,1,0:T(8,128)(2,1)} %fusion.6), channel_id=1, source_target_pairs={{0,4},{2,6},{4,0},{6,2},{8,12},{10,14},{12,8},{14,10},{16,20},{18,... | collective-permute-start | bytes 1032200 | tf_op jit(solution)/shard_map/ppermute | solution.py:1112
  587.2 4.9 copy-start.9
  587.2 6.2 %copy-start.2 = (bf16[8,48,896]{2,1,0:T(8,128)(2,1)S(1)}, bf16[8,48,896]{2,1,0:T(8,128)(2,1)}, u32[]{:S(2)}) copy-start(bf16[8,48,896]{2,1,0:T(8,128)(2,1)} %copy-done.1) | copy-start | bytes 2064388
  589.7 3.7 copy-start.12
  594.6 5.9 collective-permute-start.30
  595.6 6.8 %collective-permute-start.32 = (bf16[48,896]{1,0:T(8,128)(2,1)S(1)}, bf16[48,896]{1,0:T(8,128)(2,1)S(1)}, u32[]{:S(2)}, u32[]{:S(2)}) collective-permute-start(bf16[48,896]{1,0:T(8,128)(2,1)S(1)} %get-tuple-element.222), channel_id=1, source_target_pairs={{0,24},{2,26},{4,28},{6,30},{8,16},{10,18},{12,20},{14,22},{16,8},... | collective-permute-start | bytes 258056 | tf_op jit(solution)/shard_map/ppermute | solution.py:1112
  598.0 7.0 %collective-permute-start.31 = (bf16[48,896]{1,0:T(8,128)(2,1)S(1)}, bf16[48,896]{1,0:T(8,128)(2,1)S(1)}, u32[]{:S(2)}, u32[]{:S(2)}) collective-permute-start(bf16[48,896]{1,0:T(8,128)(2,1)S(1)} %get-tuple-element.223), channel_id=1, source_target_pairs={{0,16},{2,18},{4,20},{6,22},{8,24},{10,26},{12,28},{14,30},{16,0},... | collective-permute-start | bytes 258056 | tf_op jit(solution)/shard_map/ppermute | solution.py:1112
  598.5 8.1 %collective-permute-start.34 = (bf16[24,2304]{1,0:T(8,128)(2,1)S(1)}, bf16[24,2304]{1,0:T(8,128)(2,1)S(1)}, u32[]{:S(2)}, u32[]{:S(2)}) collective-permute-start(bf16[24,2304]{1,0:T(8,128)(2,1)S(1)} %dynamic-slice_bitcast_fusion.13), channel_id=1, source_target_pairs={{0,1},{1,0},{2,3},{3,2},{4,5},{5,4},{6,7},{7,6},{8,9},{9,8},{10,11... | collective-permute-start | bytes 331784 | tf_op jit(solution)/shard_map/ppermute | solution.py:1107
  605.1 4.1 collective-permute-start.33
  (1 other events, 0.8 us)
Sparse Core Ops, SparseCore 0:
  19.2 141.5 all-gather.1
  338.4 156.0 reduce-scatter.1

commit v5 on v4

--- a/solution.py
+++ b/solution.py
@@ -1222,22 +1222,27 @@
     packed = jnp.concatenate(
         [time_proj, time_out, up_order.reshape(share, -1), down_order.reshape(share, -1)], axis=1
     )
-    first, second, by_place, packed = tie(first, second, tokens.transpose(0, 2, 1, 3), packed)
+    first, second, by_place, g_place, tokens, packed = tie(
+        first, second, tokens.transpose(0, 2, 1, 3), cotangent.transpose(0, 2, 1, 3), tokens, packed
+    )
     packed = lax.all_gather(packed, axes, axis=0, tiled=True)
     half = by_place.shape[1] // 2
     send = pick(by_place, 1 - place, 0)
     rest_a = swap_axis(send[:half], "frame")
     first = collect_lines(first)
-    second, first, rest_a, send = tie(second, first, rest_a, send)
+    own, g_own, g_send = (
+        pick(tokens, place, 0), pick(g_place, place, 0), pick(g_place, 1 - place, 0)
+    )
+    second, first, rest_a, send, own, g_own, g_send = tie(
+        second, first, rest_a, send, own, g_own, g_send
+    )
     rest_b = swap_axis(send[half:], "frame")
     second = collect_lines(second)
     first = collect_half(first, 2, 1)
-    own = pick(tokens, place, 0)
-    g_own = pick(cotangent.transpose(0, 2, 1, 3), place, 0)
-    first, second, own, g_own = tie(first, second, own, g_own)
+    first, second = tie(first, second)
     second = collect_half(second, 2, 1)
-    second, rest_b, g_send = tie(second, rest_b, cotangent.transpose(0, 2, 1, 3))
-    g_rest = swap_axis(pick(g_send, 1 - place, 0), "frame")
+    second, rest_b, g_send = tie(second, rest_b, g_send)
+    g_rest = swap_axis(g_send, "frame")
     first = merged(collect_half(first, 1, 2))
     second = merged(collect_half(second, 1, 2))
     rest = jnp.concatenate([rest_a, rest_b], axis=0).transpose(1, 0, 2)

time: 625 us -> 622 us (level)
  waiting for transfers between devices: 93.9 us -> 86.8 us
    ppermute x11, waiting for transfers between devices: 28.4 us -> 16.8 us  [swap_axis(): lax.ppermute(values, axis, [(index, size - 1 - index) for index in range(...]
  transfers between devices with their start and end apart: 38 -> 38, of which waited for: 16 -> 14; matrix products, arithmetic and copies ran while one was open for 11% -> 11% of each run, Pallas kernels for 37% -> 37%
where the time goes in v5:
time: 622 us; the launch traced here: 615 us
  Pallas kernels  393 us (63%)
  waiting for transfers between devices  86.8 us (14%)
  local copies, waits for them, and re-layouts  45.2 us (7%)
  starting transfers between devices  42 us (7%)
  other arithmetic  33.2 us (5%)
  between operations  15.2 us (2%)
    pallas_call x1, Pallas kernels, middle(): pl.pallas_call(functools.partial(middle_kernel, places), grid_spec=pltpu....  125 us
    pallas_call x2, Pallas kernels, space_backward(): pl.pallas_call(functools.partial(space_backward_kernel, places), grid_spe...  77.7 us
    ppermute x25, waiting for transfers between devices, flip(): lax.ppermute(values, 'clip', [(index, index ^ mask) for index in range(si...  69.9 us
    pallas_call x1, Pallas kernels, time_backward(): pl.pallas_call(time_backward_kernel, grid=(groups // 2,), in_specs=[by_ro...  54.5 us
    pallas_call x2, Pallas kernels, space_forward(): pl.pallas_call(functools.partial(space_forward_kernel, places), grid=(fra...  45.3 us
    pallas_call x1, Pallas kernels, feed_gradient(): pl.pallas_call(functools.partial(feed_gradient_kernel, turns), grid=(coun...  39.2 us
    pallas_call x2, Pallas kernels, split_gradient(): pl.pallas_call(functools.partial(gradient_kernel, parts, tiles), grid_spe...  28.6 us
    ppermute x25, starting transfers between devices, flip(): lax.ppermute(values, 'clip', [(index, index ^ mask) for index in range(si...  28 us
  transfers between devices with their start and end apart: 38, of which 14 were waited for; matrix products, arithmetic and copies ran while one was open for 11% of the time, Pallas kernels for 37%

profile of v5, /device:TPU:0, one launch (start us, length us, event | category | flops | bytes accessed | tf_op | source)
XLA Modules:
  0.0 614.9 jit_solution(7741812632678861360)
XLA Ops:
  9.6 3.0 collective-permute-start.1
  14.6 2.1 reshape.152
  16.9 1.3 reshape.153
  19.1 2.4 dynamic-slice_bitcast_fusion.3
  21.5 2.0 collective-permute-start.5
  23.5 3.6 collective-permute-start.4
  27.9 6.1 dynamic-slice_bitcast_fusion
  34.3 2.0 copy.101
  36.2 12.0 %collective-permute-done.3 = bf16[2,24,1536]{2,1,0:T(8,128)(2,1)S(1)} collective-permute-done((bf16[2,24,1536]{2,1,0:T(8,128)(2,1)S(1)}, bf16[2,24,1536]{2,1,0:T(8,128)(2,1)S(1)}, u32[]{:S(2)}, u32[]{:S(2)}) %collective-permute-start.3) | collective-permute-done | bytes 147488 | tf_op jit(solution)/shard_map/ppermute | solution.py:1112
  48.4 4.5 collective-permute-done.5
  52.9 3.8 collective-permute-start.9
  57.4 1.8 collective-permute-start.6
  59.2 1.5 collective-permute-start.11
  60.7 4.2 collective-permute-done.9
  65.0 20.2 %collective-permute-done.8 = bf16[2,24,1664]{2,1,0:T(8,128)(2,1)S(1)} collective-permute-done((bf16[2,24,1664]{2,1,0:T(8,128)(2,1)S(1)}, bf16[2,24,1664]{2,1,0:T(8,128)(2,1)S(1)}, u32[]{:S(2)}, u32[]{:S(2)}) %collective-permute-start.8) | collective-permute-done | bytes 159776 | tf_op jit(solution)/shard_map/ppermute | solution.py:1112
  86.5 1.6 collective-permute-start.10
  88.1 20.4 %collective-permute-done.10 = bf16[4,2,24,1664]{3,2,1,0:T(8,128)(2,1)S(1)} collective-permute-done((bf16[4,2,24,1664]{3,2,1,0:T(8,128)(2,1)S(1)}, bf16[4,2,24,1664]{3,2,1,0:T(8,128)(2,1)S(1)}, u32[]{:S(2)}, u32[]{:S(2)}) %collective-permute-start.10) | collective-permute-done | bytes 639008 | tf_op jit(solution)/shard_map/ppermute | solution.py:1112
  108.8 1.4 collective-permute-start.14
  110.2 1.5 copy.74
  111.7 1.5 copy.75
  113.2 1.8 maximum_bitcast_fusion.x_ref
  115.0 2.1 maximum_select_fusion.1
  117.1 1.6 copy.72
  118.7 2.3 maximum_select_fusion
  121.2 1.3 fusion.14
  122.5 1.7 copy.78.fgain_ref
  125.7 22.5 %space_forward.2 = (bf16[8,208,768]{2,1,0:T(8,128)(2,1)}, bf16[8,208,2304]{2,1,0:T(8,128)(2,1)}, bf16[8,208,768]{2,1,0:T(8,128)(2,1)}, f32[26,8,8,768]{3,2,1,0:T(8,128)}) custom-call(bf16[8,196,768]{2,1,0:T(8,128)(2,1)} %bitcast.176, f32[1,768]{1,0:T(1,128)} %copy.73.gain_ref.gain_row_ref, bf16[768,1536]{1,0:T(8,128)(2,1)} %bitcast.172, ...), custom_call_target="tpu_custom_call" | custom-call | flops 1663041536 | bytes 4202496 | tf_op jit(solution)/shard_map/space_forward/pallas_call | solution.py:473
  148.2 22.8 %space_forward.3 = (bf16[8,208,768]{2,1,0:T(8,128)(2,1)}, bf16[8,208,2304]{2,1,0:T(8,128)(2,1)}, bf16[8,208,768]{2,1,0:T(8,128)(2,1)}, f32[26,8,8,768]{3,2,1,0:T(8,128)}) custom-call(bf16[8,196,768]{2,1,0:T(8,128)(2,1)} %maximum_bitcast_fusion.x_ref, f32[1,768]{1,0:T(1,128)} %copy.73.gain_ref.gain_row_ref, bf16[768,1536]{1,0:T(8,128)(2,1)} %bitcast.173, ...), custom_call_target="tpu_custom_call" | custom-call | flops 1663041536 | bytes 4202496 | tf_op jit(solution)/shard_map/space_forward/pallas_call | solution.py:473
  171.0 1.4 collective-permute-done.14.gr_ref
  172.4 124.9 %middle.1 = (bf16[3328,2304]{1,0:T(8,128)(2,1)}, bf16[3328,1536]{1,0:T(8,128)(2,1)}, bf16[3328,1536]{1,0:T(8,128)(2,1)}, bf16[3328,6144]{1,0:T(8,128)(2,1)}, bf1...) custom-call(s32[1]{0:T(128)} %bitcast.38.place_ref, ...), custom_call_target="tpu_custom_call" | custom-call | flops 13522436096 | bytes 18198528 | tf_op jit(solution)/shard_map/middle/pallas_call | solution.py:519
  297.3 39.2 %feed_gradient.1 = bf16[768,6144]{1,0:T(8,128)(2,1)} custom-call(bf16[3328,1536]{1,0:T(8,128)(2,1)} %get-tuple-element.134.narrow_ref, bf16[3328,6144]{1,0:T(8,128)(2,1)} %get-tuple-element.135.wide_ref), custom_call_target="tpu_custom_call" | custom-call | flops 5234491392 | bytes 10092544 | tf_op jit(solution)/shard_map/feed_gradient/pallas_call | solution.py:705
  336.6 1.7 copy-done.16
  338.6 54.5 %time_backward.1 = (bf16[3328,3072]{1,0:T(8,128)(2,1)}, f32[8,208,768]{2,1,0:T(8,128)}, f32[8,208,768]{2,1,0:T(8,128)}, f32[8,768]{1,0:T(8,128)}) custom-call(bf16[3328,2304]{1,0:T(8,128)(2,1)} %get-tuple-element.133.qkv_ref, f32[3328,768]{1,0:T(8,128)} %get-tuple-element.137.gt_ref, f32[26,8,8,768]{3,2,1,0:T(8,128)} %get-tuple-element.124.ao_ref, ...), custom_call_target="tpu_custom_call" | custom-call | flops 3707764736 | bytes 11079680 | tf_op jit(solution)/shard_map/time_backward/pallas_call | solution.py:567
  393.0 22.4 %time_gradient.1 = (bf16[8,48,3072]{2,1,0:T(8,128)(2,1)}, bf16[8,48,3072]{2,1,0:T(8,128)(2,1)}) custom-call(s32[1]{0:T(128)} %bitcast.core_ref, bf16[3328,1536]{1,0:T(8,128)(2,1)} %get-tuple-element.132.narrow_ref, bf16[3328,3072]{1,0:T(8,128)(2,1)} %get-tuple-element.138.wide_ref), custom_call_target="tpu_custom_call" | custom-call | flops 2617245696 | bytes 5898240 | tf_op jit(solution)/shard_map/time_gradient/pallas_call | solution.py:734
  415.5 4.7 collective-permute-done.16
  420.2 2.7 fusion.1
  422.9 1.6 collective-permute-start.17
  424.5 38.6 %space_backward.2 = (bf16[8,208,2304]{2,1,0:T(8,128)(2,1)}, bf16[8,208,768]{2,1,0:T(8,128)(2,1)}, bf16[196,8,768]{2,1,0:T(8,128)(2,1)}, f32[8,768]{1,0:T(8,128)}) custom-call(s32[1]{0:T(128)} %bitcast.38.place_ref, bf16[8,196,768]{2,1,0:T(8,128)(2,1)} %maximum_bitcast_fusion.x_ref, f32[8,208,768]{2,1,0:T(8,128)} %get-tuple-element.146.gs_ref, ...), custom_call_target="tpu_custom_call" | custom-call | flops 2194669568 | bytes 4640768 | tf_op jit(solution)/shard_map/space_backward/pallas_call | solution.py:599
  463.1 3.4 fusion.13
  466.5 1.5 collective-permute-start.21
  468.9 3.2 collective-permute-start.20
  472.1 1.2 collective-permute-start.18
  473.4 39.1 %space_backward.3 = (bf16[8,208,2304]{2,1,0:T(8,128)(2,1)}, bf16[8,208,768]{2,1,0:T(8,128)(2,1)}, f32[2,196,8,768]{3,2,1,0:T(8,128)}, f32[8,768]{1,0:T(8,128)}) custom-call(s32[1]{0:T(128)} %bitcast.38.place_ref, bf16[8,196,768]{2,1,0:T(8,128)(2,1)} %bitcast.177, f32[8,208,768]{2,1,0:T(8,128)} %get-tuple-element.151.gs_ref, ...), custom_call_target="tpu_custom_call" | custom-call | flops 2194669568 | bytes 5844992 | tf_op jit(solution)/shard_map/space_backward/pallas_call | solution.py:599
  512.6 19.1 %split_gradient.2 = (bf16[8,48,2304]{2,1,0:T(8,128)(2,1)}, bf16[8,48,2304]{2,1,0:T(8,128)(2,1)}) custom-call(s32[1]{0:T(128)} %bitcast.core_ref, bf16[1664,768]{1,0:T(8,128)(2,1)} %bitcast.193, bf16[1664,2304]{1,0:T(8,128)(2,1)} %bitcast.179, bf16[1664,768]{1,0:T(8,128)(2,1)} %bitcast.194, bf16[1664,2304]{1,0:T(8,128)(2,1)} %bitcast.178), custom_call_target="tpu_custom_call" | custom-call | flops 1962934272 | bytes 3997696 | tf_op jit(solution)/shard_map/split_gradient/pallas_call | solution.py:751
  532.9 3.0 collective-permute-done.22
  535.9 2.6 fusion.3
  538.4 1.4 fusion.2
  540.5 9.5 %split_gradient.3 = (bf16[8,48,768]{2,1,0:T(8,128)(2,1)}, bf16[8,48,768]{2,1,0:T(8,128)(2,1)}) custom-call(s32[1]{0:T(128)} %bitcast.core_ref, bf16[1664,768]{1,0:T(8,128)(2,1)} %bitcast.191, bf16[1664,768]{1,0:T(8,128)(2,1)} %bitcast.196, bf16[1664,768]{1,0:T(8,128)(2,1)} %bitcast.192, bf16[1664,768]{1,0:T(8,128)(2,1)} %bitcast.195), custom_call_target="tpu_custom_call" | custom-call | flops 654311424 | bytes 1900544 | tf_op jit(solution)/shard_map/split_gradient/pallas_call | solution.py:751
  552.3 8.9 %collective-permute-done.25 = bf16[98,8,768]{2,1,0:T(8,128)(2,1)} collective-permute-done((bf16[98,8,768]{2,1,0:T(8,128)(2,1)}, bf16[98,8,768]{2,1,0:T(8,128)(2,1)}, u32[]{:S(2)}, u32[]{:S(2)}) %collective-permute-start.25) | collective-permute-done | bytes 1204256 | tf_op jit(solution)/shard_map/ppermute | solution.py:1107
  562.9 3.2 collective-permute-start.28
  567.3 1.3 add_convert_fusion.8
  569.8 1.8 fusion.6
  572.2 2.9 convert_dynamic-update-slice_fusion.1
  575.1 3.3 bitcast_dynamic-update-slice_fusion
  578.3 2.9 convert_dynamic-update-slice_fusion
  583.2 1.2 copy.87
  584.5 2.6 reshape.171
  589.4 1.3 add_convert_fusion.9
  592.9 2.4 collective-permute-start.32
  595.9 1.5 collective-permute-start.34
  597.8 1.8 collective-permute-done.32
  599.6 2.6 collective-permute-done.31
  602.2 1.5 collective-permute-start.33
  604.4 1.9 collective-permute-done.33
  (145 shorter events, 30.2 us)
Async XLA Ops:
  7.2 11.0 %copy-start.11 = (bf16[24,768]{1,0:T(8,128)(2,1)S(1)}, bf16[24,768]{1,0:T(8,128)(2,1)}, u32[]{:S(2)}) copy-start(bf16[24,768]{1,0:T(8,128)(2,1)} %param.19) | copy-start | bytes 110596
  7.2 11.0 %copy-start.10 = (bf16[24,2304]{1,0:T(8,128)(2,1)S(1)}, bf16[24,2304]{1,0:T(8,128)(2,1)}, u32[]{:S(2)}) copy-start(bf16[24,2304]{1,0:T(8,128)(2,1)} %param.18) | copy-start | bytes 331780
  7.2 165.2 %all-gather.2.cloned.1.call-start = ((), (), s32[]{:S(2)}) async-start(), calls=%async_computation.1 | async-start | bytes 14598144 | tf_op jit(solution)/shard_map/all_gather | solution.py:1228
  9.6 9.4 %collective-permute-start.1 = (bf16[24,1664]{1,0:T(8,128)(2,1)S(1)}, bf16[24,1664]{1,0:T(8,128)(2,1)S(1)}, u32[]{:S(2)}, u32[]{:S(2)}) collective-permute-start(bf16[24,1664]{1,0:T(8,128)(2,1)S(1)} %get-tuple-element.239), channel_id=1, source_target_pairs={{0,1},{1,0},{2,3},{3,2},{4,5},{5,4},{6,7},{7,6},{8,9},{9,8},{10,11... | collective-permute-start | bytes 239624 | tf_op jit(solution)/shard_map/ppermute | solution.py:1107
  13.5 5.4 collective-permute-start
  19.1 542.7 %reduce-scatter.2.cloned.1.call-start = ((), (), s32[]{:S(2)}) async-start(), calls=%async_computation.2 | async-start | bytes 9732096 | tf_op jit(solution)/shard_map/reduce_scatter | solution.py:1259
  21.5 31.4 %collective-permute-start.5 = (bf16[98,8,768]{2,1,0:T(8,128)(2,1)}, bf16[98,8,768]{2,1,0:T(8,128)(2,1)}, u32[]{:S(2)}, u32[]{:S(2)}) collective-permute-start(bf16[98,8,768]{2,1,0:T(8,128)(2,1)} %dynamic-slice_bitcast_fusion.3), channel_id=1, source_target_pairs={{0,1},{1,0},{2,3},{3,2},{4,5},{5,4},{6,7},{7,6},{8,9},{9,8},{10,11... | collective-permute-start | bytes 3612680 | tf_op jit(solution)/shard_map/ppermute | solution.py:1107
  23.5 10.5 %slice-start = ((s8[4816896]{0:T(1024)(128)(4,1)}), s8[622592]{0:T(1024)(128)(4,1)S(1)}, s32[]{:S(2)}) async-start(s8[4816896]{0:T(1024)(128)(4,1)} %bitcast.182), calls=%async_computation.3 | async-start | bytes 1245184
  23.5 10.5 %slice-start.1 = ((s8[4816896]{0:T(1024)(128)(4,1)}), s8[4194304]{0:T(1024)(128)(4,1)S(1)}, s32[]{:S(2)}) async-start(s8[4816896]{0:T(1024)(128)(4,1)} %bitcast.182), calls=%async_computation.4 | async-start | bytes 8388608
  23.5 12.7 %collective-permute-start.4 = (bf16[2,24,1536]{2,1,0:T(8,128)(2,1)S(1)}, bf16[2,24,1536]{2,1,0:T(8,128)(2,1)S(1)}, u32[]{:S(2)}, u32[]{:S(2)}) collective-permute-start(bf16[2,24,1536]{2,1,0:T(8,128)(2,1)S(1)} %maximum_select_fusion.5), channel_id=1, source_target_pairs={{0,24},{2,26},{4,28},{6,30},{8,16},{10,18},{12,20},{14,22},{16,8},... | collective-permute-start | bytes 442376 | tf_op jit(solution)/shard_map/ppermute | solution.py:1112
  27.1 21.1 %collective-permute-start.3 = (bf16[2,24,1536]{2,1,0:T(8,128)(2,1)S(1)}, bf16[2,24,1536]{2,1,0:T(8,128)(2,1)S(1)}, u32[]{:S(2)}, u32[]{:S(2)}) collective-permute-start(bf16[2,24,1536]{2,1,0:T(8,128)(2,1)S(1)} %maximum_select_fusion.5), channel_id=1, source_target_pairs={{0,16},{2,18},{4,20},{6,22},{8,24},{10,26},{12,28},{14,30},{16,0},... | collective-permute-start | bytes 442376 | tf_op jit(solution)/shard_map/ppermute | solution.py:1112
  27.1 21.1 %collective-permute-start.2 = (bf16[2,24,1536]{2,1,0:T(8,128)(2,1)S(1)}, bf16[2,24,1536]{2,1,0:T(8,128)(2,1)S(1)}, u32[]{:S(2)}, u32[]{:S(2)}) collective-permute-start(bf16[2,24,1536]{2,1,0:T(8,128)(2,1)S(1)} %maximum_select_fusion.5), channel_id=1, source_target_pairs={{0,8},{2,10},{4,12},{6,14},{8,0},{10,2},{12,4},{14,6},{16,24},{18,... | collective-permute-start | bytes 442376 | tf_op jit(solution)/shard_map/ppermute | solution.py:1112
  52.9 12.0 %collective-permute-start.9 = (bf16[2,24,1664]{2,1,0:T(8,128)(2,1)S(1)}, bf16[2,24,1664]{2,1,0:T(8,128)(2,1)S(1)}, u32[]{:S(2)}, u32[]{:S(2)}) collective-permute-start(bf16[2,24,1664]{2,1,0:T(8,128)(2,1)S(1)} %maximum_select_fusion.4), channel_id=1, source_target_pairs={{0,24},{2,26},{4,28},{6,30},{8,16},{10,18},{12,20},{14,22},{16,8},... | collective-permute-start | bytes 479240 | tf_op jit(solution)/shard_map/ppermute | solution.py:1112
  56.8 28.4 %collective-permute-start.8 = (bf16[2,24,1664]{2,1,0:T(8,128)(2,1)S(1)}, bf16[2,24,1664]{2,1,0:T(8,128)(2,1)S(1)}, u32[]{:S(2)}, u32[]{:S(2)}) collective-permute-start(bf16[2,24,1664]{2,1,0:T(8,128)(2,1)S(1)} %maximum_select_fusion.4), channel_id=1, source_target_pairs={{0,16},{2,18},{4,20},{6,22},{8,24},{10,26},{12,28},{14,30},{16,0},... | collective-permute-start | bytes 479240 | tf_op jit(solution)/shard_map/ppermute | solution.py:1112
  56.8 28.4 %collective-permute-start.7 = (bf16[2,24,1664]{2,1,0:T(8,128)(2,1)S(1)}, bf16[2,24,1664]{2,1,0:T(8,128)(2,1)}, u32[]{:S(2)}, u32[]{:S(2)}) collective-permute-start(bf16[2,24,1664]{2,1,0:T(8,128)(2,1)S(1)} %maximum_select_fusion.4), channel_id=1, source_target_pairs={{0,8},{2,10},{4,12},{6,14},{8,0},{10,2},{12,4},{14,6},{16,24},{18,... | collective-permute-start | bytes 479240 | tf_op jit(solution)/shard_map/ppermute | solution.py:1112
  57.4 28.8 %collective-permute-start.6 = (bf16[4,2,24,1536]{3,2,1,0:T(8,128)(2,1)S(1)}, bf16[4,2,24,1536]{3,2,1,0:T(8,128)(2,1)S(1)}, u32[]{:S(2)}, u32[]{:S(2)}) collective-permute-start(bf16[4,2,24,1536]{3,2,1,0:T(8,128)(2,1)S(1)} %pad_maximum_fusion.3), channel_id=1, source_target_pairs={{0,4},{2,6},{4,0},{6,2},{8,12},{10,14},{12,8},{14,10},{16,20},{18,... | collective-permute-start | bytes 1769480 | tf_op jit(solution)/shard_map/ppermute | solution.py:1112
  59.2 49.5 %collective-permute-start.11 = (bf16[98,8,768]{2,1,0:T(8,128)(2,1)S(1)}, bf16[98,8,768]{2,1,0:T(8,128)(2,1)}, u32[]{:S(2)}, u32[]{:S(2)}) collective-permute-start(bf16[98,8,768]{2,1,0:T(8,128)(2,1)S(1)} %slice.61), channel_id=1, source_target_pairs={{0,1},{1,0},{2,3},{3,2},{4,5},{5,4},{6,7},{7,6},{8,9},{9,8},{10,11... | collective-permute-start | bytes 3612680 | tf_op jit(solution)/shard_map/ppermute | solution.py:1107
  86.5 22.0 %collective-permute-start.10 = (bf16[4,2,24,1664]{3,2,1,0:T(8,128)(2,1)S(1)}, bf16[4,2,24,1664]{3,2,1,0:T(8,128)(2,1)S(1)}, u32[]{:S(2)}, u32[]{:S(2)}) collective-permute-start(bf16[4,2,24,1664]{3,2,1,0:T(8,128)(2,1)S(1)} %pad_maximum_fusion.2), channel_id=1, source_target_pairs={{0,4},{2,6},{4,0},{6,2},{8,12},{10,14},{12,8},{14,10},{16,20},{18,... | collective-permute-start | bytes 1916936 | tf_op jit(solution)/shard_map/ppermute | solution.py:1112
  88.1 26.9 %collective-permute-start.13 = (bf16[4,2,2,24,1536]{4,3,2,0,1:T(8,128)(2,1)S(1)}, bf16[4,2,2,24,1536]{4,3,2,0,1:T(8,128)(2,1)}, u32[]{:S(2)}, u32[]{:S(2)}) collective-permute-start(bf16[4,2,2,24,1536]{4,3,2,0,1:T(8,128)(2,1)S(1)} %maximum_select_fusion.3), channel_id=1, source_target_pairs={{0,2},{2,0},{4,6},{6,4},{8,10},{10,8},{12,14},{14,12},{16,18},{18,... | collective-permute-start | bytes 3538952 | tf_op jit(solution)/shard_map/ppermute | solution.py:1112
  108.7 10.0 %collective-permute-start.12 = (bf16[4,2,2,24,1664]{4,3,2,0,1:T(8,128)(2,1)S(1)}, bf16[4,2,2,24,1664]{4,3,2,0,1:T(8,128)(2,1)}, u32[]{:S(2)}, u32[]{:S(2)}) collective-permute-start(bf16[4,2,2,24,1664]{4,3,2,0,1:T(8,128)(2,1)S(1)} %maximum_select_fusion.2), channel_id=1, source_target_pairs={{0,2},{2,0},{4,6},{6,4},{8,10},{10,8},{12,14},{14,12},{16,18},{18,... | collective-permute-start | bytes 3833864 | tf_op jit(solution)/shard_map/ppermute | solution.py:1112
  108.8 63.6 %collective-permute-start.14 = (bf16[196,8,768]{2,1,0:T(8,128)(2,1)}, bf16[196,8,768]{2,1,0:T(8,128)(2,1)}, u32[]{:S(2)}, u32[]{:S(2)}) collective-permute-start(bf16[196,8,768]{2,1,0:T(8,128)(2,1)} %get-tuple-element.125), channel_id=1, source_target_pairs={{0,1},{1,0},{2,3},{3,2},{4,5},{5,4},{6,7},{7,6},{8,9},{9,8},{10,11... | collective-permute-start | bytes 7225352 | tf_op jit(solution)/shard_map/ppermute | solution.py:1107
  121.2 4.5 copy-start
  336.6 1.7 copy-start.16
  338.2 77.2 %collective-permute-start.15 = (bf16[196,8,768]{2,1,0:T(8,128)(2,1)S(1)}, bf16[196,8,768]{2,1,0:T(8,128)(2,1)}, u32[]{:S(2)}, u32[]{:S(2)}) collective-permute-start(bf16[196,8,768]{2,1,0:T(8,128)(2,1)S(1)} %copy-done.16), channel_id=1, source_target_pairs={{0,1},{1,0},{2,3},{3,2},{4,5},{5,4},{6,7},{7,6},{8,9},{9,8},{10,11... | collective-permute-start | bytes 7225352 | tf_op jit(solution)/shard_map/ppermute | solution.py:1107
  415.5 4.7 collective-permute-start.16
  422.9 45.5 %collective-permute-start.17 = (bf16[4,48,3072]{2,1,0:T(8,128)(2,1)}, bf16[4,48,3072]{2,1,0:T(8,128)(2,1)S(1)}, u32[]{:S(2)}, u32[]{:S(2)}) collective-permute-start(bf16[4,48,3072]{2,1,0:T(8,128)(2,1)} %fusion.1), channel_id=1, source_target_pairs={{0,4},{2,6},{4,0},{6,2},{8,12},{10,14},{12,8},{14,10},{16,20},{18,... | collective-permute-start | bytes 3538952 | tf_op jit(solution)/shard_map/ppermute | solution.py:1112
  463.1 4.9 copy-start.3
  466.5 46.0 %collective-permute-start.21 = (bf16[98,8,768]{2,1,0:T(8,128)(2,1)}, bf16[98,8,768]{2,1,0:T(8,128)(2,1)}, u32[]{:S(2)}, u32[]{:S(2)}) collective-permute-start(bf16[98,8,768]{2,1,0:T(8,128)(2,1)} %get-tuple-element.209), channel_id=1, source_target_pairs={{0,1},{1,0},{2,3},{3,2},{4,5},{5,4},{6,7},{7,6},{8,9},{9,8},{10,11... | collective-permute-start | bytes 3612680 | tf_op jit(solution)/shard_map/ppermute | solution.py:1107
  468.9 43.6 %collective-permute-start.20 = (bf16[48,3072]{1,0:T(8,128)(2,1)S(1)}, bf16[48,3072]{1,0:T(8,128)(2,1)S(1)}, u32[]{:S(2)}, u32[]{:S(2)}) collective-permute-start(bf16[48,3072]{1,0:T(8,128)(2,1)S(1)} %get-tuple-element.210), channel_id=1, source_target_pairs={{0,24},{2,26},{4,28},{6,30},{8,16},{10,18},{12,20},{14,22},{16,8},... | collective-permute-start | bytes 884744 | tf_op jit(solution)/shard_map/ppermute | solution.py:1112
  472.1 40.4 %collective-permute-start.19 = (bf16[48,3072]{1,0:T(8,128)(2,1)S(1)}, bf16[48,3072]{1,0:T(8,128)(2,1)S(1)}, u32[]{:S(2)}, u32[]{:S(2)}) collective-permute-start(bf16[48,3072]{1,0:T(8,128)(2,1)S(1)} %get-tuple-element.211), channel_id=1, source_target_pairs={{0,16},{2,18},{4,20},{6,22},{8,24},{10,26},{12,28},{14,30},{16,0},... | collective-permute-start | bytes 884744 | tf_op jit(solution)/shard_map/ppermute | solution.py:1112
  472.1 40.4 %collective-permute-start.18 = (bf16[48,3072]{1,0:T(8,128)(2,1)S(1)}, bf16[48,3072]{1,0:T(8,128)(2,1)S(1)}, u32[]{:S(2)}, u32[]{:S(2)}) collective-permute-start(bf16[48,3072]{1,0:T(8,128)(2,1)S(1)} %get-tuple-element.212), channel_id=1, source_target_pairs={{0,8},{2,10},{4,12},{6,14},{8,0},{10,2},{12,4},{14,6},{16,24},{18,... | collective-permute-start | bytes 884744 | tf_op jit(solution)/shard_map/ppermute | solution.py:1112
  512.5 19.2 %copy-start.7 = (bf16[48,3072]{1,0:T(8,128)(2,1)}, bf16[48,3072]{1,0:T(8,128)(2,1)S(1)}, u32[]{:S(2)}) copy-start(bf16[48,3072]{1,0:T(8,128)(2,1)S(1)} %collective-permute-done.20) | copy-start | bytes 884740
  512.5 19.2 %copy-start.8 = (bf16[48,3072]{1,0:T(8,128)(2,1)}, bf16[48,3072]{1,0:T(8,128)(2,1)S(1)}, u32[]{:S(2)}) copy-start(bf16[48,3072]{1,0:T(8,128)(2,1)S(1)} %collective-permute-done.19) | copy-start | bytes 884740
  512.6 19.2 %copy-start.9 = (bf16[48,3072]{1,0:T(8,128)(2,1)}, bf16[48,3072]{1,0:T(8,128)(2,1)S(1)}, u32[]{:S(2)}) copy-start(bf16[48,3072]{1,0:T(8,128)(2,1)S(1)} %collective-permute-done.18) | copy-start | bytes 884740
  512.6 19.3 %copy-start.14 = (f32[8,768]{1,0:T(8,128)S(1)}, f32[8,768]{1,0:T(8,128)}, u32[]{:S(2)}) copy-start(f32[8,768]{1,0:T(8,128)} %get-tuple-element.172) | copy-start | bytes 73732
  512.6 19.3 %copy-start.15 = (f32[8,768]{1,0:T(8,128)S(1)}, f32[8,768]{1,0:T(8,128)}, u32[]{:S(2)}) copy-start(f32[8,768]{1,0:T(8,128)} %get-tuple-element.171) | copy-start | bytes 73732
  512.6 20.0 %copy-start.12 = (f32[8,768]{1,0:T(8,128)S(1)}, f32[8,768]{1,0:T(8,128)}, u32[]{:S(2)}) copy-start(f32[8,768]{1,0:T(8,128)} %get-tuple-element.170) | copy-start | bytes 73732
  512.6 20.0 %copy-start.13 = (f32[8,768]{1,0:T(8,128)S(1)}, f32[8,768]{1,0:T(8,128)}, u32[]{:S(2)}) copy-start(f32[8,768]{1,0:T(8,128)} %get-tuple-element.169) | copy-start | bytes 73732
  531.8 6.7 %copy-start.4 = (bf16[8,48,2304]{2,1,0:T(8,128)(2,1)S(1)}, bf16[8,48,2304]{2,1,0:T(8,128)(2,1)}, u32[]{:S(2)}) copy-start(bf16[8,48,2304]{2,1,0:T(8,128)(2,1)} %get-tuple-element.159) | copy-start | bytes 5308420
  531.8 4.1 collective-permute-start.22
  531.9 29.3 %collective-permute-start.25 = (bf16[98,8,768]{2,1,0:T(8,128)(2,1)}, bf16[98,8,768]{2,1,0:T(8,128)(2,1)}, u32[]{:S(2)}, u32[]{:S(2)}) collective-permute-start(bf16[98,8,768]{2,1,0:T(8,128)(2,1)} %get-tuple-element.208), channel_id=1, source_target_pairs={{0,1},{1,0},{2,3},{3,2},{4,5},{5,4},{6,7},{7,6},{8,9},{9,8},{10,11... | collective-permute-start | bytes 3612680 | tf_op jit(solution)/shard_map/ppermute | solution.py:1107
  539.8 22.0 %collective-permute-start.23 = (bf16[4,48,2304]{2,1,0:T(8,128)(2,1)}, bf16[4,48,2304]{2,1,0:T(8,128)(2,1)S(1)}, u32[]{:S(2)}, u32[]{:S(2)}) collective-permute-start(bf16[4,48,2304]{2,1,0:T(8,128)(2,1)} %fusion.3), channel_id=1, source_target_pairs={{0,4},{2,6},{4,0},{6,2},{8,12},{10,14},{12,8},{14,10},{16,20},{18,... | collective-permute-start | bytes 2654216 | tf_op jit(solution)/shard_map/ppermute | solution.py:1112
  551.1 10.1 %collective-permute-start.24 = (bf16[8,48,896]{2,1,0:T(8,128)(2,1)S(1)}, bf16[8,48,896]{2,1,0:T(8,128)(2,1)}, u32[]{:S(2)}, u32[]{:S(2)}) collective-permute-start(bf16[8,48,896]{2,1,0:T(8,128)(2,1)S(1)} %pad_maximum_fusion.1), channel_id=1, source_target_pairs={{0,2},{2,0},{4,6},{6,4},{8,10},{10,8},{12,14},{14,12},{16,18},{18,... | collective-permute-start | bytes 2064392 | tf_op jit(solution)/shard_map/ppermute | solution.py:1112
  552.3 17.6 %copy-start.1 = (bf16[8,48,896]{2,1,0:T(8,128)(2,1)}, bf16[8,48,896]{2,1,0:T(8,128)(2,1)S(1)}, u32[]{:S(2)}) copy-start(bf16[8,48,896]{2,1,0:T(8,128)(2,1)S(1)} %pad_maximum_fusion) | copy-start | bytes 2064388
  562.0 10.2 %copy-start.5 = (bf16[24,6144]{1,0:T(8,128)(2,1)S(1)}, bf16[24,6144]{1,0:T(8,128)(2,1)}, u32[]{:S(2)}) copy-start(bf16[24,6144]{1,0:T(8,128)(2,1)} %reduce-scatter.2.cloned.1.call-done) | copy-start | bytes 884740
  562.9 26.4 %collective-permute-start.28 = (bf16[48,2304]{1,0:T(8,128)(2,1)}, bf16[48,2304]{1,0:T(8,128)(2,1)}, u32[]{:S(2)}, u32[]{:S(2)}) collective-permute-start(bf16[48,2304]{1,0:T(8,128)(2,1)} %get-tuple-element.214), channel_id=1, source_target_pairs={{0,24},{2,26},{4,28},{6,30},{8,16},{10,18},{12,20},{14,22},{16,8},... | collective-permute-start | bytes 663560 | tf_op jit(solution)/shard_map/ppermute | solution.py:1112
  566.1 23.3 %collective-permute-start.27 = (bf16[48,2304]{1,0:T(8,128)(2,1)}, bf16[48,2304]{1,0:T(8,128)(2,1)}, u32[]{:S(2)}, u32[]{:S(2)}) collective-permute-start(bf16[48,2304]{1,0:T(8,128)(2,1)} %get-tuple-element.215), channel_id=1, source_target_pairs={{0,16},{2,18},{4,20},{6,22},{8,24},{10,26},{12,28},{14,30},{16,0},... | collective-permute-start | bytes 663560 | tf_op jit(solution)/shard_map/ppermute | solution.py:1112
  566.1 23.3 %collective-permute-start.26 = (bf16[48,2304]{1,0:T(8,128)(2,1)}, bf16[48,2304]{1,0:T(8,128)(2,1)}, u32[]{:S(2)}, u32[]{:S(2)}) collective-permute-start(bf16[48,2304]{1,0:T(8,128)(2,1)} %get-tuple-element.216), channel_id=1, source_target_pairs={{0,8},{2,10},{4,12},{6,14},{8,0},{10,2},{12,4},{14,6},{16,24},{18,... | collective-permute-start | bytes 663560 | tf_op jit(solution)/shard_map/ppermute | solution.py:1112
  569.3 17.8 %collective-permute-start.35 = (bf16[24,3072]{1,0:T(8,128)(2,1)}, bf16[24,3072]{1,0:T(8,128)(2,1)}, u32[]{:S(2)}, u32[]{:S(2)}) collective-permute-start(bf16[24,3072]{1,0:T(8,128)(2,1)} %dynamic-slice_bitcast_fusion.12), channel_id=1, source_target_pairs={{0,1},{1,0},{2,3},{3,2},{4,5},{5,4},{6,7},{7,6},{8,9},{9,8},{10,11... | collective-permute-start | bytes 442376 | tf_op jit(solution)/shard_map/ppermute | solution.py:1107
  571.6 19.0 %collective-permute-start.29 = (bf16[4,48,896]{2,1,0:T(8,128)(2,1)}, bf16[4,48,896]{2,1,0:T(8,128)(2,1)}, u32[]{:S(2)}, u32[]{:S(2)}) collective-permute-start(bf16[4,48,896]{2,1,0:T(8,128)(2,1)} %fusion.6), channel_id=1, source_target_pairs={{0,4},{2,6},{4,0},{6,2},{8,12},{10,14},{12,8},{14,10},{16,20},{18,... | collective-permute-start | bytes 1032200 | tf_op jit(solution)/shard_map/ppermute | solution.py:1112
  584.5 4.9 copy-start.6
  584.5 6.2 %copy-start.2 = (bf16[8,48,896]{2,1,0:T(8,128)(2,1)S(1)}, bf16[8,48,896]{2,1,0:T(8,128)(2,1)}, u32[]{:S(2)}) copy-start(bf16[8,48,896]{2,1,0:T(8,128)(2,1)} %copy-done.1) | copy-start | bytes 2064388
  591.9 5.8 collective-permute-start.30
  592.9 6.6 %collective-permute-start.32 = (bf16[48,896]{1,0:T(8,128)(2,1)S(1)}, bf16[48,896]{1,0:T(8,128)(2,1)S(1)}, u32[]{:S(2)}, u32[]{:S(2)}) collective-permute-start(bf16[48,896]{1,0:T(8,128)(2,1)S(1)} %get-tuple-element.230), channel_id=1, source_target_pairs={{0,24},{2,26},{4,28},{6,30},{8,16},{10,18},{12,20},{14,22},{16,8},... | collective-permute-start | bytes 258056 | tf_op jit(solution)/shard_map/ppermute | solution.py:1112
  595.4 6.8 %collective-permute-start.31 = (bf16[48,896]{1,0:T(8,128)(2,1)S(1)}, bf16[48,896]{1,0:T(8,128)(2,1)S(1)}, u32[]{:S(2)}, u32[]{:S(2)}) collective-permute-start(bf16[48,896]{1,0:T(8,128)(2,1)S(1)} %get-tuple-element.231), channel_id=1, source_target_pairs={{0,16},{2,18},{4,20},{6,22},{8,24},{10,26},{12,28},{14,30},{16,0},... | collective-permute-start | bytes 258056 | tf_op jit(solution)/shard_map/ppermute | solution.py:1112
  595.9 7.8 %collective-permute-start.34 = (bf16[24,2304]{1,0:T(8,128)(2,1)S(1)}, bf16[24,2304]{1,0:T(8,128)(2,1)S(1)}, u32[]{:S(2)}, u32[]{:S(2)}) collective-permute-start(bf16[24,2304]{1,0:T(8,128)(2,1)S(1)} %dynamic-slice_bitcast_fusion.13), channel_id=1, source_target_pairs={{0,1},{1,0},{2,3},{3,2},{4,5},{5,4},{6,7},{7,6},{8,9},{9,8},{10,11... | collective-permute-start | bytes 331784 | tf_op jit(solution)/shard_map/ppermute | solution.py:1107
  602.2 4.1 collective-permute-start.33
Sparse Core Ops, SparseCore 0:
  19.2 134.4 all-gather.1
  336.7 156.0 reduce-scatter.1

commit v6 on v5

--- a/solution.py
+++ b/solution.py
@@ -1226,7 +1226,7 @@
         first, second, tokens.transpose(0, 2, 1, 3), cotangent.transpose(0, 2, 1, 3), tokens, packed
     )
     packed = lax.all_gather(packed, axes, axis=0, tiled=True)
-    half = by_place.shape[1] // 2
+    half = by_place.shape[1] * 2 // 5
     send = pick(by_place, 1 - place, 0)
     rest_a = swap_axis(send[:half], "frame")
     first = collect_lines(first)

time: 622 us -> 632 us (1.016)
  waiting for transfers between devices: 86.8 us -> 96.1 us
    ppermute x11, waiting for transfers between devices: 16.8 us -> 48.6 us  [swap_axis(): lax.ppermute(values, axis, [(index, size - 1 - index) for index in range(...]
    ppermute x25, waiting for transfers between devices: 69.9 us -> 47.4 us  [flip(): lax.ppermute(values, 'clip', [(index, index ^ mask) for index in range(si...]
where the time goes in v6:
time: 632 us; the launch traced here: 625 us
  Pallas kernels  392 us (62%)
  waiting for transfers between devices  96.1 us (15%)
  local copies, waits for them, and re-layouts  45 us (7%)
  starting transfers between devices  41 us (6%)
  other arithmetic  35.5 us (6%)
  between operations  15.2 us (2%)
    pallas_call x1, Pallas kernels, middle(): pl.pallas_call(functools.partial(middle_kernel, places), grid_spec=pltpu....  125 us
    pallas_call x2, Pallas kernels, space_backward(): pl.pallas_call(functools.partial(space_backward_kernel, places), grid_spe...  77.7 us
    pallas_call x1, Pallas kernels, time_backward(): pl.pallas_call(time_backward_kernel, grid=(groups // 2,), in_specs=[by_ro...  54.5 us
    ppermute x11, waiting for transfers between devices, swap_axis(): lax.ppermute(values, axis, [(index, size - 1 - index) for index in range(...  48.6 us
    ppermute x25, waiting for transfers between devices, flip(): lax.ppermute(values, 'clip', [(index, index ^ mask) for index in range(si...  47.4 us
    pallas_call x2, Pallas kernels, space_forward(): pl.pallas_call(functools.partial(space_forward_kernel, places), grid=(fra...  45.1 us
    pallas_call x1, Pallas kernels, feed_gradient(): pl.pallas_call(functools.partial(feed_gradient_kernel, turns), grid=(coun...  39.4 us
    pallas_call x2, Pallas kernels, split_gradient(): pl.pallas_call(functools.partial(gradient_kernel, parts, tiles), grid_spe...  28.6 us
  transfers between devices with their start and end apart: 38, of which 14 were waited for; matrix products, arithmetic and copies ran while one was open for 11% of the time, Pallas kernels for 37%

profile of v6, /device:TPU:0, one launch (start us, length us, event | category | flops | bytes accessed | tf_op | source)
XLA Modules:
  0.0 625.2 jit_solution(7322015641054181274)
XLA Ops:
  9.6 3.0 collective-permute-start.1
  14.6 2.1 reshape.152
  16.9 1.3 reshape.153
  19.2 4.2 collective-permute-start.4
  24.0 1.4 dynamic-slice_bitcast_fusion.3
  25.4 1.7 collective-permute-start.5
  27.1 6.1 dynamic-slice_bitcast_fusion
  33.4 2.0 copy.101
  35.4 3.7 collective-permute-done.3
  39.2 11.4 %collective-permute-done.5 = bf16[78,8,768]{2,1,0:T(8,128)(2,1)} collective-permute-done((bf16[78,8,768]{2,1,0:T(8,128)(2,1)S(1)}, bf16[78,8,768]{2,1,0:T(8,128)(2,1)}, u32[]{:S(2)}, u32[]{:S(2)}) %collective-permute-start.5) | collective-permute-done | bytes 958496 | tf_op jit(solution)/shard_map/ppermute | solution.py:1107
  50.6 3.5 collective-permute-start.9
  55.1 1.6 collective-permute-start.6
  56.7 1.5 collective-permute-start.11
  58.2 4.5 collective-permute-done.9
  62.7 15.5 %collective-permute-done.8 = bf16[2,24,1664]{2,1,0:T(8,128)(2,1)S(1)} collective-permute-done((bf16[2,24,1664]{2,1,0:T(8,128)(2,1)S(1)}, bf16[2,24,1664]{2,1,0:T(8,128)(2,1)S(1)}, u32[]{:S(2)}, u32[]{:S(2)}) %collective-permute-start.8) | collective-permute-done | bytes 159776 | tf_op jit(solution)/shard_map/ppermute | solution.py:1112
  79.5 1.6 collective-permute-start.10
  81.1 12.3 %collective-permute-done.10 = bf16[4,2,24,1664]{3,2,1,0:T(8,128)(2,1)S(1)} collective-permute-done((bf16[4,2,24,1664]{3,2,1,0:T(8,128)(2,1)S(1)}, bf16[4,2,24,1664]{3,2,1,0:T(8,128)(2,1)S(1)}, u32[]{:S(2)}, u32[]{:S(2)}) %collective-permute-start.10) | collective-permute-done | bytes 639008 | tf_op jit(solution)/shard_map/ppermute | solution.py:1112
  93.6 9.9 %collective-permute-done.11 = bf16[118,8,768]{2,1,0:T(8,128)(2,1)} collective-permute-done((bf16[118,8,768]{2,1,0:T(8,128)(2,1)S(1)}, bf16[118,8,768]{2,1,0:T(8,128)(2,1)}, u32[]{:S(2)}, u32[]{:S(2)}) %collective-permute-start.11) | collective-permute-done | bytes 1450016 | tf_op jit(solution)/shard_map/ppermute | solution.py:1107
  103.9 1.4 copy.74
  105.2 1.6 copy.75
  106.9 1.9 maximum_bitcast_fusion.x_ref
  108.7 2.0 maximum_select_fusion.1
  110.7 1.6 copy.72
  112.3 2.3 maximum_select_fusion
  114.9 1.3 fusion.13
  116.2 1.7 copy.78.fgain_ref
  119.3 22.5 %space_forward.2 = (bf16[8,208,768]{2,1,0:T(8,128)(2,1)}, bf16[8,208,2304]{2,1,0:T(8,128)(2,1)}, bf16[8,208,768]{2,1,0:T(8,128)(2,1)}, f32[26,8,8,768]{3,2,1,0:T(8,128)}) custom-call(bf16[8,196,768]{2,1,0:T(8,128)(2,1)} %bitcast.176, f32[1,768]{1,0:T(1,128)} %copy.73.gain_ref.gain_row_ref, bf16[768,1536]{1,0:T(8,128)(2,1)} %bitcast.172, ...), custom_call_target="tpu_custom_call" | custom-call | flops 1663041536 | bytes 4202496 | tf_op jit(solution)/shard_map/space_forward/pallas_call | solution.py:473
  141.8 22.6 %space_forward.3 = (bf16[8,208,768]{2,1,0:T(8,128)(2,1)}, bf16[8,208,2304]{2,1,0:T(8,128)(2,1)}, bf16[8,208,768]{2,1,0:T(8,128)(2,1)}, f32[26,8,8,768]{3,2,1,0:T(8,128)}) custom-call(bf16[8,196,768]{2,1,0:T(8,128)(2,1)} %maximum_bitcast_fusion.x_ref, f32[1,768]{1,0:T(1,128)} %copy.73.gain_ref.gain_row_ref, bf16[768,1536]{1,0:T(8,128)(2,1)} %bitcast.173, ...), custom_call_target="tpu_custom_call" | custom-call | flops 1663041536 | bytes 4202496 | tf_op jit(solution)/shard_map/space_forward/pallas_call | solution.py:473
  164.4 10.2 %collective-permute-done.14.gr_ref = bf16[196,8,768]{2,1,0:T(8,128)(2,1)} collective-permute-done((bf16[196,8,768]{2,1,0:T(8,128)(2,1)}, bf16[196,8,768]{2,1,0:T(8,128)(2,1)}, u32[]{:S(2)}, u32[]{:S(2)}) %collective-permute-start.14) | collective-permute-done | bytes 2408480 | tf_op jit(solution)/shard_map/ppermute | solution.py:1107
  174.6 124.9 %middle.1 = (bf16[3328,2304]{1,0:T(8,128)(2,1)}, bf16[3328,1536]{1,0:T(8,128)(2,1)}, bf16[3328,1536]{1,0:T(8,128)(2,1)}, bf16[3328,6144]{1,0:T(8,128)(2,1)}, bf1...) custom-call(s32[1]{0:T(128)} %bitcast.38.place_ref, ...), custom_call_target="tpu_custom_call" | custom-call | flops 13522436096 | bytes 18198528 | tf_op jit(solution)/shard_map/middle/pallas_call | solution.py:519
  299.5 39.4 %feed_gradient.1 = bf16[768,6144]{1,0:T(8,128)(2,1)} custom-call(bf16[3328,1536]{1,0:T(8,128)(2,1)} %get-tuple-element.134.narrow_ref, bf16[3328,6144]{1,0:T(8,128)(2,1)} %get-tuple-element.135.wide_ref), custom_call_target="tpu_custom_call" | custom-call | flops 5234491392 | bytes 10092544 | tf_op jit(solution)/shard_map/feed_gradient/pallas_call | solution.py:705
  338.9 1.7 copy-done.18
  340.9 54.5 %time_backward.1 = (bf16[3328,3072]{1,0:T(8,128)(2,1)}, f32[8,208,768]{2,1,0:T(8,128)}, f32[8,208,768]{2,1,0:T(8,128)}, f32[8,768]{1,0:T(8,128)}) custom-call(bf16[3328,2304]{1,0:T(8,128)(2,1)} %get-tuple-element.133.qkv_ref, f32[3328,768]{1,0:T(8,128)} %get-tuple-element.137.gt_ref, f32[26,8,8,768]{3,2,1,0:T(8,128)} %get-tuple-element.124.ao_ref, ...), custom_call_target="tpu_custom_call" | custom-call | flops 3707764736 | bytes 11079680 | tf_op jit(solution)/shard_map/time_backward/pallas_call | solution.py:567
  395.4 22.4 %time_gradient.1 = (bf16[8,48,3072]{2,1,0:T(8,128)(2,1)}, bf16[8,48,3072]{2,1,0:T(8,128)(2,1)}) custom-call(s32[1]{0:T(128)} %bitcast.core_ref, bf16[3328,1536]{1,0:T(8,128)(2,1)} %get-tuple-element.132.narrow_ref, bf16[3328,3072]{1,0:T(8,128)(2,1)} %get-tuple-element.138.wide_ref), custom_call_target="tpu_custom_call" | custom-call | flops 2617245696 | bytes 5898240 | tf_op jit(solution)/shard_map/time_gradient/pallas_call | solution.py:734
  417.8 4.7 collective-permute-done.16
  422.5 3.6 fusion.1
  426.1 1.6 collective-permute-start.17
  427.8 38.6 %space_backward.2 = (bf16[8,208,2304]{2,1,0:T(8,128)(2,1)}, bf16[8,208,768]{2,1,0:T(8,128)(2,1)}, bf16[196,8,768]{2,1,0:T(8,128)(2,1)}, f32[8,768]{1,0:T(8,128)}) custom-call(s32[1]{0:T(128)} %bitcast.38.place_ref, bf16[8,196,768]{2,1,0:T(8,128)(2,1)} %maximum_bitcast_fusion.x_ref, f32[8,208,768]{2,1,0:T(8,128)} %get-tuple-element.146.gs_ref, ...), custom_call_target="tpu_custom_call" | custom-call | flops 2194669568 | bytes 4640768 | tf_op jit(solution)/shard_map/space_backward/pallas_call | solution.py:599
  466.4 2.2 slice.66
  468.6 1.5 collective-permute-start.21
  470.1 1.7 fusion
  472.3 3.3 collective-permute-start.20
  476.7 39.1 %space_backward.3 = (bf16[8,208,2304]{2,1,0:T(8,128)(2,1)}, bf16[8,208,768]{2,1,0:T(8,128)(2,1)}, f32[2,196,8,768]{3,2,1,0:T(8,128)}, f32[8,768]{1,0:T(8,128)}) custom-call(s32[1]{0:T(128)} %bitcast.38.place_ref, bf16[8,196,768]{2,1,0:T(8,128)(2,1)} %bitcast.177, f32[8,208,768]{2,1,0:T(8,128)} %get-tuple-element.151.gs_ref, ...), custom_call_target="tpu_custom_call" | custom-call | flops 2194669568 | bytes 5844992 | tf_op jit(solution)/shard_map/space_backward/pallas_call | solution.py:599
  516.8 19.1 %split_gradient.2 = (bf16[8,48,2304]{2,1,0:T(8,128)(2,1)}, bf16[8,48,2304]{2,1,0:T(8,128)(2,1)}) custom-call(s32[1]{0:T(128)} %bitcast.core_ref, bf16[1664,768]{1,0:T(8,128)(2,1)} %bitcast.193, bf16[1664,2304]{1,0:T(8,128)(2,1)} %bitcast.179, bf16[1664,768]{1,0:T(8,128)(2,1)} %bitcast.194, bf16[1664,2304]{1,0:T(8,128)(2,1)} %bitcast.178), custom_call_target="tpu_custom_call" | custom-call | flops 1962934272 | bytes 3997696 | tf_op jit(solution)/shard_map/split_gradient/pallas_call | solution.py:751
  538.2 1.8 collective-permute-done.22
  540.0 2.6 fusion.3
  542.5 1.4 fusion.2
  544.6 9.5 %split_gradient.3 = (bf16[8,48,768]{2,1,0:T(8,128)(2,1)}, bf16[8,48,768]{2,1,0:T(8,128)(2,1)}) custom-call(s32[1]{0:T(128)} %bitcast.core_ref, bf16[1664,768]{1,0:T(8,128)(2,1)} %bitcast.191, bf16[1664,768]{1,0:T(8,128)(2,1)} %bitcast.196, bf16[1664,768]{1,0:T(8,128)(2,1)} %bitcast.192, bf16[1664,768]{1,0:T(8,128)(2,1)} %bitcast.195), custom_call_target="tpu_custom_call" | custom-call | flops 654311424 | bytes 1900544 | tf_op jit(solution)/shard_map/split_gradient/pallas_call | solution.py:751
  556.5 15.3 %collective-permute-done.25 = bf16[118,8,768]{2,1,0:T(8,128)(2,1)} collective-permute-done((bf16[118,8,768]{2,1,0:T(8,128)(2,1)}, bf16[118,8,768]{2,1,0:T(8,128)(2,1)}, u32[]{:S(2)}, u32[]{:S(2)}) %collective-permute-start.25) | collective-permute-done | bytes 1450016 | tf_op jit(solution)/shard_map/ppermute | solution.py:1107
  572.9 3.3 collective-permute-start.28
  577.3 1.3 add_convert_fusion.8
  579.9 1.8 fusion.6
  582.2 2.6 convert_dynamic-update-slice_fusion.1
  584.8 3.3 bitcast_dynamic-update-slice_fusion
  588.1 3.2 convert_dynamic-update-slice_fusion
  593.3 1.2 copy.87
  594.5 2.6 reshape.171
  599.4 1.3 add_convert_fusion.9
  602.9 2.4 collective-permute-start.32
  605.9 1.6 collective-permute-start.34
  607.9 1.8 collective-permute-done.32
  609.7 2.7 collective-permute-done.31
  612.5 1.6 collective-permute-start.33
  614.8 1.8 collective-permute-done.33
  (150 shorter events, 32.8 us)
Async XLA Ops:
  7.2 11.0 %copy-start.13 = (bf16[24,768]{1,0:T(8,128)(2,1)S(1)}, bf16[24,768]{1,0:T(8,128)(2,1)}, u32[]{:S(2)}) copy-start(bf16[24,768]{1,0:T(8,128)(2,1)} %param.19) | copy-start | bytes 110596
  7.2 11.0 %copy-start.12 = (bf16[24,2304]{1,0:T(8,128)(2,1)S(1)}, bf16[24,2304]{1,0:T(8,128)(2,1)}, u32[]{:S(2)}) copy-start(bf16[24,2304]{1,0:T(8,128)(2,1)} %param.18) | copy-start | bytes 331780
  7.2 167.4 %all-gather.2.cloned.1.call-start = ((), (), s32[]{:S(2)}) async-start(), calls=%async_computation.1 | async-start | bytes 14598144 | tf_op jit(solution)/shard_map/all_gather | solution.py:1228
  9.6 9.4 %collective-permute-start.1 = (bf16[24,1664]{1,0:T(8,128)(2,1)S(1)}, bf16[24,1664]{1,0:T(8,128)(2,1)S(1)}, u32[]{:S(2)}, u32[]{:S(2)}) collective-permute-start(bf16[24,1664]{1,0:T(8,128)(2,1)S(1)} %get-tuple-element.237), channel_id=1, source_target_pairs={{0,1},{1,0},{2,3},{3,2},{4,5},{5,4},{6,7},{7,6},{8,9},{9,8},{10,11... | collective-permute-start | bytes 239624 | tf_op jit(solution)/shard_map/ppermute | solution.py:1107
  13.5 5.4 collective-permute-start
  19.1 552.7 %reduce-scatter.2.cloned.1.call-start = ((), (), s32[]{:S(2)}) async-start(), calls=%async_computation.2 | async-start | bytes 9732096 | tf_op jit(solution)/shard_map/reduce_scatter | solution.py:1259
  19.2 16.2 %collective-permute-start.4 = (bf16[2,24,1536]{2,1,0:T(8,128)(2,1)S(1)}, bf16[2,24,1536]{2,1,0:T(8,128)(2,1)S(1)}, u32[]{:S(2)}, u32[]{:S(2)}) collective-permute-start(bf16[2,24,1536]{2,1,0:T(8,128)(2,1)S(1)} %maximum_select_fusion.5), channel_id=1, source_target_pairs={{0,24},{2,26},{4,28},{6,30},{8,16},{10,18},{12,20},{14,22},{16,8},... | collective-permute-start | bytes 442376 | tf_op jit(solution)/shard_map/ppermute | solution.py:1112
  23.4 15.7 %collective-permute-start.3 = (bf16[2,24,1536]{2,1,0:T(8,128)(2,1)S(1)}, bf16[2,24,1536]{2,1,0:T(8,128)(2,1)S(1)}, u32[]{:S(2)}, u32[]{:S(2)}) collective-permute-start(bf16[2,24,1536]{2,1,0:T(8,128)(2,1)S(1)} %maximum_select_fusion.5), channel_id=1, source_target_pairs={{0,16},{2,18},{4,20},{6,22},{8,24},{10,26},{12,28},{14,30},{16,0},... | collective-permute-start | bytes 442376 | tf_op jit(solution)/shard_map/ppermute | solution.py:1112
  23.4 15.7 %collective-permute-start.2 = (bf16[2,24,1536]{2,1,0:T(8,128)(2,1)S(1)}, bf16[2,24,1536]{2,1,0:T(8,128)(2,1)S(1)}, u32[]{:S(2)}, u32[]{:S(2)}) collective-permute-start(bf16[2,24,1536]{2,1,0:T(8,128)(2,1)S(1)} %maximum_select_fusion.5), channel_id=1, source_target_pairs={{0,8},{2,10},{4,12},{6,14},{8,0},{10,2},{12,4},{14,6},{16,24},{18,... | collective-permute-start | bytes 442376 | tf_op jit(solution)/shard_map/ppermute | solution.py:1112
  24.0 9.2 %slice-start = ((s8[4816896]{0:T(1024)(128)(4,1)}), s8[4194304]{0:T(1024)(128)(4,1)S(1)}, s32[]{:S(2)}) async-start(s8[4816896]{0:T(1024)(128)(4,1)} %bitcast.182), calls=%async_computation.3 | async-start | bytes 8388608
  25.4 7.8 %slice-start.1 = ((s8[4816896]{0:T(1024)(128)(4,1)}), s8[622592]{0:T(1024)(128)(4,1)S(1)}, s32[]{:S(2)}) async-start(s8[4816896]{0:T(1024)(128)(4,1)} %bitcast.182), calls=%async_computation.4 | async-start | bytes 1245184
  25.4 25.2 %collective-permute-start.5 = (bf16[78,8,768]{2,1,0:T(8,128)(2,1)S(1)}, bf16[78,8,768]{2,1,0:T(8,128)(2,1)}, u32[]{:S(2)}, u32[]{:S(2)}) collective-permute-start(bf16[78,8,768]{2,1,0:T(8,128)(2,1)S(1)} %dynamic-slice_bitcast_fusion.3), channel_id=1, source_target_pairs={{0,1},{1,0},{2,3},{3,2},{4,5},{5,4},{6,7},{7,6},{8,9},{9,8},{10,11... | collective-permute-start | bytes 2875400 | tf_op jit(solution)/shard_map/ppermute | solution.py:1107
  50.6 12.0 %collective-permute-start.9 = (bf16[2,24,1664]{2,1,0:T(8,128)(2,1)S(1)}, bf16[2,24,1664]{2,1,0:T(8,128)(2,1)S(1)}, u32[]{:S(2)}, u32[]{:S(2)}) collective-permute-start(bf16[2,24,1664]{2,1,0:T(8,128)(2,1)S(1)} %maximum_select_fusion.4), channel_id=1, source_target_pairs={{0,24},{2,26},{4,28},{6,30},{8,16},{10,18},{12,20},{14,22},{16,8},... | collective-permute-start | bytes 479240 | tf_op jit(solution)/shard_map/ppermute | solution.py:1112
  54.1 24.1 %collective-permute-start.8 = (bf16[2,24,1664]{2,1,0:T(8,128)(2,1)S(1)}, bf16[2,24,1664]{2,1,0:T(8,128)(2,1)S(1)}, u32[]{:S(2)}, u32[]{:S(2)}) collective-permute-start(bf16[2,24,1664]{2,1,0:T(8,128)(2,1)S(1)} %maximum_select_fusion.4), channel_id=1, source_target_pairs={{0,16},{2,18},{4,20},{6,22},{8,24},{10,26},{12,28},{14,30},{16,0},... | collective-permute-start | bytes 479240 | tf_op jit(solution)/shard_map/ppermute | solution.py:1112
  54.1 24.1 %collective-permute-start.7 = (bf16[2,24,1664]{2,1,0:T(8,128)(2,1)S(1)}, bf16[2,24,1664]{2,1,0:T(8,128)(2,1)}, u32[]{:S(2)}, u32[]{:S(2)}) collective-permute-start(bf16[2,24,1664]{2,1,0:T(8,128)(2,1)S(1)} %maximum_select_fusion.4), channel_id=1, source_target_pairs={{0,8},{2,10},{4,12},{6,14},{8,0},{10,2},{12,4},{14,6},{16,24},{18,... | collective-permute-start | bytes 479240 | tf_op jit(solution)/shard_map/ppermute | solution.py:1112
  55.1 24.2 %collective-permute-start.6 = (bf16[4,2,24,1536]{3,2,1,0:T(8,128)(2,1)S(1)}, bf16[4,2,24,1536]{3,2,1,0:T(8,128)(2,1)S(1)}, u32[]{:S(2)}, u32[]{:S(2)}) collective-permute-start(bf16[4,2,24,1536]{3,2,1,0:T(8,128)(2,1)S(1)} %pad_maximum_fusion.3), channel_id=1, source_target_pairs={{0,4},{2,6},{4,0},{6,2},{8,12},{10,14},{12,8},{14,10},{16,20},{18,... | collective-permute-start | bytes 1769480 | tf_op jit(solution)/shard_map/ppermute | solution.py:1112
  56.7 46.9 %collective-permute-start.11 = (bf16[118,8,768]{2,1,0:T(8,128)(2,1)S(1)}, bf16[118,8,768]{2,1,0:T(8,128)(2,1)}, u32[]{:S(2)}, u32[]{:S(2)}) collective-permute-start(bf16[118,8,768]{2,1,0:T(8,128)(2,1)S(1)} %slice.61), channel_id=1, source_target_pairs={{0,1},{1,0},{2,3},{3,2},{4,5},{5,4},{6,7},{7,6},{8,9},{9,8},{10,11... | collective-permute-start | bytes 4349960 | tf_op jit(solution)/shard_map/ppermute | solution.py:1107
  79.5 13.9 %collective-permute-start.10 = (bf16[4,2,24,1664]{3,2,1,0:T(8,128)(2,1)S(1)}, bf16[4,2,24,1664]{3,2,1,0:T(8,128)(2,1)S(1)}, u32[]{:S(2)}, u32[]{:S(2)}) collective-permute-start(bf16[4,2,24,1664]{3,2,1,0:T(8,128)(2,1)S(1)} %pad_maximum_fusion.2), channel_id=1, source_target_pairs={{0,4},{2,6},{4,0},{6,2},{8,12},{10,14},{12,8},{14,10},{16,20},{18,... | collective-permute-start | bytes 1916936 | tf_op jit(solution)/shard_map/ppermute | solution.py:1112
  81.1 27.7 %collective-permute-start.13 = (bf16[4,2,2,24,1536]{4,3,2,0,1:T(8,128)(2,1)S(1)}, bf16[4,2,2,24,1536]{4,3,2,0,1:T(8,128)(2,1)}, u32[]{:S(2)}, u32[]{:S(2)}) collective-permute-start(bf16[4,2,2,24,1536]{4,3,2,0,1:T(8,128)(2,1)S(1)} %maximum_select_fusion.3), channel_id=1, source_target_pairs={{0,2},{2,0},{4,6},{6,4},{8,10},{10,8},{12,14},{14,12},{16,18},{18,... | collective-permute-start | bytes 3538952 | tf_op jit(solution)/shard_map/ppermute | solution.py:1112
  103.6 8.8 %collective-permute-start.12 = (bf16[4,2,2,24,1664]{4,3,2,0,1:T(8,128)(2,1)S(1)}, bf16[4,2,2,24,1664]{4,3,2,0,1:T(8,128)(2,1)}, u32[]{:S(2)}, u32[]{:S(2)}) collective-permute-start(bf16[4,2,2,24,1664]{4,3,2,0,1:T(8,128)(2,1)S(1)} %maximum_select_fusion.2), channel_id=1, source_target_pairs={{0,2},{2,0},{4,6},{6,4},{8,10},{10,8},{12,14},{14,12},{16,18},{18,... | collective-permute-start | bytes 3833864 | tf_op jit(solution)/shard_map/ppermute | solution.py:1112
  103.6 71.1 %collective-permute-start.14 = (bf16[196,8,768]{2,1,0:T(8,128)(2,1)}, bf16[196,8,768]{2,1,0:T(8,128)(2,1)}, u32[]{:S(2)}, u32[]{:S(2)}) collective-permute-start(bf16[196,8,768]{2,1,0:T(8,128)(2,1)} %get-tuple-element.125), channel_id=1, source_target_pairs={{0,1},{1,0},{2,3},{3,2},{4,5},{5,4},{6,7},{7,6},{8,9},{9,8},{10,11... | collective-permute-start | bytes 7225352 | tf_op jit(solution)/shard_map/ppermute | solution.py:1107
  114.8 4.5 copy-start
  338.9 1.7 copy-start.18
  340.6 77.2 %collective-permute-start.15 = (bf16[196,8,768]{2,1,0:T(8,128)(2,1)S(1)}, bf16[196,8,768]{2,1,0:T(8,128)(2,1)}, u32[]{:S(2)}, u32[]{:S(2)}) collective-permute-start(bf16[196,8,768]{2,1,0:T(8,128)(2,1)S(1)} %copy-done.18), channel_id=1, source_target_pairs={{0,1},{1,0},{2,3},{3,2},{4,5},{5,4},{6,7},{7,6},{8,9},{9,8},{10,11... | collective-permute-start | bytes 7225352 | tf_op jit(solution)/shard_map/ppermute | solution.py:1107
  417.8 4.7 collective-permute-start.16
  422.5 5.3 copy-start.5
  426.1 45.6 %collective-permute-start.17 = (bf16[4,48,3072]{2,1,0:T(8,128)(2,1)}, bf16[4,48,3072]{2,1,0:T(8,128)(2,1)S(1)}, u32[]{:S(2)}, u32[]{:S(2)}) collective-permute-start(bf16[4,48,3072]{2,1,0:T(8,128)(2,1)} %fusion.1), channel_id=1, source_target_pairs={{0,4},{2,6},{4,0},{6,2},{8,12},{10,14},{12,8},{14,10},{16,20},{18,... | collective-permute-start | bytes 3538952 | tf_op jit(solution)/shard_map/ppermute | solution.py:1112
  427.8 42.3 %copy-start.4 = (bf16[8,48,3072]{2,1,0:T(8,128)(2,1)S(1)}, bf16[8,48,3072]{2,1,0:T(8,128)(2,1)}, u32[]{:S(2)}) copy-start(bf16[8,48,3072]{2,1,0:T(8,128)(2,1)} %get-tuple-element.143) | copy-start | bytes 7077892
  468.6 47.2 %collective-permute-start.21 = (bf16[78,8,768]{2,1,0:T(8,128)(2,1)}, bf16[78,8,768]{2,1,0:T(8,128)(2,1)}, u32[]{:S(2)}, u32[]{:S(2)}) collective-permute-start(bf16[78,8,768]{2,1,0:T(8,128)(2,1)} %slice.66), channel_id=1, source_target_pairs={{0,1},{1,0},{2,3},{3,2},{4,5},{5,4},{6,7},{7,6},{8,9},{9,8},{10,11... | collective-permute-start | bytes 2875400 | tf_op jit(solution)/shard_map/ppermute | solution.py:1107
  472.3 43.6 %collective-permute-start.20 = (bf16[48,3072]{1,0:T(8,128)(2,1)S(1)}, bf16[48,3072]{1,0:T(8,128)(2,1)S(1)}, u32[]{:S(2)}, u32[]{:S(2)}) collective-permute-start(bf16[48,3072]{1,0:T(8,128)(2,1)S(1)} %get-tuple-element.208), channel_id=1, source_target_pairs={{0,24},{2,26},{4,28},{6,30},{8,16},{10,18},{12,20},{14,22},{16,8},... | collective-permute-start | bytes 884744 | tf_op jit(solution)/shard_map/ppermute | solution.py:1112
  475.6 40.3 %collective-permute-start.19 = (bf16[48,3072]{1,0:T(8,128)(2,1)S(1)}, bf16[48,3072]{1,0:T(8,128)(2,1)S(1)}, u32[]{:S(2)}, u32[]{:S(2)}) collective-permute-start(bf16[48,3072]{1,0:T(8,128)(2,1)S(1)} %get-tuple-element.209), channel_id=1, source_target_pairs={{0,16},{2,18},{4,20},{6,22},{8,24},{10,26},{12,28},{14,30},{16,0},... | collective-permute-start | bytes 884744 | tf_op jit(solution)/shard_map/ppermute | solution.py:1112
  475.6 40.3 %collective-permute-start.18 = (bf16[48,3072]{1,0:T(8,128)(2,1)S(1)}, bf16[48,3072]{1,0:T(8,128)(2,1)S(1)}, u32[]{:S(2)}, u32[]{:S(2)}) collective-permute-start(bf16[48,3072]{1,0:T(8,128)(2,1)S(1)} %get-tuple-element.210), channel_id=1, source_target_pairs={{0,8},{2,10},{4,12},{6,14},{8,0},{10,2},{12,4},{14,6},{16,24},{18,... | collective-permute-start | bytes 884744 | tf_op jit(solution)/shard_map/ppermute | solution.py:1112
  515.9 20.0 %copy-start.9 = (bf16[48,3072]{1,0:T(8,128)(2,1)}, bf16[48,3072]{1,0:T(8,128)(2,1)S(1)}, u32[]{:S(2)}) copy-start(bf16[48,3072]{1,0:T(8,128)(2,1)S(1)} %collective-permute-done.20) | copy-start | bytes 884740
  515.9 0.8 copy-start.10
  515.9 0.9 copy-start.11
  516.8 19.2 %copy-start.16 = (f32[8,768]{1,0:T(8,128)S(1)}, f32[8,768]{1,0:T(8,128)}, u32[]{:S(2)}) copy-start(f32[8,768]{1,0:T(8,128)} %get-tuple-element.172) | copy-start | bytes 73732
  516.8 19.3 %copy-start.17 = (f32[8,768]{1,0:T(8,128)S(1)}, f32[8,768]{1,0:T(8,128)}, u32[]{:S(2)}) copy-start(f32[8,768]{1,0:T(8,128)} %get-tuple-element.171) | copy-start | bytes 73732
  516.8 19.3 %copy-start.3 = (bf16[196,8,768]{2,1,0:T(8,128)(2,1)S(1)}, bf16[196,8,768]{2,1,0:T(8,128)(2,1)}, u32[]{:S(2)}) copy-start(bf16[196,8,768]{2,1,0:T(8,128)(2,1)} %get-tuple-element.155) | copy-start | bytes 7225348
  535.9 2.0 copy-start.14
  535.9 2.0 copy-start.15
  535.9 4.1 collective-permute-start.22
  537.3 5.3 copy-start.6
  537.3 34.5 %collective-permute-start.25 = (bf16[118,8,768]{2,1,0:T(8,128)(2,1)}, bf16[118,8,768]{2,1,0:T(8,128)(2,1)}, u32[]{:S(2)}, u32[]{:S(2)}) collective-permute-start(bf16[118,8,768]{2,1,0:T(8,128)(2,1)} %slice.67), channel_id=1, source_target_pairs={{0,1},{1,0},{2,3},{3,2},{4,5},{5,4},{6,7},{7,6},{8,9},{9,8},{10,11... | collective-permute-start | bytes 4349960 | tf_op jit(solution)/shard_map/ppermute | solution.py:1107
  543.9 27.8 %collective-permute-start.23 = (bf16[4,48,2304]{2,1,0:T(8,128)(2,1)}, bf16[4,48,2304]{2,1,0:T(8,128)(2,1)S(1)}, u32[]{:S(2)}, u32[]{:S(2)}) collective-permute-start(bf16[4,48,2304]{2,1,0:T(8,128)(2,1)} %fusion.3), channel_id=1, source_target_pairs={{0,4},{2,6},{4,0},{6,2},{8,12},{10,14},{12,8},{14,10},{16,20},{18,... | collective-permute-start | bytes 2654216 | tf_op jit(solution)/shard_map/ppermute | solution.py:1112
  555.2 16.5 %collective-permute-start.24 = (bf16[8,48,896]{2,1,0:T(8,128)(2,1)S(1)}, bf16[8,48,896]{2,1,0:T(8,128)(2,1)}, u32[]{:S(2)}, u32[]{:S(2)}) collective-permute-start(bf16[8,48,896]{2,1,0:T(8,128)(2,1)S(1)} %pad_maximum_fusion.1), channel_id=1, source_target_pairs={{0,2},{2,0},{4,6},{6,4},{8,10},{10,8},{12,14},{14,12},{16,18},{18,... | collective-permute-start | bytes 2064392 | tf_op jit(solution)/shard_map/ppermute | solution.py:1112
  556.4 23.4 %copy-start.1 = (bf16[8,48,896]{2,1,0:T(8,128)(2,1)}, bf16[8,48,896]{2,1,0:T(8,128)(2,1)S(1)}, u32[]{:S(2)}) copy-start(bf16[8,48,896]{2,1,0:T(8,128)(2,1)S(1)} %pad_maximum_fusion) | copy-start | bytes 2064388
  572.0 10.2 %copy-start.7 = (bf16[24,6144]{1,0:T(8,128)(2,1)S(1)}, bf16[24,6144]{1,0:T(8,128)(2,1)}, u32[]{:S(2)}) copy-start(bf16[24,6144]{1,0:T(8,128)(2,1)} %reduce-scatter.2.cloned.1.call-done) | copy-start | bytes 884740
  572.9 26.5 %collective-permute-start.28 = (bf16[48,2304]{1,0:T(8,128)(2,1)}, bf16[48,2304]{1,0:T(8,128)(2,1)}, u32[]{:S(2)}, u32[]{:S(2)}) collective-permute-start(bf16[48,2304]{1,0:T(8,128)(2,1)} %get-tuple-element.212), channel_id=1, source_target_pairs={{0,24},{2,26},{4,28},{6,30},{8,16},{10,18},{12,20},{14,22},{16,8},... | collective-permute-start | bytes 663560 | tf_op jit(solution)/shard_map/ppermute | solution.py:1112
  576.2 23.2 %collective-permute-start.27 = (bf16[48,2304]{1,0:T(8,128)(2,1)}, bf16[48,2304]{1,0:T(8,128)(2,1)}, u32[]{:S(2)}, u32[]{:S(2)}) collective-permute-start(bf16[48,2304]{1,0:T(8,128)(2,1)} %get-tuple-element.213), channel_id=1, source_target_pairs={{0,16},{2,18},{4,20},{6,22},{8,24},{10,26},{12,28},{14,30},{16,0},... | collective-permute-start | bytes 663560 | tf_op jit(solution)/shard_map/ppermute | solution.py:1112
  576.2 23.2 %collective-permute-start.26 = (bf16[48,2304]{1,0:T(8,128)(2,1)}, bf16[48,2304]{1,0:T(8,128)(2,1)}, u32[]{:S(2)}, u32[]{:S(2)}) collective-permute-start(bf16[48,2304]{1,0:T(8,128)(2,1)} %get-tuple-element.214), channel_id=1, source_target_pairs={{0,8},{2,10},{4,12},{6,14},{8,0},{10,2},{12,4},{14,6},{16,24},{18,... | collective-permute-start | bytes 663560 | tf_op jit(solution)/shard_map/ppermute | solution.py:1112
  579.3 17.8 %collective-permute-start.35 = (bf16[24,3072]{1,0:T(8,128)(2,1)}, bf16[24,3072]{1,0:T(8,128)(2,1)}, u32[]{:S(2)}, u32[]{:S(2)}) collective-permute-start(bf16[24,3072]{1,0:T(8,128)(2,1)} %dynamic-slice_bitcast_fusion.12), channel_id=1, source_target_pairs={{0,1},{1,0},{2,3},{3,2},{4,5},{5,4},{6,7},{7,6},{8,9},{9,8},{10,11... | collective-permute-start | bytes 442376 | tf_op jit(solution)/shard_map/ppermute | solution.py:1107
  581.7 19.0 %collective-permute-start.29 = (bf16[4,48,896]{2,1,0:T(8,128)(2,1)}, bf16[4,48,896]{2,1,0:T(8,128)(2,1)}, u32[]{:S(2)}, u32[]{:S(2)}) collective-permute-start(bf16[4,48,896]{2,1,0:T(8,128)(2,1)} %fusion.6), channel_id=1, source_target_pairs={{0,4},{2,6},{4,0},{6,2},{8,12},{10,14},{12,8},{14,10},{16,20},{18,... | collective-permute-start | bytes 1032200 | tf_op jit(solution)/shard_map/ppermute | solution.py:1112
  594.5 4.9 copy-start.8
  594.5 6.2 copy-start.2
  602.0 5.9 collective-permute-start.30
  602.9 6.8 %collective-permute-start.32 = (bf16[48,896]{1,0:T(8,128)(2,1)S(1)}, bf16[48,896]{1,0:T(8,128)(2,1)S(1)}, u32[]{:S(2)}, u32[]{:S(2)}) collective-permute-start(bf16[48,896]{1,0:T(8,128)(2,1)S(1)} %get-tuple-element.228), channel_id=1, source_target_pairs={{0,24},{2,26},{4,28},{6,30},{8,16},{10,18},{12,20},{14,22},{16,8},... | collective-permute-start | bytes 258056 | tf_op jit(solution)/shard_map/ppermute | solution.py:1112
  605.4 7.0 %collective-permute-start.31 = (bf16[48,896]{1,0:T(8,128)(2,1)S(1)}, bf16[48,896]{1,0:T(8,128)(2,1)S(1)}, u32[]{:S(2)}, u32[]{:S(2)}) collective-permute-start(bf16[48,896]{1,0:T(8,128)(2,1)S(1)} %get-tuple-element.229), channel_id=1, source_target_pairs={{0,16},{2,18},{4,20},{6,22},{8,24},{10,26},{12,28},{14,30},{16,0},... | collective-permute-start | bytes 258056 | tf_op jit(solution)/shard_map/ppermute | solution.py:1112
  605.9 8.2 %collective-permute-start.34 = (bf16[24,2304]{1,0:T(8,128)(2,1)S(1)}, bf16[24,2304]{1,0:T(8,128)(2,1)S(1)}, u32[]{:S(2)}, u32[]{:S(2)}) collective-permute-start(bf16[24,2304]{1,0:T(8,128)(2,1)S(1)} %dynamic-slice_bitcast_fusion.13), channel_id=1, source_target_pairs={{0,1},{1,0},{2,3},{3,2},{4,5},{5,4},{6,7},{7,6},{8,9},{9,8},{10,11... | collective-permute-start | bytes 331784 | tf_op jit(solution)/shard_map/ppermute | solution.py:1107
  612.5 4.1 collective-permute-start.33
Sparse Core Ops, SparseCore 0:
  19.2 138.6 all-gather.1
  339.0 157.4 reduce-scatter.1
